TPU v7x, 512 devices: a whole 4x8x8 slice. The times are simulated.
512 devices in a mesh: energy: 64 (over y, x, core), space: 8 (over z).
Axes of the slice: x: 4, y: 8, z: 8, core: 2. Of those that a mesh axis runs over, the one named last changes fastest.
Arguments:
- inverses: float32 [128, 16, 256, 256], P('energy', 'space'), may hold values from -0.375 to 0.375
- coupling: float32 [16, 256, 256], P('space'), may hold values from -0.375 to 0.375
- source: float32 [128, 16, 256, 256], P('energy', 'space'), may hold values from -6 to 6
- screened: float32 [128, 4096, 256], P('energy', 'space'), may hold values from -0.12 to 0.12
- kept_rows: int32 [4096], P('space'), may hold values from 0 to 511
- live_count: int32 [8], P('space'), may hold values from 128 to 512, as said below
Outputs:
- sigma_kept: float32 [128, 4096, 256], P('energy', 'space')
Inputs may be any that keep to these rules, and one draw needn't show every extreme that they name: `live_count`: between 128 and 512; some partition has exactly 512 live slots.
All inputs are finite; a program needn't handle non-finite values.
Results may differ from a plain program's by a relative error of at most 0.00021.
Values sent between devices are 32-bit elements; how exact they have to be, the bound alone decides.
No kernel may reach another device: no remote copies, remote signals or barrier semaphores. Data moves between devices by JAX's collectives and lax.ppermute only.
A program may use at most 64 MiB of HBM per device.

v0:
```python
import math

import jax
import jax.numpy as jnp
from jax import lax
from jax.sharding import PartitionSpec as P


def shifted(shard, axis, by):
    count = lax.axis_size(axis)
    pairs = [(i, i + by) for i in range(count) if 0 <= i + by < count]
    return lax.ppermute(shard, axis, pairs)


def mult(left, right):
    return jnp.matmul(left, right, precision=lax.Precision.HIGHEST)


def flip(matrix):
    return jnp.swapaxes(matrix, -1, -2)


def convolve(pair):
    lesser_all, screened_all = pair
    count = lesser_all.shape[0]
    freq = jnp.arange(count, dtype=jnp.int32)
    phase = (freq[:, None] * freq[None, :] % count).astype(jnp.float32)
    angle = phase * (2.0 * math.pi / count)
    cosine = jnp.cos(angle)
    sine = jnp.sin(angle)
    highest = lax.Precision.HIGHEST
    real_a = jnp.einsum("wk,krc->wrc", cosine, lesser_all, precision=highest)
    imag_a = -jnp.einsum("wk,krc->wrc", sine, lesser_all, precision=highest)
    real_b = jnp.einsum("wk,krc->wrc", cosine, screened_all, precision=highest)
    imag_b = -jnp.einsum("wk,krc->wrc", sine, screened_all, precision=highest)
    real_p = real_a * real_b - imag_a * imag_b
    imag_p = real_a * imag_b + imag_a * real_b
    sigma = (
        jnp.einsum("kw,wrc->krc", cosine, real_p, precision=highest)
        - jnp.einsum("kw,wrc->krc", sine, imag_p, precision=highest)
    ) / count
    return lax.all_to_all(sigma, "energy", split_axis=0, concat_axis=1, tiled=True)


def body(inverses, coupling, source, screened, kept_rows, live_count):
    energies = inverses.shape[0]
    blocks = coupling.shape[0]
    width = coupling.shape[1]
    transfer = mult(inverses, coupling[None])
    injected = mult(mult(inverses, source), flip(inverses))
    identity = jnp.broadcast_to(jnp.eye(width, dtype=jnp.float32), (energies, width, width))
    nothing = jnp.zeros((energies, width, width), jnp.float32)
    total_map = identity
    total_add = nothing
    for index in range(blocks):
        step_map = transfer[:, index]
        total_map = mult(step_map, total_map)
        total_add = mult(mult(step_map, total_add), flip(step_map)) + injected[:, index]

    def advance(step, carry):
        outgoing = mult(mult(total_map, carry), flip(total_map)) + total_add
        return shifted(outgoing, "space", 1)

    entry = lax.fori_loop(0, lax.axis_size("space") - 1, advance, nothing)
    state = entry
    sweep = []
    for index in range(blocks):
        step_map = transfer[:, index]
        state = mult(mult(step_map, state), flip(step_map)) + injected[:, index]
        sweep.append(state)
    lesser = jnp.stack(sweep, axis=1).reshape(energies, blocks * width, width)
    picked = jnp.take(lesser, kept_rows, axis=1)
    live = (jnp.arange(kept_rows.shape[0], dtype=jnp.int32) < live_count[0]).astype(jnp.float32)
    picked = picked * live[None, :, None]
    return convolve(
        (
            lax.all_to_all(picked, "energy", split_axis=1, concat_axis=0, tiled=True),
            lax.all_to_all(screened, "energy", split_axis=1, concat_axis=0, tiled=True),
        )
    )


def solution(mesh):
    return jax.shard_map(
        body,
        mesh=mesh,
        in_specs=(
            P("energy", "space", None, None),
            P("space", None, None),
            P("energy", "space", None, None),
            P("energy", "space", None),
            P("space"),
            P("space"),
        ),
        out_specs=P("energy", "space", None),
        check_vma=False,
    )
```

profile of v0, /device:TPU:192, one launch (start us, length us, event | category | flops | bytes accessed | tf_op | source)
XLA Modules:
  0.0 261.6 jit_solution(9148876044822511578)
XLA Ops:
  10.8 118.5 %while.10 = (s32[]{:T(128)}, f32[2,256,256]{2,1,0:T(8,128)S(1)}, f32[2,256,256]{2,1,0:T(8,128)S(1)}, f32[2,256,256]{2,1,0:T(8,128)}, s32[]{:T(128)}) while((s32[]{:T(128)}, f32[2,256,256]{2,1,0:T(8,128)S(1)}, f32[2,256,256]{2,1,0:T(8,128)S(1)}, f32[2,256,256]{2,1,0:T(8,128)}, s32[]{:T(128)}) %tuple.19), condition=%wide.region_1.0_spmd, body=%wide.region_0.0_spmd.sunk | while | flops 805437440 | bytes 7864449 | solution.py:64
  13.5 5.5 %collective-permute-start = (f32[2,256,256]{2,1,0:T(8,128)}, f32[2,256,256]{2,1,0:T(8,128)S(1)}, u32[]{:S(2)}, u32[]{:S(2)}) collective-permute-start(f32[2,256,256]{2,1,0:T(8,128)} %convolution_add_fusion.6), channel_id=1, source_target_pairs={{0,1},{1,2},{2,3},{3,4},{4,5},{5,6},{6,7},{8,9},{9,10},{10,11},{11... | collective-permute-start | bytes 1572872 | tf_op jit(solution)/shard_map/while/body/eval_jaxpr/ppermute | solution.py:12
  19.0 11.5 %collective-permute-done = f32[2,256,256]{2,1,0:T(8,128)S(1)} collective-permute-done((f32[2,256,256]{2,1,0:T(8,128)}, f32[2,256,256]{2,1,0:T(8,128)S(1)}, u32[]{:S(2)}, u32[]{:S(2)}) %collective-permute-start) | collective-permute-done | bytes 524320 | tf_op jit(solution)/shard_map/while/body/eval_jaxpr/ppermute | solution.py:12
  33.0 5.5 %collective-permute-start = (f32[2,256,256]{2,1,0:T(8,128)}, f32[2,256,256]{2,1,0:T(8,128)S(1)}, u32[]{:S(2)}, u32[]{:S(2)}) collective-permute-start(f32[2,256,256]{2,1,0:T(8,128)} %convolution_add_fusion.6), channel_id=1, source_target_pairs={{0,1},{1,2},{2,3},{3,4},{4,5},{5,6},{6,7},{8,9},{9,10},{10,11},{11... | collective-permute-start | bytes 1572872 | tf_op jit(solution)/shard_map/while/body/eval_jaxpr/ppermute | solution.py:12
  38.5 10.6 %collective-permute-done = f32[2,256,256]{2,1,0:T(8,128)S(1)} collective-permute-done((f32[2,256,256]{2,1,0:T(8,128)}, f32[2,256,256]{2,1,0:T(8,128)S(1)}, u32[]{:S(2)}, u32[]{:S(2)}) %collective-permute-start) | collective-permute-done | bytes 524320 | tf_op jit(solution)/shard_map/while/body/eval_jaxpr/ppermute | solution.py:12
  51.6 5.5 %collective-permute-start = (f32[2,256,256]{2,1,0:T(8,128)}, f32[2,256,256]{2,1,0:T(8,128)S(1)}, u32[]{:S(2)}, u32[]{:S(2)}) collective-permute-start(f32[2,256,256]{2,1,0:T(8,128)} %convolution_add_fusion.6), channel_id=1, source_target_pairs={{0,1},{1,2},{2,3},{3,4},{4,5},{5,6},{6,7},{8,9},{9,10},{10,11},{11... | collective-permute-start | bytes 1572872 | tf_op jit(solution)/shard_map/while/body/eval_jaxpr/ppermute | solution.py:12
  57.1 9.7 %collective-permute-done = f32[2,256,256]{2,1,0:T(8,128)S(1)} collective-permute-done((f32[2,256,256]{2,1,0:T(8,128)}, f32[2,256,256]{2,1,0:T(8,128)S(1)}, u32[]{:S(2)}, u32[]{:S(2)}) %collective-permute-start) | collective-permute-done | bytes 524320 | tf_op jit(solution)/shard_map/while/body/eval_jaxpr/ppermute | solution.py:12
  69.3 5.5 %collective-permute-start = (f32[2,256,256]{2,1,0:T(8,128)}, f32[2,256,256]{2,1,0:T(8,128)S(1)}, u32[]{:S(2)}, u32[]{:S(2)}) collective-permute-start(f32[2,256,256]{2,1,0:T(8,128)} %convolution_add_fusion.6), channel_id=1, source_target_pairs={{0,1},{1,2},{2,3},{3,4},{4,5},{5,6},{6,7},{8,9},{9,10},{10,11},{11... | collective-permute-start | bytes 1572872 | tf_op jit(solution)/shard_map/while/body/eval_jaxpr/ppermute | solution.py:12
  74.8 8.8 %collective-permute-done = f32[2,256,256]{2,1,0:T(8,128)S(1)} collective-permute-done((f32[2,256,256]{2,1,0:T(8,128)}, f32[2,256,256]{2,1,0:T(8,128)S(1)}, u32[]{:S(2)}, u32[]{:S(2)}) %collective-permute-start) | collective-permute-done | bytes 524320 | tf_op jit(solution)/shard_map/while/body/eval_jaxpr/ppermute | solution.py:12
  86.0 5.5 %collective-permute-start = (f32[2,256,256]{2,1,0:T(8,128)}, f32[2,256,256]{2,1,0:T(8,128)S(1)}, u32[]{:S(2)}, u32[]{:S(2)}) collective-permute-start(f32[2,256,256]{2,1,0:T(8,128)} %convolution_add_fusion.6), channel_id=1, source_target_pairs={{0,1},{1,2},{2,3},{3,4},{4,5},{5,6},{6,7},{8,9},{9,10},{10,11},{11... | collective-permute-start | bytes 1572872 | tf_op jit(solution)/shard_map/while/body/eval_jaxpr/ppermute | solution.py:12
  91.5 7.8 %collective-permute-done = f32[2,256,256]{2,1,0:T(8,128)S(1)} collective-permute-done((f32[2,256,256]{2,1,0:T(8,128)}, f32[2,256,256]{2,1,0:T(8,128)S(1)}, u32[]{:S(2)}, u32[]{:S(2)}) %collective-permute-start) | collective-permute-done | bytes 524320 | tf_op jit(solution)/shard_map/while/body/eval_jaxpr/ppermute | solution.py:12
  101.9 5.5 %collective-permute-start = (f32[2,256,256]{2,1,0:T(8,128)}, f32[2,256,256]{2,1,0:T(8,128)S(1)}, u32[]{:S(2)}, u32[]{:S(2)}) collective-permute-start(f32[2,256,256]{2,1,0:T(8,128)} %convolution_add_fusion.6), channel_id=1, source_target_pairs={{0,1},{1,2},{2,3},{3,4},{4,5},{5,6},{6,7},{8,9},{9,10},{10,11},{11... | collective-permute-start | bytes 1572872 | tf_op jit(solution)/shard_map/while/body/eval_jaxpr/ppermute | solution.py:12
  107.4 7.0 %collective-permute-done = f32[2,256,256]{2,1,0:T(8,128)S(1)} collective-permute-done((f32[2,256,256]{2,1,0:T(8,128)}, f32[2,256,256]{2,1,0:T(8,128)S(1)}, u32[]{:S(2)}, u32[]{:S(2)}) %collective-permute-start) | collective-permute-done | bytes 524320 | tf_op jit(solution)/shard_map/while/body/eval_jaxpr/ppermute | solution.py:12
  116.9 5.5 %collective-permute-start = (f32[2,256,256]{2,1,0:T(8,128)}, f32[2,256,256]{2,1,0:T(8,128)S(1)}, u32[]{:S(2)}, u32[]{:S(2)}) collective-permute-start(f32[2,256,256]{2,1,0:T(8,128)} %convolution_add_fusion.6), channel_id=1, source_target_pairs={{0,1},{1,2},{2,3},{3,4},{4,5},{5,6},{6,7},{8,9},{9,10},{10,11},{11... | collective-permute-start | bytes 1572872 | tf_op jit(solution)/shard_map/while/body/eval_jaxpr/ppermute | solution.py:12
  122.4 7.0 %collective-permute-done = f32[2,256,256]{2,1,0:T(8,128)S(1)} collective-permute-done((f32[2,256,256]{2,1,0:T(8,128)}, f32[2,256,256]{2,1,0:T(8,128)S(1)}, u32[]{:S(2)}, u32[]{:S(2)}) %collective-permute-start) | collective-permute-done | bytes 524320 | tf_op jit(solution)/shard_map/while/body/eval_jaxpr/ppermute | solution.py:12
  133.6 2.6 gather_fusion
  136.2 3.2 %multiply_bitcast_fusion = f32[2,512,256]{2,0,1:T(2,128)} fusion(f32[512,2,256]{2,1,0:T(2,128)S(1)} %gather_fusion, pred[512]{0:T(512)(128)(4,1)S(1)} %get-tuple-element.37, f32[512]{0:T(512)S(1)} %get-tuple-element.36), kind=kLoop, calls=%fused_computation.16 | loop fusion | flops 524288 | bytes 2099712 | tf_op jit(solution)/shard_map/mul | solution.py:74
  139.3 10.7 %all-to-all-start = ((f32[2,512,256]{2,0,1:T(2,128)}), f32[2,512,256]{2,0,1:T(2,128)S(1)}, u32[]{:S(2)}, u32[]{:S(2)}) async-start(f32[2,512,256]{2,0,1:T(2,128)} %multiply_bitcast_fusion), calls=%async_computation | async-start | bytes 2097152 | tf_op jit(solution)/shard_map/all_to_all | solution.py:77
  151.9 27.1 %all-to-all-done = f32[2,512,256]{2,0,1:T(2,128)S(1)} async-done(((f32[2,512,256]{2,0,1:T(2,128)}), f32[2,512,256]{2,0,1:T(2,128)S(1)}, u32[]{:S(2)}, u32[]{:S(2)}) %all-to-all-start) | async-done | bytes 1048608 | tf_op jit(solution)/shard_map/all_to_all | solution.py:77
  178.9 6.0 %all-to-all-start.1 = ((f32[2,512,256]{2,0,1:T(2,128)}), f32[2,512,256]{2,0,1:T(2,128)}, u32[]{:S(2)}, u32[]{:S(2)}) async-start(f32[2,512,256]{2,0,1:T(2,128)} %copy.26), calls=%async_computation.1 | async-start | bytes 2097152 | tf_op jit(solution)/shard_map/all_to_all | solution.py:78
  191.4 22.1 %all-to-all-done.1 = f32[2,512,256]{2,0,1:T(2,128)} async-done(((f32[2,512,256]{2,0,1:T(2,128)}), f32[2,512,256]{2,0,1:T(2,128)}, u32[]{:S(2)}, u32[]{:S(2)}) %all-to-all-start.1) | async-done | bytes 1048608 | tf_op jit(solution)/shard_map/all_to_all | solution.py:78
  213.5 2.6 copy.43
  216.1 2.9 %all_to_all.46 = f32[128,8,256]{2,0,1:T(8,128)} reshape(f32[64,2,8,256]{3,1,0,2:T(2,128)} %bitcast.103) | data formatting | bytes 2097152 | tf_op jit(solution)/shard_map/all_to_all | solution.py:78
  226.3 34.3 %all_to_all.54 = f32[128,8,256]{2,1,0:T(8,128)S(1)} all-to-all(f32[128,8,256]{2,1,0:T(8,128)S(1)} %copy.28), channel_id=1, replica_groups=mesh['energy'=64,'space'=8] {'energy'}, dimensions={0} | all-to-all | bytes 2097152 | tf_op jit(solution)/shard_map/all_to_all | solution.py:42
  (77 shorter events, 48.1 us)
Async XLA Ops:
  0.0 5.1 %copy-start = (f32[2,2,256,256]{3,2,1,0:T(8,128)S(1)}, f32[2,2,256,256]{3,2,1,0:T(8,128)}, u32[]{:S(2)}) copy-start(f32[2,2,256,256]{3,2,1,0:T(8,128)} %param.10) | copy-start | bytes 3145732
  0.0 0.8 copy-start.8
  4.5 1.2 copy-start.2
  8.0 1.3 copy-start.5
  11.0 1.0 copy-start.1
  13.5 17.0 %collective-permute-start = (f32[2,256,256]{2,1,0:T(8,128)}, f32[2,256,256]{2,1,0:T(8,128)S(1)}, u32[]{:S(2)}, u32[]{:S(2)}) collective-permute-start(f32[2,256,256]{2,1,0:T(8,128)} %convolution_add_fusion.6), channel_id=1, source_target_pairs={{0,1},{1,2},{2,3},{3,4},{4,5},{5,6},{6,7},{8,9},{9,10},{10,11},{11... | collective-permute-start | bytes 1572872 | tf_op jit(solution)/shard_map/while/body/eval_jaxpr/ppermute | solution.py:12
  30.5 1.0 copy-start.1
  33.0 16.1 %collective-permute-start = (f32[2,256,256]{2,1,0:T(8,128)}, f32[2,256,256]{2,1,0:T(8,128)S(1)}, u32[]{:S(2)}, u32[]{:S(2)}) collective-permute-start(f32[2,256,256]{2,1,0:T(8,128)} %convolution_add_fusion.6), channel_id=1, source_target_pairs={{0,1},{1,2},{2,3},{3,4},{4,5},{5,6},{6,7},{8,9},{9,10},{10,11},{11... | collective-permute-start | bytes 1572872 | tf_op jit(solution)/shard_map/while/body/eval_jaxpr/ppermute | solution.py:12
  49.1 1.0 copy-start.1
  51.6 15.2 %collective-permute-start = (f32[2,256,256]{2,1,0:T(8,128)}, f32[2,256,256]{2,1,0:T(8,128)S(1)}, u32[]{:S(2)}, u32[]{:S(2)}) collective-permute-start(f32[2,256,256]{2,1,0:T(8,128)} %convolution_add_fusion.6), channel_id=1, source_target_pairs={{0,1},{1,2},{2,3},{3,4},{4,5},{5,6},{6,7},{8,9},{9,10},{10,11},{11... | collective-permute-start | bytes 1572872 | tf_op jit(solution)/shard_map/while/body/eval_jaxpr/ppermute | solution.py:12
  66.8 1.0 copy-start.1
  69.3 14.2 %collective-permute-start = (f32[2,256,256]{2,1,0:T(8,128)}, f32[2,256,256]{2,1,0:T(8,128)S(1)}, u32[]{:S(2)}, u32[]{:S(2)}) collective-permute-start(f32[2,256,256]{2,1,0:T(8,128)} %convolution_add_fusion.6), channel_id=1, source_target_pairs={{0,1},{1,2},{2,3},{3,4},{4,5},{5,6},{6,7},{8,9},{9,10},{10,11},{11... | collective-permute-start | bytes 1572872 | tf_op jit(solution)/shard_map/while/body/eval_jaxpr/ppermute | solution.py:12
  83.5 1.0 copy-start.1
  86.0 13.3 %collective-permute-start = (f32[2,256,256]{2,1,0:T(8,128)}, f32[2,256,256]{2,1,0:T(8,128)S(1)}, u32[]{:S(2)}, u32[]{:S(2)}) collective-permute-start(f32[2,256,256]{2,1,0:T(8,128)} %convolution_add_fusion.6), channel_id=1, source_target_pairs={{0,1},{1,2},{2,3},{3,4},{4,5},{5,6},{6,7},{8,9},{9,10},{10,11},{11... | collective-permute-start | bytes 1572872 | tf_op jit(solution)/shard_map/while/body/eval_jaxpr/ppermute | solution.py:12
  99.4 1.0 copy-start.1
  101.9 12.5 %collective-permute-start = (f32[2,256,256]{2,1,0:T(8,128)}, f32[2,256,256]{2,1,0:T(8,128)S(1)}, u32[]{:S(2)}, u32[]{:S(2)}) collective-permute-start(f32[2,256,256]{2,1,0:T(8,128)} %convolution_add_fusion.6), channel_id=1, source_target_pairs={{0,1},{1,2},{2,3},{3,4},{4,5},{5,6},{6,7},{8,9},{9,10},{10,11},{11... | collective-permute-start | bytes 1572872 | tf_op jit(solution)/shard_map/while/body/eval_jaxpr/ppermute | solution.py:12
  114.4 1.0 copy-start.1
  116.9 12.5 %collective-permute-start = (f32[2,256,256]{2,1,0:T(8,128)}, f32[2,256,256]{2,1,0:T(8,128)S(1)}, u32[]{:S(2)}, u32[]{:S(2)}) collective-permute-start(f32[2,256,256]{2,1,0:T(8,128)} %convolution_add_fusion.6), channel_id=1, source_target_pairs={{0,1},{1,2},{2,3},{3,4},{4,5},{5,6},{6,7},{8,9},{9,10},{10,11},{11... | collective-permute-start | bytes 1572872 | tf_op jit(solution)/shard_map/while/body/eval_jaxpr/ppermute | solution.py:12
  129.4 1.2 copy-start.6
  139.3 10.7 %copy-start.7 = (f32[2,512,256]{2,1,0:T(8,128)S(1)}, f32[2,512,256]{2,1,0:T(8,128)}, u32[]{:S(2)}) copy-start(f32[2,512,256]{2,1,0:T(8,128)} %param.11) | copy-start | bytes 3145732
  139.3 39.6 %all-to-all-start = ((f32[2,512,256]{2,0,1:T(2,128)}), f32[2,512,256]{2,0,1:T(2,128)S(1)}, u32[]{:S(2)}, u32[]{:S(2)}) async-start(f32[2,512,256]{2,0,1:T(2,128)} %multiply_bitcast_fusion), calls=%async_computation | async-start | bytes 2097152 | tf_op jit(solution)/shard_map/all_to_all | solution.py:77
  178.9 34.6 %all-to-all-start.1 = ((f32[2,512,256]{2,0,1:T(2,128)}), f32[2,512,256]{2,0,1:T(2,128)}, u32[]{:S(2)}, u32[]{:S(2)}) async-start(f32[2,512,256]{2,0,1:T(2,128)} %copy.26), calls=%async_computation.1 | async-start | bytes 2097152 | tf_op jit(solution)/shard_map/all_to_all | solution.py:78
  186.6 1.0 copy-start.3
  219.0 2.6 copy-start.4
where the time goes:
time: 263 us; the launch traced here: 262 us
  waiting for transfers between devices  111 us (42%)
  starting transfers between devices  55.1 us (21%)
  matrix products  37.2 us (14%)
  blocking collectives  34.3 us (13%)
  local copies, waits for them, and re-layouts  18.8 us (7%)
  other arithmetic  3.31 us (1%)
    ppermute x7, waiting for transfers between devices, shifted(): return lax.ppermute(shard, axis, pairs)  62.3 us
    ppermute x7, starting transfers between devices, shifted(): return lax.ppermute(shard, axis, pairs)  38.4 us
    all_to_all x1, blocking collectives, convolve(): lax.all_to_all(sigma, 'energy', split_axis=0, concat_axis=1, tiled=True)  34.3 us
    all_to_all x1, waiting for transfers between devices, body(): lax.all_to_all(picked, 'energy', split_axis=1, concat_axis=0, tiled=True)  27.1 us
    dot_general x27, matrix products, mult(): return jnp.matmul(left, right, precision=lax.Precision.HIGHEST)  26.8 us
    all_to_all x1, waiting for transfers between devices, body(): lax.all_to_all(screened, 'energy', split_axis=1, concat_axis=0, tiled=True)  22.1 us
    all_to_all x1, starting transfers between devices, body(): lax.all_to_all(picked, 'energy', split_axis=1, concat_axis=0, tiled=True)  10.7 us
    all_to_all x1, starting transfers between devices, body(): lax.all_to_all(screened, 'energy', split_axis=1, concat_axis=0, tiled=True)  6.04 us
  transfers between devices with their start and end apart: 9, of which 9 were waited for; matrix products, arithmetic and copies ran while one was open for 2% of the time, Pallas kernels for 0%

commit v1 on v0

v1 whole, which is shorter than its diff:
```python
import functools
import math

import jax
import jax.numpy as jnp
import numpy as np
from jax import lax
from jax.experimental import pallas as pl
from jax.experimental.pallas import tpu as pltpu
from jax.sharding import PartitionSpec as P

BF = jnp.bfloat16
F32 = jnp.float32
VMEM = pl.BlockSpec(memory_space=pltpu.VMEM)
SMEM = pl.BlockSpec(memory_space=pltpu.SMEM)
ANY = pl.BlockSpec(memory_space=pl.ANY)


def params():
    return pltpu.CompilerParams(vmem_limit_bytes=48 * 1024 * 1024)


def cost(products, size=256):
    return pl.CostEstimate(flops=int(products * 3 * 2 * size**3), bytes_accessed=1 << 20, transcendentals=0)


def split(value):
    high = value.astype(BF)
    return high, (value - high.astype(F32)).astype(BF)


def product(left, right, right_dim=0):
    dims = (((1,), (right_dim,)), ((), ()))

    def one(a, b):
        return lax.dot_general(a, b, dims, preferred_element_type=F32)

    return one(left[0], right[0]) + (one(left[0], right[1]) + one(left[1], right[0]))


def sandwich(outer, inner):
    return product(split(product(outer, inner)), outer, 1)


def prepare_kernel(inv_ref, coup_ref, src_ref, map_h, map_l, add, first_h, first_l, inject):
    inv0, inv1 = split(inv_ref[0, 0]), split(inv_ref[0, 1])
    step0 = split(product(inv0, split(coup_ref[0])))
    inj0 = sandwich(inv0, split(src_ref[0, 0]))
    step1 = split(product(inv1, split(coup_ref[1])))
    inj1 = sandwich(inv1, split(src_ref[0, 1]))
    add[...] = sandwich(step1, split(inj0)) + inj1
    map_h[...], map_l[...] = split(product(step1, step0))
    first_h[...], first_l[...] = step0
    inject[...] = inj0


def prepare(inverses, coupling, source, energy):
    width = coupling.shape[1]
    square = lambda kind: jax.ShapeDtypeStruct((width, width), kind)
    block = pl.BlockSpec((1, 2, width, width), lambda i: (energy, 0, 0, 0))
    whole = pl.BlockSpec((width, width), lambda i: (0, 0))
    return pl.pallas_call(
        prepare_kernel,
        grid=(1,),
        in_specs=[block, pl.BlockSpec((2, width, width), lambda i: (0, 0, 0)), block],
        out_specs=[whole] * 6,
        out_shape=[square(BF), square(BF), square(F32), square(BF), square(BF), square(F32)],
        compiler_params=params(),
        cost_estimate=cost(9),
        name="prepare",
    )(inverses, coupling, source)


def hop_kernel(step, place, state, map_h, map_l, add, out):
    @pl.when(place[0] == step + 1)
    def _():
        out[...] = sandwich((map_h[...], map_l[...]), split(state[...])) + add[...]


def hop(step, place, state, given):
    return pl.pallas_call(
        functools.partial(hop_kernel, step),
        in_specs=[SMEM] + [VMEM] * 4,
        out_specs=VMEM,
        out_shape=jax.ShapeDtypeStruct(state.shape, F32),
        compiler_params=params(),
        cost_estimate=cost(2),
        name="hop",
    )(place, state, *given[:3])


def pick_kernel(count, place, live, rows, *refs):
    states = refs[: 2 * count]
    given = refs[2 * count : 2 * count + 12]
    out, entry, sem = refs[2 * count + 12 :]
    here = place[0]
    width = entry.shape[1]

    @pl.when(here == 0)
    def _():
        entry[...] = jnp.zeros_like(entry)

    for step in range(count):

        @pl.when(here == step + 1)
        def _():
            copies = [pltpu.make_async_copy(states[e * count + step], entry.at[e], sem.at[e]) for e in range(2)]
            for copy in copies:
                copy.start()
            for copy in copies:
                copy.wait()

    slots = rows.shape[0]
    column = lax.broadcasted_iota(jnp.int32, (slots, 2 * width), 1)
    slot = lax.broadcasted_iota(jnp.int32, (slots, 2 * width), 0)
    chosen = jnp.where((column == rows[...]) & (slot < live[0]), 1.0, 0.0).astype(BF)
    for e in range(2):
        map_h, map_l, add, first_h, first_l, inject = given[6 * e : 6 * e + 6]
        state = split(entry[e])
        last = sandwich((map_h[...], map_l[...]), state) + add[...]
        first = sandwich((first_h[...], first_l[...]), state) + inject[...]
        high, low = split(jnp.concatenate([first, last], axis=0))
        dot = lambda a, b: jnp.dot(a, b, preferred_element_type=F32)
        picked = dot(chosen, high) + dot(chosen, low)
        out[:, e] = picked.reshape(slots // 8, 8, width)


def pick(place, live, rows, states, given):
    width = given[0][2].shape[0]
    slots = rows.shape[0]
    count = len(states[0])
    return pl.pallas_call(
        functools.partial(pick_kernel, count),
        in_specs=[SMEM, SMEM, VMEM] + [ANY] * (2 * count) + [VMEM] * 12,
        out_specs=VMEM,
        out_shape=jax.ShapeDtypeStruct((slots // 8, 2, 8, width), F32),
        scratch_shapes=[pltpu.VMEM((2, width, width), F32), pltpu.SemaphoreType.DMA((2,))],
        compiler_params=params(),
        cost_estimate=cost(16),
        name="pick",
    )(place, live, rows, *states[0], *states[1], *given[0], *given[1])


def transforms(count):
    half = count // 2
    points = np.arange(count)
    waves = np.arange(half)
    angle = 2.0 * math.pi * ((waves[:, None] * points[None, :]) % count) / count
    forward = np.concatenate([np.cos(angle), -np.sin(angle)], axis=0)
    forward[half] = np.where(points % 2 == 0, 1.0, -1.0)
    weight = np.full(count, 2.0 / count)
    weight[[0, half]] = 1.0 / count
    return forward.astype(np.float32), (forward.T * weight[None, :]).astype(np.float32)


def spectrum_kernel(fwd_h, fwd_l, data, out):
    for j in range(data.shape[1]):
        out[j] = product((fwd_h[...], fwd_l[...]), split(data[:, j]))


def spectrum(matrix, data):
    count, group, width = data.shape
    return pl.pallas_call(
        spectrum_kernel,
        in_specs=[VMEM] * 3,
        out_specs=VMEM,
        out_shape=jax.ShapeDtypeStruct((group, count, width), F32),
        compiler_params=params(),
        cost_estimate=cost(2),
        name="spectrum",
    )(*matrix, data)


def convolve_kernel(fwd_h, fwd_l, inv_h, inv_l, data, other, out):
    count = data.shape[0]
    half = count // 2
    single = lax.broadcasted_iota(jnp.int32, (half, data.shape[2]), 0) == 0
    for j in range(data.shape[1]):
        left = product((fwd_h[...], fwd_l[...]), split(data[:, j]))
        right = other[j]
        real_a, imag_a = left[:half], left[half:]
        real_b, imag_b = right[:half], right[half:]
        real_p = real_a * real_b - jnp.where(single, 0.0, imag_a * imag_b)
        imag_p = jnp.where(single, imag_a * imag_b, real_a * imag_b + imag_a * real_b)
        both = jnp.concatenate([real_p, imag_p], axis=0)
        out[:, j] = product((inv_h[...], inv_l[...]), split(both))


def convolve(forward, inverse, data, other):
    count, group, width = data.shape
    return pl.pallas_call(
        convolve_kernel,
        in_specs=[VMEM] * 6,
        out_specs=VMEM,
        out_shape=jax.ShapeDtypeStruct((count, group, width), F32),
        compiler_params=params(),
        cost_estimate=cost(4),
        name="convolve",
    )(*forward, *inverse, data, other)


def exchange(chunks):
    return lax.all_to_all(chunks, "energy", split_axis=0, concat_axis=0, tiled=True)


def body(inverses, coupling, source, screened, kept_rows, live_count):
    energies, slots, width = screened.shape
    parts = lax.axis_size("energy")
    spaces = lax.axis_size("space")
    place = lax.axis_index("space").astype(jnp.int32).reshape(1)
    group = slots // parts
    count = energies * parts
    forward, inverse = [split(jnp.asarray(m)) for m in transforms(count)]

    chunks = screened.reshape(energies, parts, group, width).swapaxes(0, 1)
    other = spectrum(forward, exchange(chunks).reshape(count, group, width))

    given = [prepare(inverses, coupling, source, e) for e in range(energies)]
    outgoing = [given[e][2] for e in range(energies)]
    states = [[], []]
    for step in range(spaces - 1):
        for e in range(energies):
            state = lax.ppermute(outgoing[e], "space", [(step, step + 1)])
            states[e].append(state)
            if step + 2 < spaces:
                outgoing[e] = hop(step, place, state, given[e])

    picked = pick(place, live_count, kept_rows.reshape(slots, 1), states, given)
    data = exchange(picked).reshape(count, group, width)
    sigma = convolve(forward, inverse, data, other)
    back = exchange(sigma.reshape(parts, energies, group, width))
    return back.swapaxes(0, 1).reshape(energies, slots, width)


def solution(mesh):
    return jax.shard_map(
        body,
        mesh=mesh,
        in_specs=(
            P("energy", "space", None, None),
            P("space", None, None),
            P("energy", "space", None, None),
            P("energy", "space", None),
            P("space"),
            P("space"),
        ),
        out_specs=P("energy", "space", None),
        check_vma=False,
    )
```

time: 263 us -> 176 us (0.67)
  the two profiles are of different devices: /device:TPU:192 before, /device:TPU:448 now
where the time goes in v1:
time: 176 us; the launch traced here: 174 us
  waiting for transfers between devices  57 us (32%)
  blocking collectives  34.2 us (19%)
  starting transfers between devices  32.6 us (19%)
  local copies, waits for them, and re-layouts  32.2 us (18%)
  Pallas kernels  17.2 us (10%)
    all_to_all x1, blocking collectives, exchange(): lax.all_to_all(chunks, 'energy', split_axis=0, concat_axis=0, tiled=True)  34.2 us
    ppermute x14, waiting for transfers between devices, body(): state = lax.ppermute(outgoing[e], 'space', [(step, step + 1)])  32.9 us
    unnamed x88, local copies, waits for them, and re-layouts  29.8 us
    all_to_all x2, waiting for transfers between devices, exchange(): lax.all_to_all(chunks, 'energy', split_axis=0, concat_axis=0, tiled=True)  24.2 us
    all_to_all x2, starting transfers between devices, exchange(): lax.all_to_all(chunks, 'energy', split_axis=0, concat_axis=0, tiled=True)  21.3 us
    ppermute x14, starting transfers between devices, body(): state = lax.ppermute(outgoing[e], 'space', [(step, step + 1)])  11.3 us
    pallas_call x1, Pallas kernels, pick(): pl.pallas_call(functools.partial(pick_kernel, count), in_specs=[SMEM, SME...  4.17 us
    pallas_call x1, Pallas kernels, convolve(): pl.pallas_call(convolve_kernel, in_specs=[VMEM] * 6, out_specs=VMEM, out_...  4.16 us
  transfers between devices with their start and end apart: 16, of which 3 were waited for; matrix products, arithmetic and copies ran while one was open for 1% of the time, Pallas kernels for 7%

profile of v1, /device:TPU:448, one launch (start us, length us, event | category | flops | bytes accessed | tf_op | source)
XLA Modules:
  0.0 174.4 jit_solution(9376481112071772472)
XLA Ops:
  0.0 1.3 copy-done.39
  1.3 1.2 copy-done.40
  2.5 1.0 copy-done.42
  3.6 1.4 prepare.3
  7.0 1.4 prepare.2
  9.8 1.4 collective-permute-start
  11.2 1.2 copy_bitcast_fusion.1
  12.4 10.6 %all-to-all-start.1 = ((f32[64,2,8,256]{3,2,1,0:T(8,128)}), f32[64,2,8,256]{3,2,1,0:T(8,128)S(1)}, u32[]{:S(2)}, u32[]{:S(2)}) async-start(f32[64,2,8,256]{3,2,1,0:T(8,128)} %copy_bitcast_fusion.1), calls=%async_computation.1 | async-start | bytes 2097152 | tf_op jit(solution)/shard_map/all_to_all | solution.py:203
  24.4 1.0 hop.12
  38.0 1.3 collective-permute-start.13
  40.1 1.3 collective-permute-start.6
  42.2 27.4 %collective-permute-done.13.refs_13_ = f32[256,256]{1,0:T(8,128)} collective-permute-done((f32[256,256]{1,0:T(8,128)}, f32[256,256]{1,0:T(8,128)}, u32[]{:S(2)}, u32[]{:S(2)}) %collective-permute-start.13) | collective-permute-done | bytes 262176 | tf_op jit(solution)/shard_map/ppermute | solution.py:223
  69.6 5.4 %collective-permute-done.6.refs_6_ = f32[256,256]{1,0:T(8,128)} collective-permute-done((f32[256,256]{1,0:T(8,128)}, f32[256,256]{1,0:T(8,128)}, u32[]{:S(2)}, u32[]{:S(2)}) %collective-permute-start.6) | collective-permute-done | bytes 262176 | tf_op jit(solution)/shard_map/ppermute | solution.py:223
  75.0 0.9 copy-done.4
  76.0 0.9 copy-done.6
  90.1 4.2 %pick.1 = f32[64,2,8,256]{3,2,1,0:T(8,128)} custom-call(s32[1]{0:T(128)} %bitcast.place, s32[1]{0:T(128)S(6)} %copy.16.live, s32[512,1]{1,0:T(8,128)S(1)} %copy.11.rows, f32[256,256]{1,0:T(8,128)} %collective-permute-done.state.refs_0_, f32[256,256]{1,0:T(8,128)S(1)} %copy-done.8, f32[256,256]{1,0:T(8,128)S(1)} %copy-done.12, f32[256,256]{1,0:T(8,128)S(1)} %copy-done.16, ...), custom_call_target="tpu_custom_call" | custom-call | flops 1610612736 | bytes 1048576 | tf_op jit(solution)/shard_map/pick/pallas_call | solution.py:132
  94.3 1.0 copy-done.1
  95.3 10.7 %all-to-all-start = ((f32[64,2,8,256]{3,2,1,0:T(8,128)}), f32[64,2,8,256]{3,2,1,0:T(8,128)S(1)}, u32[]{:S(2)}, u32[]{:S(2)}) async-start(f32[64,2,8,256]{3,2,1,0:T(8,128)} %pick.1), calls=%async_computation | async-start | bytes 2097152 | tf_op jit(solution)/shard_map/all_to_all | solution.py:203
  106.1 1.2 copy-done.2
  107.3 3.5 %spectrum.1.other = f32[8,128,256]{2,1,0:T(8,128)S(1)} custom-call(bf16[128,128]{1,0:T(8,128)(2,1)S(1)} %copy-done.29, bf16[128,128]{1,0:T(8,128)(2,1)S(1)} %copy-done.30, f32[128,8,256]{2,1,0:T(8,128)S(1)} %bitcast.17), custom_call_target="tpu_custom_call" | custom-call | flops 201326592 | bytes 1048576 | tf_op jit(solution)/shard_map/spectrum/pallas_call | solution.py:163
  110.8 24.2 %all-to-all-done = f32[64,2,8,256]{3,2,1,0:T(8,128)S(1)} async-done(((f32[64,2,8,256]{3,2,1,0:T(8,128)}), f32[64,2,8,256]{3,2,1,0:T(8,128)S(1)}, u32[]{:S(2)}, u32[]{:S(2)}) %all-to-all-start) | async-done | bytes 1048608 | tf_op jit(solution)/shard_map/all_to_all | solution.py:203
  135.0 4.2 %convolve.1 = f32[128,8,256]{2,1,0:T(8,128)S(1)} custom-call(bf16[128,128]{1,0:T(8,128)(2,1)S(1)} %copy-done.29, bf16[128,128]{1,0:T(8,128)(2,1)S(1)} %copy-done.30, bf16[128,128]{1,0:T(8,128)(2,1)S(1)} %copy-done.37, bf16[128,128]{1,0:T(8,128)(2,1)S(1)} %copy-done.38, f32[128,8,256]{2,1,0:T(8,128)S(1)} %bitcast.15, f32[8,128,256]{2,1,0:T(8,128)S(1)} %spectrum.1.other), custom_call_target="tpu_custom_call" | custom-call | flops 402653184 | bytes 1048576 | tf_op jit(solution)/shard_map/convolve/pallas_call | solution.py:191
  139.1 34.2 %all_to_all.15 = f32[64,2,8,256]{3,2,1,0:T(8,128)S(1)} all-to-all(f32[64,2,8,256]{3,2,1,0:T(8,128)S(1)} %bitcast.16), channel_id=1, replica_groups=mesh['energy'=64,'space'=8] {'energy'}, dimensions={0} | all-to-all | bytes 2097152 | tf_op jit(solution)/shard_map/all_to_all | solution.py:203
  173.4 1.1 copy_bitcast_fusion
  (117 shorter events, 31.2 us)
Async XLA Ops:
  0.0 11.2 %copy-start = (f32[2,512,256]{2,1,0:T(8,128)S(1)}, f32[2,512,256]{2,1,0:T(8,128)}, u32[]{:S(2)}) copy-start(f32[2,512,256]{2,1,0:T(8,128)} %param.11) | copy-start | bytes 3145732
  3.6 3.4 %copy-start.41 = (f32[2,2,256,256]{3,2,1,0:T(8,128)S(1)}, f32[2,2,256,256]{3,2,1,0:T(8,128)}, u32[]{:S(2)}) copy-start(f32[2,2,256,256]{3,2,1,0:T(8,128)} %src_ref.3) | copy-start | bytes 3145732
  6.4 16.6 %collective-permute-start.7 = (f32[256,256]{1,0:T(8,128)S(1)}, f32[256,256]{1,0:T(8,128)S(1)}, u32[]{:S(2)}, u32[]{:S(2)}) collective-permute-start(f32[256,256]{1,0:T(8,128)S(1)} %get-tuple-element.20.add.refs_22_), channel_id=1, source_target_pairs={{0,1},{8,9},{16,17},{24,25},{32,33},{40,41},{48,49},{56,57},{64,65... | collective-permute-start | bytes 786440 | tf_op jit(solution)/shard_map/ppermute | solution.py:223
  9.8 2.6 %copy-start.35 = (bf16[256,256]{1,0:T(8,128)(2,1)}, bf16[256,256]{1,0:T(8,128)(2,1)S(1)}, u32[]{:S(2)}) copy-start(bf16[256,256]{1,0:T(8,128)(2,1)S(1)} %get-tuple-element.24.refs_18_) | copy-start | bytes 393220
  9.8 14.5 %collective-permute-start = (f32[256,256]{1,0:T(8,128)S(1)}, f32[256,256]{1,0:T(8,128)}, u32[]{:S(2)}, u32[]{:S(2)}) collective-permute-start(f32[256,256]{1,0:T(8,128)S(1)} %get-tuple-element.17.add.refs_16_), channel_id=1, source_target_pairs={{0,1},{8,9},{16,17},{24,25},{32,33},{40,41},{48,49},{56,57},{64,65... | collective-permute-start | bytes 786440 | tf_op jit(solution)/shard_map/ppermute | solution.py:223
  12.4 81.9 %all-to-all-start.1 = ((f32[64,2,8,256]{3,2,1,0:T(8,128)}), f32[64,2,8,256]{3,2,1,0:T(8,128)S(1)}, u32[]{:S(2)}, u32[]{:S(2)}) async-start(f32[64,2,8,256]{3,2,1,0:T(8,128)} %copy_bitcast_fusion.1), calls=%async_computation.1 | async-start | bytes 2097152 | tf_op jit(solution)/shard_map/all_to_all | solution.py:203
  23.7 2.3 %collective-permute-start.8 = (f32[256,256]{1,0:T(8,128)S(1)}, f32[256,256]{1,0:T(8,128)S(1)}, u32[]{:S(2)}, u32[]{:S(2)}) collective-permute-start(f32[256,256]{1,0:T(8,128)S(1)} %hop.18), channel_id=1, source_target_pairs={{1,2},{9,10},{17,18},{25,26},{33,34},{41,42},{49,50},{57,58},{65,6... | collective-permute-start | bytes 786440 | tf_op jit(solution)/shard_map/ppermute | solution.py:223
  25.3 2.1 %collective-permute-start.1 = (f32[256,256]{1,0:T(8,128)S(1)}, f32[256,256]{1,0:T(8,128)S(1)}, u32[]{:S(2)}, u32[]{:S(2)}) collective-permute-start(f32[256,256]{1,0:T(8,128)S(1)} %hop.12), channel_id=1, source_target_pairs={{1,2},{9,10},{17,18},{25,26},{33,34},{41,42},{49,50},{57,58},{65,6... | collective-permute-start | bytes 786440 | tf_op jit(solution)/shard_map/ppermute | solution.py:223
  26.7 2.1 %collective-permute-start.9 = (f32[256,256]{1,0:T(8,128)S(1)}, f32[256,256]{1,0:T(8,128)S(1)}, u32[]{:S(2)}, u32[]{:S(2)}) collective-permute-start(f32[256,256]{1,0:T(8,128)S(1)} %hop.19), channel_id=1, source_target_pairs={{2,3},{10,11},{18,19},{26,27},{34,35},{42,43},{50,51},{58,59},{66,... | collective-permute-start | bytes 786440 | tf_op jit(solution)/shard_map/ppermute | solution.py:223
  28.1 2.1 %collective-permute-start.2 = (f32[256,256]{1,0:T(8,128)S(1)}, f32[256,256]{1,0:T(8,128)S(1)}, u32[]{:S(2)}, u32[]{:S(2)}) collective-permute-start(f32[256,256]{1,0:T(8,128)S(1)} %hop.13), channel_id=1, source_target_pairs={{2,3},{10,11},{18,19},{26,27},{34,35},{42,43},{50,51},{58,59},{66,... | collective-permute-start | bytes 786440 | tf_op jit(solution)/shard_map/ppermute | solution.py:223
  29.5 2.1 %collective-permute-start.10 = (f32[256,256]{1,0:T(8,128)S(1)}, f32[256,256]{1,0:T(8,128)S(1)}, u32[]{:S(2)}, u32[]{:S(2)}) collective-permute-start(f32[256,256]{1,0:T(8,128)S(1)} %hop.20), channel_id=1, source_target_pairs={{3,4},{11,12},{19,20},{27,28},{35,36},{43,44},{51,52},{59,60},{67,... | collective-permute-start | bytes 786440 | tf_op jit(solution)/shard_map/ppermute | solution.py:223
  30.9 2.1 %collective-permute-start.3 = (f32[256,256]{1,0:T(8,128)S(1)}, f32[256,256]{1,0:T(8,128)S(1)}, u32[]{:S(2)}, u32[]{:S(2)}) collective-permute-start(f32[256,256]{1,0:T(8,128)S(1)} %hop.14), channel_id=1, source_target_pairs={{3,4},{11,12},{19,20},{27,28},{35,36},{43,44},{51,52},{59,60},{67,... | collective-permute-start | bytes 786440 | tf_op jit(solution)/shard_map/ppermute | solution.py:223
  32.3 2.1 %collective-permute-start.11 = (f32[256,256]{1,0:T(8,128)S(1)}, f32[256,256]{1,0:T(8,128)S(1)}, u32[]{:S(2)}, u32[]{:S(2)}) collective-permute-start(f32[256,256]{1,0:T(8,128)S(1)} %hop.21), channel_id=1, source_target_pairs={{4,5},{12,13},{20,21},{28,29},{36,37},{44,45},{52,53},{60,61},{68,... | collective-permute-start | bytes 786440 | tf_op jit(solution)/shard_map/ppermute | solution.py:223
  33.7 2.1 %collective-permute-start.4 = (f32[256,256]{1,0:T(8,128)S(1)}, f32[256,256]{1,0:T(8,128)S(1)}, u32[]{:S(2)}, u32[]{:S(2)}) collective-permute-start(f32[256,256]{1,0:T(8,128)S(1)} %hop.15), channel_id=1, source_target_pairs={{4,5},{12,13},{20,21},{28,29},{36,37},{44,45},{52,53},{60,61},{68,... | collective-permute-start | bytes 786440 | tf_op jit(solution)/shard_map/ppermute | solution.py:223
  35.1 2.1 %collective-permute-start.12 = (f32[256,256]{1,0:T(8,128)S(1)}, f32[256,256]{1,0:T(8,128)S(1)}, u32[]{:S(2)}, u32[]{:S(2)}) collective-permute-start(f32[256,256]{1,0:T(8,128)S(1)} %hop.22), channel_id=1, source_target_pairs={{5,6},{13,14},{21,22},{29,30},{37,38},{45,46},{53,54},{61,62},{69,... | collective-permute-start | bytes 786440 | tf_op jit(solution)/shard_map/ppermute | solution.py:223
  36.5 2.8 %collective-permute-start.5 = (f32[256,256]{1,0:T(8,128)S(1)}, f32[256,256]{1,0:T(8,128)S(1)}, u32[]{:S(2)}, u32[]{:S(2)}) collective-permute-start(f32[256,256]{1,0:T(8,128)S(1)} %hop.16), channel_id=1, source_target_pairs={{5,6},{13,14},{21,22},{29,30},{37,38},{45,46},{53,54},{61,62},{69,... | collective-permute-start | bytes 786440 | tf_op jit(solution)/shard_map/ppermute | solution.py:223
  38.0 31.6 %collective-permute-start.13 = (f32[256,256]{1,0:T(8,128)}, f32[256,256]{1,0:T(8,128)}, u32[]{:S(2)}, u32[]{:S(2)}) collective-permute-start(f32[256,256]{1,0:T(8,128)} %hop.23), channel_id=1, source_target_pairs={{6,7},{14,15},{22,23},{30,31},{38,39},{46,47},{54,55},{62,63},{70,... | collective-permute-start | bytes 786440 | tf_op jit(solution)/shard_map/ppermute | solution.py:223
  39.3 2.1 %copy-start.43 = (s32[512]{0:T(512)S(1)}, s32[512]{0:T(512)}, u32[]{:S(2)}) copy-start(s32[512]{0:T(512)} %param.12) | copy-start | bytes 6148
  40.1 34.9 %collective-permute-start.6 = (f32[256,256]{1,0:T(8,128)}, f32[256,256]{1,0:T(8,128)}, u32[]{:S(2)}, u32[]{:S(2)}) collective-permute-start(f32[256,256]{1,0:T(8,128)} %hop.17), channel_id=1, source_target_pairs={{6,7},{14,15},{22,23},{30,31},{38,39},{46,47},{54,55},{62,63},{70,... | collective-permute-start | bytes 786440 | tf_op jit(solution)/shard_map/ppermute | solution.py:223
  94.3 11.8 %copy-start.29 = (bf16[128,128]{1,0:T(8,128)(2,1)S(1)}, bf16[128,128]{1,0:T(8,128)(2,1)}, u32[]{:S(2)}) copy-start(bf16[128,128]{1,0:T(8,128)(2,1)} %constant.15.fwd_h) | copy-start | bytes 98308
  94.3 11.8 %copy-start.30 = (bf16[128,128]{1,0:T(8,128)(2,1)S(1)}, bf16[128,128]{1,0:T(8,128)(2,1)}, u32[]{:S(2)}) copy-start(bf16[128,128]{1,0:T(8,128)(2,1)} %constant.18.fwd_l) | copy-start | bytes 98308
  95.3 39.6 %all-to-all-start = ((f32[64,2,8,256]{3,2,1,0:T(8,128)}), f32[64,2,8,256]{3,2,1,0:T(8,128)S(1)}, u32[]{:S(2)}, u32[]{:S(2)}) async-start(f32[64,2,8,256]{3,2,1,0:T(8,128)} %pick.1), calls=%async_computation | async-start | bytes 2097152 | tf_op jit(solution)/shard_map/all_to_all | solution.py:203
  107.3 27.6 %copy-start.37 = (bf16[128,128]{1,0:T(8,128)(2,1)S(1)}, bf16[128,128]{1,0:T(8,128)(2,1)}, u32[]{:S(2)}) copy-start(bf16[128,128]{1,0:T(8,128)(2,1)} %constant.19.inv_h) | copy-start | bytes 98308
  107.3 27.6 %copy-start.38 = (bf16[128,128]{1,0:T(8,128)(2,1)S(1)}, bf16[128,128]{1,0:T(8,128)(2,1)}, u32[]{:S(2)}) copy-start(bf16[128,128]{1,0:T(8,128)(2,1)} %constant.22.inv_l) | copy-start | bytes 98308
  (36 other events, 31.6 us)

commit v2 on v1

v2 whole, which is shorter than its diff:
```python
import functools
import math

import jax
import jax.numpy as jnp
import numpy as np
from jax import lax
from jax.experimental import pallas as pl
from jax.experimental.pallas import tpu as pltpu
from jax.sharding import PartitionSpec as P

BF = jnp.bfloat16
F32 = jnp.float32
VMEM = pl.BlockSpec(memory_space=pltpu.VMEM)
SMEM = pl.BlockSpec(memory_space=pltpu.SMEM)
HBM = pl.BlockSpec(memory_space=pltpu.HBM)


def params(mebibytes=8):
    return pltpu.CompilerParams(vmem_limit_bytes=mebibytes * 1024 * 1024)


def cost(products, size=256):
    return pl.CostEstimate(flops=int(products * 3 * 2 * size**3), bytes_accessed=1 << 20, transcendentals=0)


def split(value):
    high = value.astype(BF)
    return high, (value - high.astype(F32)).astype(BF)


def product(left, right, right_dim=0):
    dims = (((1,), (right_dim,)), ((), ()))

    def one(a, b):
        return lax.dot_general(a, b, dims, preferred_element_type=F32)

    return one(left[0], right[0]) + (one(left[0], right[1]) + one(left[1], right[0]))


def sandwich(outer, inner):
    return product(split(product(outer, inner)), outer, 1)


def prepare_kernel(energy, inv_all, coup_all, src_all, map_h, map_l, add, first_h, first_l, inject, inv, coup, src, sem):
    copies = {}
    for b in range(2):
        for n, (name, source, target) in enumerate(
            (("inv", inv_all.at[energy, b], inv), ("coup", coup_all.at[b], coup), ("src", src_all.at[energy, b], src))
        ):
            copies[name, b] = pltpu.make_async_copy(source, target.at[b], sem.at[3 * b + n])
            copies[name, b].start()
    copies["inv", 0].wait()
    copies["coup", 0].wait()
    inv0 = split(inv[0])
    step0 = split(product(inv0, split(coup[0])))
    copies["src", 0].wait()
    inj0 = sandwich(inv0, split(src[0]))
    copies["inv", 1].wait()
    copies["coup", 1].wait()
    inv1 = split(inv[1])
    step1 = split(product(inv1, split(coup[1])))
    copies["src", 1].wait()
    inj1 = sandwich(inv1, split(src[1]))
    add[...] = sandwich(step1, split(inj0)) + inj1
    map_h[...], map_l[...] = split(product(step1, step0))
    first_h[...], first_l[...] = step0
    inject[...] = inj0


def prepare(inverses, coupling, source, energy):
    width = coupling.shape[1]
    square = lambda kind: jax.ShapeDtypeStruct((width, width), kind)
    pair = pltpu.VMEM((2, width, width), F32)
    return pl.pallas_call(
        functools.partial(prepare_kernel, energy),
        in_specs=[HBM] * 3,
        out_specs=[VMEM] * 6,
        out_shape=[square(BF), square(BF), square(F32), square(BF), square(BF), square(F32)],
        scratch_shapes=[pair, pair, pair, pltpu.SemaphoreType.DMA((6,))],
        compiler_params=params(12),
        cost_estimate=cost(9),
        name="prepare",
    )(inverses, coupling, source)


def hop_kernel(step, place, state, map_h, map_l, add, out):
    @pl.when(place[0] == step + 1)
    def _():
        out[...] = sandwich((map_h[...], map_l[...]), split(state[...])) + add[...]


def hop(step, place, state, given):
    return pl.pallas_call(
        functools.partial(hop_kernel, step),
        in_specs=[SMEM] + [VMEM] * 4,
        out_specs=VMEM,
        out_shape=jax.ShapeDtypeStruct(state.shape, F32),
        compiler_params=params(),
        cost_estimate=cost(2),
        name="hop",
    )(place, state, *given[:3])


def pick_kernel(energy, count, place, live, rows, *refs):
    states = refs[:count]
    map_h, map_l, add, first_h, first_l, inject = refs[count : count + 6]
    out, entry, picked, sem = refs[-4:]
    here = place[0]
    width = entry.shape[1]

    @pl.when(here == 0)
    def _():
        entry[...] = jnp.zeros_like(entry)

    for step in range(count):

        @pl.when(here == step + 1)
        def _():
            entry[...] = states[step][...]

    slots = rows.shape[0]
    column = lax.broadcasted_iota(jnp.int32, (slots, 2 * width), 1)
    slot = lax.broadcasted_iota(jnp.int32, (slots, 2 * width), 0)
    chosen = jnp.where((column == rows[...]) & (slot < live[0]), 1.0, 0.0).astype(BF)
    state = split(entry[...])
    last = sandwich((map_h[...], map_l[...]), state) + add[...]
    first = sandwich((first_h[...], first_l[...]), state) + inject[...]
    high, low = split(jnp.concatenate([first, last], axis=0))
    dot = lambda a, b: jnp.dot(a, b, preferred_element_type=F32)
    picked[...] = (dot(chosen, high) + dot(chosen, low)).reshape(picked.shape)
    copy = pltpu.make_async_copy(picked, out.at[:, energy], sem)
    copy.start()
    copy.wait()


def pick(energy, place, live, rows, states, given, before=None):
    width = given[2].shape[0]
    slots = rows.shape[0]
    count = len(states)
    operands = [place, live, rows, *states, *given]
    specs = [SMEM, SMEM] + [VMEM] * (len(operands) - 2)
    aliases = {}
    if before is not None:
        aliases = {len(operands): 0}
        operands.append(before)
        specs.append(HBM)
    return pl.pallas_call(
        functools.partial(pick_kernel, energy, count),
        in_specs=specs,
        out_specs=HBM,
        out_shape=jax.ShapeDtypeStruct((slots // 8, 2, 8, width), F32),
        scratch_shapes=[
            pltpu.VMEM((width, width), F32),
            pltpu.VMEM((slots // 8, 8, width), F32),
            pltpu.SemaphoreType.DMA,
        ],
        input_output_aliases=aliases,
        compiler_params=params(12),
        cost_estimate=cost(8),
        name="pick",
    )(*operands)


def transforms(count):
    half = count // 2
    points = np.arange(count)
    waves = np.arange(half)
    angle = 2.0 * math.pi * ((waves[:, None] * points[None, :]) % count) / count
    forward = np.concatenate([np.cos(angle), -np.sin(angle)], axis=0)
    forward[half] = np.where(points % 2 == 0, 1.0, -1.0)
    weight = np.full(count, 2.0 / count)
    weight[[0, half]] = 1.0 / count
    return forward.astype(np.float32), (forward.T * weight[None, :]).astype(np.float32)


def stacked(matrix):
    high, low = split(jnp.asarray(matrix))
    return jnp.concatenate(
        [jnp.concatenate([high, high], axis=1), jnp.concatenate([low, jnp.zeros_like(low)], axis=1)], axis=0
    )


def apply(matrix, data):
    both = jnp.dot(matrix, jnp.concatenate(split(data), axis=0), preferred_element_type=F32)
    return both[: data.shape[0]] + both[data.shape[0] :]


def spectrum_kernel(fwd, data, out):
    for j in range(data.shape[1]):
        out[j] = apply(fwd[...], data[:, j])


def spectrum(forward, data):
    count, group, width = data.shape
    return pl.pallas_call(
        spectrum_kernel,
        in_specs=[VMEM] * 2,
        out_specs=VMEM,
        out_shape=jax.ShapeDtypeStruct((group, count, width), F32),
        compiler_params=params(),
        cost_estimate=cost(2),
        name="spectrum",
    )(forward, data)


def convolve_kernel(fwd, inv, data, other, out):
    count = data.shape[0]
    half = count // 2
    single = lax.broadcasted_iota(jnp.int32, (half, data.shape[2]), 0) == 0
    for j in range(data.shape[1]):
        left = apply(fwd[...], data[:, j])
        right = other[j]
        real_a, imag_a = left[:half], left[half:]
        real_b, imag_b = right[:half], right[half:]
        real_p = real_a * real_b - jnp.where(single, 0.0, imag_a * imag_b)
        imag_p = jnp.where(single, imag_a * imag_b, real_a * imag_b + imag_a * real_b)
        out[:, j] = apply(inv[...], jnp.concatenate([real_p, imag_p], axis=0))


def convolve(forward, inverse, data, other):
    count, group, width = data.shape
    return pl.pallas_call(
        convolve_kernel,
        in_specs=[VMEM] * 4,
        out_specs=VMEM,
        out_shape=jax.ShapeDtypeStruct((count, group, width), F32),
        compiler_params=params(),
        cost_estimate=cost(4),
        name="convolve",
    )(forward, inverse, data, other)


def exchange(chunks):
    return lax.all_to_all(chunks, "energy", split_axis=0, concat_axis=0, tiled=True)


def body(inverses, coupling, source, screened, kept_rows, live_count):
    energies, slots, width = screened.shape
    parts = lax.axis_size("energy")
    spaces = lax.axis_size("space")
    place = lax.axis_index("space").astype(jnp.int32).reshape(1)
    group = slots // parts
    count = energies * parts
    forward, inverse = [stacked(m) for m in transforms(count)]
    chunks = screened.reshape(energies, parts, group, width).swapaxes(0, 1)

    given = [prepare(inverses, coupling, source, e) for e in range(energies)]
    outgoing = [given[e][2] for e in range(energies)]
    states = [[], []]
    for step in range(spaces - 1):
        for e in range(energies):
            state = lax.ppermute(outgoing[e], "space", [(step, step + 1)])
            states[e].append(state)
            if step + 2 < spaces:
                outgoing[e] = hop(step, place, state, given[e])
        if step == 0:
            chunks = lax.optimization_barrier((chunks, *outgoing))[0]
            other = spectrum(forward, exchange(chunks).reshape(count, group, width))

    rows = kept_rows.reshape(slots, 1)
    picked = None
    for e in range(energies):
        picked = pick(e, place, live_count, rows, states[e], given[e], picked)
    data = exchange(picked).reshape(count, group, width)
    sigma = convolve(forward, inverse, data, other)
    back = exchange(sigma.reshape(parts, energies, group, width))
    return back.swapaxes(0, 1).reshape(energies, slots, width)


def solution(mesh):
    return jax.shard_map(
        body,
        mesh=mesh,
        in_specs=(
            P("energy", "space", None, None),
            P("space", None, None),
            P("energy", "space", None, None),
            P("energy", "space", None),
            P("space"),
            P("space"),
        ),
        out_specs=P("energy", "space", None),
        check_vma=False,
    )
```

time: 176 us -> 177 us (level)
  the two profiles are of different devices: /device:TPU:448 before, /device:TPU:384 now
where the time goes in v2:
time: 177 us; the launch traced here: 176 us
  waiting for transfers between devices  58.7 us (33%)
  starting transfers between devices  34.7 us (20%)
  blocking collectives  34.2 us (19%)
  local copies, waits for them, and re-layouts  26.4 us (15%)
  Pallas kernels  21 us (12%)
    all_to_all x1, blocking collectives, exchange(): lax.all_to_all(chunks, 'energy', split_axis=0, concat_axis=0, tiled=True)  34.2 us
    ppermute x14, waiting for transfers between devices, body(): state = lax.ppermute(outgoing[e], 'space', [(step, step + 1)])  34.2 us
    all_to_all x2, waiting for transfers between devices, exchange(): lax.all_to_all(chunks, 'energy', split_axis=0, concat_axis=0, tiled=True)  24.4 us
    unnamed x88, local copies, waits for them, and re-layouts  24 us
    all_to_all x2, starting transfers between devices, exchange(): lax.all_to_all(chunks, 'energy', split_axis=0, concat_axis=0, tiled=True)  21.4 us
    ppermute x14, starting transfers between devices, body(): state = lax.ppermute(outgoing[e], 'space', [(step, step + 1)])  13.2 us
    pallas_call x2, Pallas kernels, pick(): pl.pallas_call(functools.partial(pick_kernel, energy, count), in_specs=sp...  6.32 us
    pallas_call x2, Pallas kernels, prepare(): pl.pallas_call(functools.partial(prepare_kernel, energy), in_specs=[HBM]...  4.58 us
  transfers between devices with their start and end apart: 16, of which 3 were waited for; matrix products, arithmetic and copies ran while one was open for 1% of the time, Pallas kernels for 8%

profile of v2, /device:TPU:384, one launch (start us, length us, event | category | flops | bytes accessed | tf_op | source)
XLA Modules:
  0.0 176.2 jit_solution(1869802515720106038)
XLA Ops:
  0.0 1.3 copy-done.40
  1.3 1.2 copy-done.41
  2.5 1.0 copy-done.42
  3.6 2.3 %prepare.3 = (bf16[256,256]{1,0:T(8,128)(2,1)S(1)}, bf16[256,256]{1,0:T(8,128)(2,1)S(1)}, f32[256,256]{1,0:T(8,128)S(1)}, bf16[256,256]{1,0:T(8,128)(2,1)S(1)}, ...) custom-call(f32[2,2,256,256]{3,2,1,0:T(8,128)S(1)} %copy-done.40, f32[2,256,256]{2,1,0:T(8,128)S(1)} %copy-done.42, ...), custom_call_target="tpu_custom_call" | custom-call | flops 905969664 | bytes 1048576 | tf_op jit(solution)/shard_map/prepare/pallas_call | solution.py:75
  8.5 2.3 %prepare.2 = (bf16[256,256]{1,0:T(8,128)(2,1)S(1)}, bf16[256,256]{1,0:T(8,128)(2,1)S(1)}, f32[256,256]{1,0:T(8,128)S(1)}, bf16[256,256]{1,0:T(8,128)(2,1)S(1)}, ...) custom-call(f32[2,2,256,256]{3,2,1,0:T(8,128)S(1)} %copy-done.40, f32[2,256,256]{2,1,0:T(8,128)S(1)} %copy-done.42, ...), custom_call_target="tpu_custom_call" | custom-call | flops 905969664 | bytes 1048576 | tf_op jit(solution)/shard_map/prepare/pallas_call | solution.py:75
  12.3 1.2 copy_bitcast_fusion.1
  15.0 10.6 %all-to-all-start.1 = ((f32[64,2,8,256]{3,2,1,0:T(8,128)}), f32[64,2,8,256]{3,2,1,0:T(8,128)S(1)}, u32[]{:S(2)}, u32[]{:S(2)}) async-start(f32[64,2,8,256]{3,2,1,0:T(8,128)} %copy_bitcast_fusion.1), calls=%async_computation.1 | async-start | bytes 2097152 | tf_op jit(solution)/shard_map/all_to_all | solution.py:235
  36.0 1.3 collective-permute-start.12
  38.0 1.3 collective-permute-start.5
  39.3 30.8 %collective-permute-done.12.state.refs_5_ = f32[256,256]{1,0:T(8,128)S(1)} collective-permute-done((f32[256,256]{1,0:T(8,128)S(1)}, f32[256,256]{1,0:T(8,128)S(1)}, u32[]{:S(2)}, u32[]{:S(2)}) %collective-permute-start.12) | collective-permute-done | bytes 262176 | tf_op jit(solution)/shard_map/ppermute | solution.py:253
  70.2 1.3 hop.23
  71.5 2.0 %collective-permute-start.13 = (f32[256,256]{1,0:T(8,128)}, f32[256,256]{1,0:T(8,128)}, u32[]{:S(2)}, u32[]{:S(2)}) collective-permute-start(f32[256,256]{1,0:T(8,128)} %hop.23), channel_id=1, source_target_pairs={{6,7},{14,15},{22,23},{30,31},{38,39},{46,47},{54,55},{62,63},{70,... | collective-permute-start | bytes 786440 | tf_op jit(solution)/shard_map/ppermute | solution.py:253
  73.5 3.3 %collective-permute-done.5.state.refs_5_ = f32[256,256]{1,0:T(8,128)S(1)} collective-permute-done((f32[256,256]{1,0:T(8,128)S(1)}, f32[256,256]{1,0:T(8,128)S(1)}, u32[]{:S(2)}, u32[]{:S(2)}) %collective-permute-start.5) | collective-permute-done | bytes 262176 | tf_op jit(solution)/shard_map/ppermute | solution.py:253
  76.8 1.3 hop.17
  78.1 2.0 %collective-permute-start.6 = (f32[256,256]{1,0:T(8,128)}, f32[256,256]{1,0:T(8,128)}, u32[]{:S(2)}, u32[]{:S(2)}) collective-permute-start(f32[256,256]{1,0:T(8,128)} %hop.17), channel_id=1, source_target_pairs={{6,7},{14,15},{22,23},{30,31},{38,39},{46,47},{54,55},{62,63},{70,... | collective-permute-start | bytes 786440 | tf_op jit(solution)/shard_map/ppermute | solution.py:253
  89.5 3.1 %pick.2.refs_13_ = f32[64,2,8,256]{3,2,1,0:T(8,128)} custom-call(s32[1]{0:T(128)} %bitcast.place, s32[1]{0:T(128)S(6)} %copy.19.live, s32[512,1]{1,0:T(8,128)S(1)} %copy.13.rows, f32[256,256]{1,0:T(8,128)S(1)} %copy-done.6, f32[256,256]{1,0:T(8,128)S(1)} %copy-done.10, f32[256,256]{1,0:T(8,128)S(1)} %copy-done.14, f32[256,256]{1,0:T(8,128)S(1)} %copy-done.18, ...), custom_call_target="tpu_custom_call" | custom-call | flops 805306368 | bytes 1048576 | tf_op jit(solution)/shard_map/pick/pallas_call | solution.py:148
  92.7 3.2 %pick.3 = f32[64,2,8,256]{3,2,1,0:T(8,128)} custom-call(s32[1]{0:T(128)} %bitcast.place, s32[1]{0:T(128)S(6)} %copy.19.live, s32[512,1]{1,0:T(8,128)S(1)} %copy.13.rows, f32[256,256]{1,0:T(8,128)S(1)} %copy-done.4, f32[256,256]{1,0:T(8,128)S(1)} %copy-done.8, f32[256,256]{1,0:T(8,128)S(1)} %copy-done.12, ...), custom_call_target="tpu_custom_call", output_to_operand_aliasing={{}: (16, {})} | custom-call | flops 805306368 | bytes 1048576 | tf_op jit(solution)/shard_map/pick/pallas_call | solution.py:148
  95.9 10.9 %all-to-all-start = ((f32[64,2,8,256]{3,2,1,0:T(8,128)}), f32[64,2,8,256]{3,2,1,0:T(8,128)S(1)}, u32[]{:S(2)}, u32[]{:S(2)}) async-start(f32[64,2,8,256]{3,2,1,0:T(8,128)} %pick.3), calls=%async_computation | async-start | bytes 2097152 | tf_op jit(solution)/shard_map/all_to_all | solution.py:235
  106.8 3.4 %spectrum.1.other = f32[8,128,256]{2,1,0:T(8,128)S(1)} custom-call(bf16[256,256]{1,0:T(8,128)(2,1)S(1)} %copy-done.27, f32[128,8,256]{2,1,0:T(8,128)S(1)} %bitcast.15), custom_call_target="tpu_custom_call" | custom-call | flops 201326592 | bytes 1048576 | tf_op jit(solution)/shard_map/spectrum/pallas_call | solution.py:196
  111.3 24.4 %all-to-all-done = f32[64,2,8,256]{3,2,1,0:T(8,128)S(1)} async-done(((f32[64,2,8,256]{3,2,1,0:T(8,128)}), f32[64,2,8,256]{3,2,1,0:T(8,128)S(1)}, u32[]{:S(2)}, u32[]{:S(2)}) %all-to-all-start) | async-done | bytes 1048608 | tf_op jit(solution)/shard_map/all_to_all | solution.py:235
  135.7 1.2 copy-done.2
  136.9 4.0 %convolve.1 = f32[128,8,256]{2,1,0:T(8,128)S(1)} custom-call(bf16[256,256]{1,0:T(8,128)(2,1)S(1)} %copy-done.27, bf16[256,256]{1,0:T(8,128)(2,1)S(1)} %copy-done.39, f32[128,8,256]{2,1,0:T(8,128)S(1)} %bitcast.16, f32[8,128,256]{2,1,0:T(8,128)S(1)} %copy-done.2), custom_call_target="tpu_custom_call" | custom-call | flops 402653184 | bytes 1048576 | tf_op jit(solution)/shard_map/convolve/pallas_call | solution.py:223
  140.9 34.2 %all_to_all.15 = f32[64,2,8,256]{3,2,1,0:T(8,128)S(1)} all-to-all(f32[64,2,8,256]{3,2,1,0:T(8,128)S(1)} %bitcast.17), channel_id=1, replica_groups=mesh['energy'=64,'space'=8] {'energy'}, dimensions={0} | all-to-all | bytes 2097152 | tf_op jit(solution)/shard_map/all_to_all | solution.py:235
  175.2 1.1 copy_bitcast_fusion
  (118 shorter events, 26.2 us)
Async XLA Ops:
  0.0 12.3 %copy-start = (f32[2,512,256]{2,1,0:T(8,128)S(1)}, f32[2,512,256]{2,1,0:T(8,128)}, u32[]{:S(2)}) copy-start(f32[2,512,256]{2,1,0:T(8,128)} %param.11) | copy-start | bytes 3145732
  7.9 5.6 %collective-permute-start.7 = (f32[256,256]{1,0:T(8,128)S(1)}, f32[256,256]{1,0:T(8,128)S(1)}, u32[]{:S(2)}, u32[]{:S(2)}) collective-permute-start(f32[256,256]{1,0:T(8,128)S(1)} %get-tuple-element.24.add.refs_9_), channel_id=1, source_target_pairs={{0,1},{8,9},{16,17},{24,25},{32,33},{40,41},{48,49},{56,57},{64,65... | collective-permute-start | bytes 786440 | tf_op jit(solution)/shard_map/ppermute | solution.py:253
  11.6 2.6 %collective-permute-start = (f32[256,256]{1,0:T(8,128)S(1)}, f32[256,256]{1,0:T(8,128)S(1)}, u32[]{:S(2)}, u32[]{:S(2)}) collective-permute-start(f32[256,256]{1,0:T(8,128)S(1)} %get-tuple-element.18.add.refs_9_), channel_id=1, source_target_pairs={{0,1},{8,9},{16,17},{24,25},{32,33},{40,41},{48,49},{56,57},{64,65... | collective-permute-start | bytes 786440 | tf_op jit(solution)/shard_map/ppermute | solution.py:253
  15.0 81.0 %all-to-all-start.1 = ((f32[64,2,8,256]{3,2,1,0:T(8,128)}), f32[64,2,8,256]{3,2,1,0:T(8,128)S(1)}, u32[]{:S(2)}, u32[]{:S(2)}) async-start(f32[64,2,8,256]{3,2,1,0:T(8,128)} %copy_bitcast_fusion.1), calls=%async_computation.1 | async-start | bytes 2097152 | tf_op jit(solution)/shard_map/all_to_all | solution.py:235
  25.6 1.4 collective-permute-start.8
  26.2 2.1 %collective-permute-start.1 = (f32[256,256]{1,0:T(8,128)S(1)}, f32[256,256]{1,0:T(8,128)S(1)}, u32[]{:S(2)}, u32[]{:S(2)}) collective-permute-start(f32[256,256]{1,0:T(8,128)S(1)} %hop.12), channel_id=1, source_target_pairs={{1,2},{9,10},{17,18},{25,26},{33,34},{41,42},{49,50},{57,58},{65,6... | collective-permute-start | bytes 786440 | tf_op jit(solution)/shard_map/ppermute | solution.py:253
  27.6 2.1 %collective-permute-start.9 = (f32[256,256]{1,0:T(8,128)S(1)}, f32[256,256]{1,0:T(8,128)S(1)}, u32[]{:S(2)}, u32[]{:S(2)}) collective-permute-start(f32[256,256]{1,0:T(8,128)S(1)} %hop.19), channel_id=1, source_target_pairs={{2,3},{10,11},{18,19},{26,27},{34,35},{42,43},{50,51},{58,59},{66,... | collective-permute-start | bytes 786440 | tf_op jit(solution)/shard_map/ppermute | solution.py:253
  29.0 2.1 %collective-permute-start.2 = (f32[256,256]{1,0:T(8,128)S(1)}, f32[256,256]{1,0:T(8,128)S(1)}, u32[]{:S(2)}, u32[]{:S(2)}) collective-permute-start(f32[256,256]{1,0:T(8,128)S(1)} %hop.13), channel_id=1, source_target_pairs={{2,3},{10,11},{18,19},{26,27},{34,35},{42,43},{50,51},{58,59},{66,... | collective-permute-start | bytes 786440 | tf_op jit(solution)/shard_map/ppermute | solution.py:253
  30.4 2.1 %collective-permute-start.10 = (f32[256,256]{1,0:T(8,128)S(1)}, f32[256,256]{1,0:T(8,128)S(1)}, u32[]{:S(2)}, u32[]{:S(2)}) collective-permute-start(f32[256,256]{1,0:T(8,128)S(1)} %hop.20), channel_id=1, source_target_pairs={{3,4},{11,12},{19,20},{27,28},{35,36},{43,44},{51,52},{59,60},{67,... | collective-permute-start | bytes 786440 | tf_op jit(solution)/shard_map/ppermute | solution.py:253
  31.8 2.1 %collective-permute-start.3 = (f32[256,256]{1,0:T(8,128)S(1)}, f32[256,256]{1,0:T(8,128)S(1)}, u32[]{:S(2)}, u32[]{:S(2)}) collective-permute-start(f32[256,256]{1,0:T(8,128)S(1)} %hop.14), channel_id=1, source_target_pairs={{3,4},{11,12},{19,20},{27,28},{35,36},{43,44},{51,52},{59,60},{67,... | collective-permute-start | bytes 786440 | tf_op jit(solution)/shard_map/ppermute | solution.py:253
  33.2 2.1 %collective-permute-start.11 = (f32[256,256]{1,0:T(8,128)S(1)}, f32[256,256]{1,0:T(8,128)S(1)}, u32[]{:S(2)}, u32[]{:S(2)}) collective-permute-start(f32[256,256]{1,0:T(8,128)S(1)} %hop.21), channel_id=1, source_target_pairs={{4,5},{12,13},{20,21},{28,29},{36,37},{44,45},{52,53},{60,61},{68,... | collective-permute-start | bytes 786440 | tf_op jit(solution)/shard_map/ppermute | solution.py:253
  34.6 2.7 %collective-permute-start.4 = (f32[256,256]{1,0:T(8,128)S(1)}, f32[256,256]{1,0:T(8,128)S(1)}, u32[]{:S(2)}, u32[]{:S(2)}) collective-permute-start(f32[256,256]{1,0:T(8,128)S(1)} %hop.15), channel_id=1, source_target_pairs={{4,5},{12,13},{20,21},{28,29},{36,37},{44,45},{52,53},{60,61},{68,... | collective-permute-start | bytes 786440 | tf_op jit(solution)/shard_map/ppermute | solution.py:253
  36.0 34.1 %collective-permute-start.12 = (f32[256,256]{1,0:T(8,128)S(1)}, f32[256,256]{1,0:T(8,128)S(1)}, u32[]{:S(2)}, u32[]{:S(2)}) collective-permute-start(f32[256,256]{1,0:T(8,128)S(1)} %hop.22), channel_id=1, source_target_pairs={{5,6},{13,14},{21,22},{29,30},{37,38},{45,46},{53,54},{61,62},{69,... | collective-permute-start | bytes 786440 | tf_op jit(solution)/shard_map/ppermute | solution.py:253
  38.0 38.8 %collective-permute-start.5 = (f32[256,256]{1,0:T(8,128)S(1)}, f32[256,256]{1,0:T(8,128)S(1)}, u32[]{:S(2)}, u32[]{:S(2)}) collective-permute-start(f32[256,256]{1,0:T(8,128)S(1)} %hop.16), channel_id=1, source_target_pairs={{5,6},{13,14},{21,22},{29,30},{37,38},{45,46},{53,54},{61,62},{69,... | collective-permute-start | bytes 786440 | tf_op jit(solution)/shard_map/ppermute | solution.py:253
  71.5 9.5 %collective-permute-start.13 = (f32[256,256]{1,0:T(8,128)}, f32[256,256]{1,0:T(8,128)}, u32[]{:S(2)}, u32[]{:S(2)}) collective-permute-start(f32[256,256]{1,0:T(8,128)} %hop.23), channel_id=1, source_target_pairs={{6,7},{14,15},{22,23},{30,31},{38,39},{46,47},{54,55},{62,63},{70,... | collective-permute-start | bytes 786440 | tf_op jit(solution)/shard_map/ppermute | solution.py:253
  76.8 3.3 %copy-start.43 = (s32[512]{0:T(512)S(1)}, s32[512]{0:T(512)}, u32[]{:S(2)}) copy-start(s32[512]{0:T(512)} %param.12) | copy-start | bytes 6148
  78.1 14.5 %collective-permute-start.6 = (f32[256,256]{1,0:T(8,128)}, f32[256,256]{1,0:T(8,128)}, u32[]{:S(2)}, u32[]{:S(2)}) collective-permute-start(f32[256,256]{1,0:T(8,128)} %hop.17), channel_id=1, source_target_pairs={{6,7},{14,15},{22,23},{30,31},{38,39},{46,47},{54,55},{62,63},{70,... | collective-permute-start | bytes 786440 | tf_op jit(solution)/shard_map/ppermute | solution.py:253
  89.4 3.2 %copy-start.20 = (f32[256,256]{1,0:T(8,128)S(1)}, f32[256,256]{1,0:T(8,128)}, u32[]{:S(2)}) copy-start(f32[256,256]{1,0:T(8,128)} %copy-done.19) | copy-start | bytes 786436
  89.5 3.2 %copy-start.24 = (f32[256,256]{1,0:T(8,128)S(1)}, f32[256,256]{1,0:T(8,128)}, u32[]{:S(2)}) copy-start(f32[256,256]{1,0:T(8,128)} %copy-done.23) | copy-start | bytes 786436
  89.5 3.2 %copy-start.29 = (f32[256,256]{1,0:T(8,128)S(1)}, f32[256,256]{1,0:T(8,128)}, u32[]{:S(2)}) copy-start(f32[256,256]{1,0:T(8,128)} %copy-done.28) | copy-start | bytes 786436
  89.5 3.2 %copy-start.34 = (bf16[256,256]{1,0:T(8,128)(2,1)S(1)}, bf16[256,256]{1,0:T(8,128)(2,1)}, u32[]{:S(2)}) copy-start(bf16[256,256]{1,0:T(8,128)(2,1)} %copy-done.33) | copy-start | bytes 393220
  95.9 10.9 %copy-start.27 = (bf16[256,256]{1,0:T(8,128)(2,1)S(1)}, bf16[256,256]{1,0:T(8,128)(2,1)}, u32[]{:S(2)}) copy-start(bf16[256,256]{1,0:T(8,128)(2,1)} %constant.27.fwd) | copy-start | bytes 393220
  95.9 39.8 %all-to-all-start = ((f32[64,2,8,256]{3,2,1,0:T(8,128)}), f32[64,2,8,256]{3,2,1,0:T(8,128)S(1)}, u32[]{:S(2)}, u32[]{:S(2)}) async-start(f32[64,2,8,256]{3,2,1,0:T(8,128)} %pick.3), calls=%async_computation | async-start | bytes 2097152 | tf_op jit(solution)/shard_map/all_to_all | solution.py:235
  106.8 28.9 %copy-start.39 = (bf16[256,256]{1,0:T(8,128)(2,1)S(1)}, bf16[256,256]{1,0:T(8,128)(2,1)}, u32[]{:S(2)}) copy-start(bf16[256,256]{1,0:T(8,128)(2,1)} %constant.34.inv) | copy-start | bytes 393220
  (36 other events, 42.3 us)

commit v3 on v2

v3 whole, which is shorter than its diff:
```python
import functools
import math

import jax
import jax.numpy as jnp
import numpy as np
from jax import lax
from jax.experimental import pallas as pl
from jax.experimental.pallas import tpu as pltpu
from jax.sharding import PartitionSpec as P

BF = jnp.bfloat16
F32 = jnp.float32
VMEM = pl.BlockSpec(memory_space=pltpu.VMEM)
SMEM = pl.BlockSpec(memory_space=pltpu.SMEM)
HBM = pl.BlockSpec(memory_space=pltpu.HBM)


def far(array):
    return pltpu.with_memory_space_constraint(array, pltpu.HBM)


def near(array):
    return pltpu.with_memory_space_constraint(array, pltpu.VMEM)


def params(mebibytes=8):
    return pltpu.CompilerParams(vmem_limit_bytes=mebibytes * 1024 * 1024)


def cost(products, size=256):
    return pl.CostEstimate(flops=int(products * 3 * 2 * size**3), bytes_accessed=1 << 20, transcendentals=0)


def split(value):
    high = value.astype(BF)
    return high, (value - high.astype(F32)).astype(BF)


def product(left, right, right_dim=0):
    dims = (((1,), (right_dim,)), ((), ()))

    def one(a, b):
        return lax.dot_general(a, b, dims, preferred_element_type=F32)

    return one(left[0], right[0]) + (one(left[0], right[1]) + one(left[1], right[0]))


def sandwich(outer, inner):
    return product(split(product(outer, inner)), outer, 1)


def prepare_kernel(inv_all, coup_all, src_all, *refs):
    energies = inv_all.shape[0]
    outs = [refs[5 * e : 5 * e + 5] for e in range(energies)]
    inv, coup, src, kept, sem, out_sem = refs[5 * energies :]
    copies = {}

    def fetch(name, source, target):
        copies[name] = pltpu.make_async_copy(source, target, sem.at[len(copies)])
        copies[name].start()

    for e in range(energies):
        for b in range(2):
            if e == 0:
                fetch(("coup", b), coup_all.at[b], coup.at[b])
            fetch(("inv", e, b), inv_all.at[e, b], inv.at[e, b])
            fetch(("src", e, b), src_all.at[e, b], src.at[e, b])

    def ready(ref, *name):
        if name in copies:
            copies.pop(name).wait()
        return split(ref[name[1:]])

    stores = []
    for e in range(energies):
        map_h, map_l, add, first, pair = outs[e]
        step, inj = [], []
        for b in range(2):
            left = ready(inv, "inv", e, b)
            moved = product(left, ready(coup, "coup", b))
            step.append(split(moved))
            inj.append(sandwich(left, ready(src, "src", e, b)))
            if b == 0:
                kept[e, 0, 0] = moved
                kept[e, 0, 1] = inj[0]
                stores.append(pltpu.make_async_copy(kept.at[e, 0], first, out_sem.at[e, 0]))
                stores[-1].start()
        added = sandwich(step[1], split(inj[0])) + inj[1]
        mapped = product(step[1], step[0])
        add[...] = added
        map_h[...], map_l[...] = split(mapped)
        kept[e, 1, 0] = mapped
        kept[e, 1, 1] = added
        stores.append(pltpu.make_async_copy(kept.at[e, 1], pair, out_sem.at[e, 1]))
        stores[-1].start()
    for store in stores:
        store.wait()


def prepare(inverses, coupling, source):
    energies, _, width, _ = inverses.shape
    square = (width, width)
    outs = [pltpu.VMEM(square, BF)] * 2 + [pltpu.VMEM(square, F32)] + [pltpu.HBM((2, *square), F32)] * 2
    results = pl.pallas_call(
        prepare_kernel,
        in_specs=[HBM] * 3,
        out_specs=([VMEM] * 3 + [HBM] * 2) * energies,
        out_shape=outs * energies,
        scratch_shapes=[
            pltpu.VMEM(inverses.shape, F32),
            pltpu.VMEM(coupling.shape, F32),
            pltpu.VMEM(source.shape, F32),
            pltpu.VMEM((energies, 2, 2, *square), F32),
            pltpu.SemaphoreType.DMA((2 + 4 * energies,)),
            pltpu.SemaphoreType.DMA((energies, 2)),
        ],
        compiler_params=params(16),
        cost_estimate=cost(18),
        name="prepare",
    )(*[far(a) for a in (inverses, coupling, source)])
    return [results[5 * e : 5 * e + 5] for e in range(energies)]


def through(pair, state):
    return sandwich(split(pair[0]), split(state)) + pair[1]


def hop_kernel(target, skips, place, entry, before, state, map_h, map_l, add, *refs):
    out, entry_out = refs[-2:]
    active = place[0] == target

    @pl.when(active)
    def _():
        begin = through(refs[0], state[...]) if skips else state[...]
        entry_out[...] = begin
        out[...] = sandwich((map_h[...], map_l[...]), split(begin)) + add[...]

    @pl.when(jnp.logical_not(active))
    def _():
        entry_out[...] = entry[...]
        out[...] = before[...]


def hop(target, place, entry, before, state, given, pair=None, weight=2):
    operands = [place, entry, before, state, *given[:3]]
    if pair is not None:
        operands.append(pair)
    return pl.pallas_call(
        functools.partial(hop_kernel, target, pair is not None),
        in_specs=[SMEM] + [VMEM] * (len(operands) - 1),
        out_specs=[VMEM] * 2,
        out_shape=[pltpu.VMEM(state.shape, F32)] * 2,
        compiler_params=params(),
        cost_estimate=cost(weight),
        name="hop",
    )(*operands)


def pick_kernel(energy, end, late, place, live, rows, entry, state, side, map_h, map_l, add, pair, first, *refs):
    out, begin, block, picked, sem = refs[-5:]
    here = place[0]
    sideways = functools.reduce(jnp.logical_or, [here == z for z in late])
    fetch = pltpu.make_async_copy(first, block, sem.at[0])
    fetch.start()

    @pl.when(here == end)
    def _():
        begin[...] = through(pair, state[...])

    @pl.when(sideways)
    def _():
        begin[...] = side[...]

    @pl.when(jnp.logical_not(jnp.logical_or(here == end, sideways)))
    def _():
        begin[...] = entry[...]

    width = entry.shape[1]
    slots = rows.shape[0]
    column = lax.broadcasted_iota(jnp.int32, (slots, 2 * width), 1)
    slot = lax.broadcasted_iota(jnp.int32, (slots, 2 * width), 0)
    chosen = jnp.where((column == rows[...]) & (slot < live[0]), 1.0, 0.0).astype(BF)
    start = split(begin[...])
    last = sandwich((map_h[...], map_l[...]), start) + add[...]
    fetch.wait()
    high, low = split(jnp.concatenate([through(block, begin[...]), last], axis=0))
    dot = lambda a, b: jnp.dot(a, b, preferred_element_type=F32)
    picked[...] = (dot(chosen, high) + dot(chosen, low)).reshape(picked.shape)
    store = pltpu.make_async_copy(picked, out.at[:, energy], sem.at[1])
    store.start()
    store.wait()


def pick(energy, end, late, place, live, rows, entry, state, side, pair, given, before=None):
    width = entry.shape[1]
    slots = rows.shape[0]
    operands = [place, live, rows, *[near(a) for a in (entry, state, side, *given[:3])], pair, far(given[3])]
    specs = [SMEM, SMEM] + [VMEM] * (len(operands) - 3) + [HBM]
    aliases = {}
    if before is not None:
        aliases = {len(operands): 0}
        operands.append(before)
        specs.append(HBM)
    return pl.pallas_call(
        functools.partial(pick_kernel, energy, end, late),
        in_specs=specs,
        out_specs=HBM,
        out_shape=pltpu.HBM((slots // 8, 2, 8, width), F32),
        scratch_shapes=[
            pltpu.VMEM((width, width), F32),
            pltpu.VMEM((2, width, width), F32),
            pltpu.VMEM((slots // 8, 8, width), F32),
            pltpu.SemaphoreType.DMA((2,)),
        ],
        input_output_aliases=aliases,
        compiler_params=params(12),
        cost_estimate=cost(8),
        name="pick",
    )(*operands)


def transforms(count):
    half = count // 2
    points = np.arange(count)
    waves = np.arange(half)
    angle = 2.0 * math.pi * ((waves[:, None] * points[None, :]) % count) / count
    forward = np.concatenate([np.cos(angle), -np.sin(angle)], axis=0)
    forward[half] = np.where(points % 2 == 0, 1.0, -1.0)
    weight = np.full(count, 2.0 / count)
    weight[[0, half]] = 1.0 / count
    return forward.astype(np.float32), (forward.T * weight[None, :]).astype(np.float32)


def spectrum_kernel(fwd_h, fwd_l, data, out):
    for j in range(data.shape[1]):
        out[j] = product((fwd_h[...], fwd_l[...]), split(data[:, j]))


def spectrum(forward, data):
    count, group, width = data.shape
    return pl.pallas_call(
        spectrum_kernel,
        in_specs=[VMEM] * 3,
        out_specs=VMEM,
        out_shape=pltpu.VMEM((group, count, width), F32),
        compiler_params=params(),
        cost_estimate=cost(2),
        name="spectrum",
    )(*forward, far(data))


def convolve_kernel(fwd_h, fwd_l, inv_h, inv_l, data, other, out):
    count = data.shape[0]
    half = count // 2
    single = lax.broadcasted_iota(jnp.int32, (half, data.shape[2]), 0) == 0
    for j in range(data.shape[1]):
        left = product((fwd_h[...], fwd_l[...]), split(data[:, j]))
        right = other[j]
        real_a, imag_a = left[:half], left[half:]
        real_b, imag_b = right[:half], right[half:]
        real_p = real_a * real_b - jnp.where(single, 0.0, imag_a * imag_b)
        imag_p = jnp.where(single, imag_a * imag_b, real_a * imag_b + imag_a * real_b)
        out[:, j] = product((inv_h[...], inv_l[...]), split(jnp.concatenate([real_p, imag_p], axis=0)))


def convolve(forward, inverse, data, other):
    count, group, width = data.shape
    return pl.pallas_call(
        convolve_kernel,
        in_specs=[VMEM] * 6,
        out_specs=VMEM,
        out_shape=jax.ShapeDtypeStruct((count, group, width), F32),
        compiler_params=params(),
        cost_estimate=cost(4),
        name="convolve",
    )(*forward, *inverse, data, near(other))


def arrange_kernel(data, after, out, sem):
    del after
    copies = [pltpu.make_async_copy(data.at[e], out.at[:, e], sem.at[e]) for e in range(data.shape[0])]
    for copy in copies:
        copy.start()
    for copy in copies:
        copy.wait()


def arrange(data, after):
    energies, parts = data.shape[:2]
    return pl.pallas_call(
        arrange_kernel,
        in_specs=[VMEM, VMEM],
        out_specs=HBM,
        out_shape=pltpu.HBM((parts, energies, *data.shape[2:]), F32),
        scratch_shapes=[pltpu.SemaphoreType.DMA((energies,))],
        compiler_params=params(),
        cost_estimate=cost(0.1),
        name="arrange",
    )(data, after)


def exchange(chunks):
    return lax.all_to_all(chunks, "energy", split_axis=0, concat_axis=0, tiled=True)


def body(inverses, coupling, source, screened, kept_rows, live_count):
    energies, slots, width = screened.shape
    parts = lax.axis_size("energy")
    spaces = lax.axis_size("space")
    place = lax.axis_index("space").astype(jnp.int32).reshape(1)
    group = slots // parts
    count = energies * parts
    forward, inverse = [split(jnp.asarray(m)) for m in transforms(count)]

    middle = spaces // 2
    direct = list(range(middle))
    odd = list(range(middle + 1, spaces, 2))
    path = direct + odd
    given = prepare(inverses, coupling, source)
    pairs = [lax.ppermute(given[e][4], "space", [(z - 1, z) for z in odd]) for e in range(energies)]
    outgoing = [given[e][2] for e in range(energies)]
    entry = [jnp.zeros((width, width), F32)] * energies
    state = [None] * energies
    for step, (here, target) in enumerate(zip(path[:-1], path[1:])):
        for e in range(energies):
            state[e] = lax.ppermute(outgoing[e], "space", [(here, target)])
            if target != path[-1]:
                pair = pairs[e] if target in odd else None
                weight = 60 if step == 1 else 2
                outgoing[e], entry[e] = hop(target, place, entry[e], outgoing[e], state[e], given[e], pair, weight)
        if step == 0:
            chunks = arrange(screened.reshape(energies, parts, group, width), outgoing[-1])
    late = [z - 1 for z in odd]
    other = spectrum(forward, exchange(chunks).reshape(count, group, width))
    side = [lax.ppermute(outgoing[e], "space", [(path[path.index(z) - 1], z - 1) for z in odd]) for e in range(energies)]

    rows = kept_rows.reshape(slots, 1)
    other, state[0] = lax.optimization_barrier((other, state[0]))
    picked = None
    for e in range(energies):
        picked = pick(
            e, path[-1], late, place, live_count, rows, entry[e], state[e], side[e], pairs[e], given[e], picked
        )
    data = exchange(picked).reshape(count, group, width)
    sigma = convolve(forward, inverse, data, other)
    back = exchange(sigma.reshape(parts, energies, group, width))
    return back.swapaxes(0, 1).reshape(energies, slots, width)


def solution(mesh):
    return jax.shard_map(
        body,
        mesh=mesh,
        in_specs=(
            P("energy", "space", None, None),
            P("space", None, None),
            P("energy", "space", None, None),
            P("energy", "space", None),
            P("space"),
            P("space"),
        ),
        out_specs=P("energy", "space", None),
        check_vma=False,
    )
```

time: 177 us -> 157 us (0.89)
  the two profiles are of different devices: /device:TPU:384 before, /device:TPU:192 now
where the time goes in v3:
time: 157 us; the launch traced here: 156 us
  blocking collectives  73.3 us (47%)
  starting transfers between devices  29.7 us (19%)
  Pallas kernels  25.9 us (16%)
  waiting for transfers between devices  24.9 us (16%)
    all_to_all x2, blocking collectives, exchange(): lax.all_to_all(chunks, 'energy', split_axis=0, concat_axis=0, tiled=True)  73.3 us
    ppermute x10, waiting for transfers between devices, body(): state[e] = lax.ppermute(outgoing[e], 'space', [(here, target)])  24.9 us
    all_to_all x1, starting transfers between devices, exchange(): lax.all_to_all(chunks, 'energy', split_axis=0, concat_axis=0, tiled=True)  11 us
    ppermute x10, starting transfers between devices, body(): state[e] = lax.ppermute(outgoing[e], 'space', [(here, target)])  10.4 us
    ppermute x2, starting transfers between devices, body(): lax.ppermute(outgoing[e], 'space', [(path[path.index(z) - 1], z - 1) for...  6.94 us
    pallas_call x2, Pallas kernels, pick(): pl.pallas_call(functools.partial(pick_kernel, energy, end, late), in_spec...  6.76 us
    pallas_call x1, Pallas kernels, prepare(): pl.pallas_call(prepare_kernel, in_specs=[HBM] * 3, out_specs=([VMEM] * 3...  6.36 us
    pallas_call x1, Pallas kernels, spectrum(): pl.pallas_call(spectrum_kernel, in_specs=[VMEM] * 3, out_specs=VMEM, out_...  4.7 us
  transfers between devices with their start and end apart: 15, of which 3 were waited for; matrix products, arithmetic and copies ran while one was open for 0% of the time, Pallas kernels for 8%

profile of v3, /device:TPU:192, one launch (start us, length us, event | category | flops | bytes accessed | tf_op | source)
XLA Modules:
  0.0 156.4 jit_solution(11050058363577271816)
XLA Ops:
  0.0 6.4 %prepare.1 = (bf16[256,256]{1,0:T(8,128)(2,1)S(1)}, bf16[256,256]{1,0:T(8,128)(2,1)S(1)}, f32[256,256]{1,0:T(8,128)S(1)}, f32[2,256,256]{2,1,0:T(8,128)}, f32[2,...) custom-call(f32[2,2,256,256]{3,2,1,0:T(8,128)} %inv_all.1, ...), custom_call_target="tpu_custom_call" | custom-call | flops 1811939328 | bytes 1048576 | tf_op jit(solution)/shard_map/prepare/pallas_call | solution.py:105
  7.8 0.8 collective-permute-start.8
  9.0 1.0 arrange.1
  10.0 11.0 %all-to-all-start = ((f32[64,2,8,256]{3,2,1,0:T(8,128)}), f32[64,2,8,256]{3,2,1,0:T(8,128)}, u32[]{:S(2)}, u32[]{:S(2)}) async-start(f32[64,2,8,256]{3,2,1,0:T(8,128)} %arrange.1), calls=%async_computation | async-start | bytes 2097152 | tf_op jit(solution)/shard_map/all_to_all | solution.py:304
  22.5 1.3 collective-permute-start.9
  23.8 1.4 collective-permute-start.2
  26.0 6.6 %collective-permute-done.9.state = f32[256,256]{1,0:T(8,128)S(1)} collective-permute-done((f32[256,256]{1,0:T(8,128)S(1)}, f32[256,256]{1,0:T(8,128)S(1)}, u32[]{:S(2)}, u32[]{:S(2)}) %collective-permute-start.9) | collective-permute-done | bytes 262176 | tf_op jit(solution)/shard_map/ppermute | solution.py:327
  33.2 1.3 collective-permute-start.10
  34.5 15.7 %collective-permute-done.2.state = f32[256,256]{1,0:T(8,128)S(1)} collective-permute-done((f32[256,256]{1,0:T(8,128)S(1)}, f32[256,256]{1,0:T(8,128)S(1)}, u32[]{:S(2)}, u32[]{:S(2)}) %collective-permute-start.2) | collective-permute-done | bytes 262176 | tf_op jit(solution)/shard_map/ppermute | solution.py:327
  50.8 1.3 collective-permute-start.3
  52.2 0.8 hop.15
  52.9 1.4 collective-permute-start.12
  54.3 2.0 %collective-permute-start.13 = (f32[256,256]{1,0:T(8,128)}, f32[256,256]{1,0:T(8,128)}, u32[]{:S(2)}, u32[]{:S(2)}) collective-permute-start(f32[256,256]{1,0:T(8,128)} %get-tuple-element.57), channel_id=1, source_target_pairs={{3,4},{5,6},{11,12},{13,14},{19,20},{21,22},{27,28},{29,30},{35,36... | collective-permute-start | bytes 786440 | tf_op jit(solution)/shard_map/ppermute | solution.py:336
  56.3 2.6 %collective-permute-done.3.state = f32[256,256]{1,0:T(8,128)S(1)} collective-permute-done((f32[256,256]{1,0:T(8,128)S(1)}, f32[256,256]{1,0:T(8,128)S(1)}, u32[]{:S(2)}, u32[]{:S(2)}) %collective-permute-start.3) | collective-permute-done | bytes 262176 | tf_op jit(solution)/shard_map/ppermute | solution.py:327
  58.9 0.7 hop.11
  59.7 0.8 collective-permute-start.5
  60.5 4.9 %collective-permute-start.6 = (f32[256,256]{1,0:T(8,128)}, f32[256,256]{1,0:T(8,128)S(1)}, u32[]{:S(2)}, u32[]{:S(2)}) collective-permute-start(f32[256,256]{1,0:T(8,128)} %get-tuple-element.44), channel_id=1, source_target_pairs={{3,4},{5,6},{11,12},{13,14},{19,20},{21,22},{27,28},{29,30},{35,36... | collective-permute-start | bytes 786440 | tf_op jit(solution)/shard_map/ppermute | solution.py:336
  66.3 4.7 %spectrum.1.other = f32[8,128,256]{2,1,0:T(8,128)S(1)} custom-call(bf16[128,128]{1,0:T(8,128)(2,1)S(1)} %copy-done.1, bf16[128,128]{1,0:T(8,128)(2,1)S(1)} %copy-done.2, f32[128,8,256]{2,1,0:T(8,128)} %bitcast.3.data), custom_call_target="tpu_custom_call" | custom-call | flops 201326592 | bytes 1048576 | tf_op jit(solution)/shard_map/spectrum/pallas_call | solution.py:242
  71.0 3.9 %pick.2.refs_0_ = f32[64,2,8,256]{3,2,1,0:T(8,128)} custom-call(s32[1]{0:T(128)} %bitcast.place, s32[1]{0:T(128)S(6)} %copy.16.live, s32[512,1]{1,0:T(8,128)S(1)} %copy.12.rows, f32[256,256]{1,0:T(8,128)S(1)} %get-tuple-element.56.entry, f32[256,256]{1,0:T(8,128)} %collective-permute-done.12.state, f32[256,256]{1,0:T(8,128)} %collective-permute-done.13.side, ...), custom_call_target="tpu_custom_call" | custom-call | flops 805306368 | bytes 1048576 | tf_op jit(solution)/shard_map/pick/pallas_call | solution.py:205
  75.0 2.9 %pick.3 = f32[64,2,8,256]{3,2,1,0:T(8,128)} custom-call(s32[1]{0:T(128)} %bitcast.place, s32[1]{0:T(128)S(6)} %copy.16.live, s32[512,1]{1,0:T(8,128)S(1)} %copy.12.rows, f32[256,256]{1,0:T(8,128)S(1)} %get-tuple-element.43.entry, f32[256,256]{1,0:T(8,128)S(1)} %collective-permute-done.5.state, ...), custom_call_target="tpu_custom_call", output_to_operand_aliasing={{}: (11, {})} | custom-call | flops 805306368 | bytes 1048576 | tf_op jit(solution)/shard_map/pick/pallas_call | solution.py:205
  77.9 39.1 %all_to_all.15 = f32[64,2,8,256]{3,2,1,0:T(8,128)S(1)} all-to-all(f32[64,2,8,256]{3,2,1,0:T(8,128)} %pick.3), channel_id=1, replica_groups=mesh['energy'=64,'space'=8] {'energy'}, dimensions={0} | all-to-all | bytes 2097152 | tf_op jit(solution)/shard_map/all_to_all | solution.py:304
  117.0 4.2 %convolve.1 = f32[128,8,256]{2,1,0:T(8,128)S(1)} custom-call(bf16[128,128]{1,0:T(8,128)(2,1)S(1)} %copy-done.1, bf16[128,128]{1,0:T(8,128)(2,1)S(1)} %copy-done.2, bf16[128,128]{1,0:T(8,128)(2,1)S(1)} %copy-done.3, bf16[128,128]{1,0:T(8,128)(2,1)S(1)} %copy-done.4, f32[128,8,256]{2,1,0:T(8,128)S(1)} %bitcast.11, f32[8,128,256]{2,1,0:T(8,128)S(1)} %spectrum.1.other), custom_call_target="tpu_custom_call" | custom-call | flops 402653184 | bytes 1048576 | tf_op jit(solution)/shard_map/convolve/pallas_call | solution.py:269
  121.1 34.3 %all_to_all.16 = f32[64,2,8,256]{3,2,1,0:T(8,128)S(1)} all-to-all(f32[64,2,8,256]{3,2,1,0:T(8,128)S(1)} %bitcast.12), channel_id=1, replica_groups=mesh['energy'=64,'space'=8] {'energy'}, dimensions={0} | all-to-all | bytes 2097152 | tf_op jit(solution)/shard_map/all_to_all | solution.py:304
  155.4 1.1 copy_bitcast_fusion
  (41 shorter events, 5.4 us)
Async XLA Ops:
  6.4 1.4 collective-permute-start.7
  7.1 1.6 %collective-permute-start = (f32[256,256]{1,0:T(8,128)S(1)}, f32[256,256]{1,0:T(8,128)S(1)}, u32[]{:S(2)}, u32[]{:S(2)}) collective-permute-start(f32[256,256]{1,0:T(8,128)S(1)} %get-tuple-element.33.before.add), channel_id=1, source_target_pairs={{0,1},{8,9},{16,17},{24,25},{32,33},{40,41},{48,49},{56,57},{64,65... | collective-permute-start | bytes 786440 | tf_op jit(solution)/shard_map/ppermute | solution.py:327
  7.8 1.2 copy-start
  7.8 14.5 %collective-permute-start.8 = (f32[256,256]{1,0:T(8,128)S(1)}, f32[256,256]{1,0:T(8,128)S(1)}, u32[]{:S(2)}, u32[]{:S(2)}) collective-permute-start(f32[256,256]{1,0:T(8,128)S(1)} %get-tuple-element.50.before), channel_id=1, source_target_pairs={{1,2},{9,10},{17,18},{25,26},{33,34},{41,42},{49,50},{57,58},{65,6... | collective-permute-start | bytes 786440 | tf_op jit(solution)/shard_map/ppermute | solution.py:327
  10.0 11.0 %copy-start.7 = (f32[2,256,256]{2,1,0:T(8,128)S(1)}, f32[2,256,256]{2,1,0:T(8,128)}, u32[]{:S(2)}) copy-start(f32[2,256,256]{2,1,0:T(8,128)} %get-tuple-element.55) | copy-start | bytes 1572868
  10.0 56.3 %all-to-all-start = ((f32[64,2,8,256]{3,2,1,0:T(8,128)}), f32[64,2,8,256]{3,2,1,0:T(8,128)}, u32[]{:S(2)}, u32[]{:S(2)}) async-start(f32[64,2,8,256]{3,2,1,0:T(8,128)} %arrange.1), calls=%async_computation | async-start | bytes 2097152 | tf_op jit(solution)/shard_map/all_to_all | solution.py:304
  21.0 31.1 %collective-permute-start.11 = (f32[2,256,256]{2,1,0:T(8,128)S(1)}, f32[2,256,256]{2,1,0:T(8,128)S(1)}, u32[]{:S(2)}, u32[]{:S(2)}) collective-permute-start(f32[2,256,256]{2,1,0:T(8,128)S(1)} %copy-done.7), channel_id=1, source_target_pairs={{4,5},{6,7},{12,13},{14,15},{20,21},{22,23},{28,29},{30,31},{36,37... | collective-permute-start | bytes 1572872 | tf_op jit(solution)/shard_map/ppermute | solution.py:321
  21.7 2.1 %collective-permute-start.1 = (f32[256,256]{1,0:T(8,128)S(1)}, f32[256,256]{1,0:T(8,128)S(1)}, u32[]{:S(2)}, u32[]{:S(2)}) collective-permute-start(f32[256,256]{1,0:T(8,128)S(1)} %get-tuple-element.37.before.after), channel_id=1, source_target_pairs={{1,2},{9,10},{17,18},{25,26},{33,34},{41,42},{49,50},{57,58},{65,6... | collective-permute-start | bytes 786440 | tf_op jit(solution)/shard_map/ppermute | solution.py:327
  22.5 10.1 %collective-permute-start.9 = (f32[256,256]{1,0:T(8,128)S(1)}, f32[256,256]{1,0:T(8,128)S(1)}, u32[]{:S(2)}, u32[]{:S(2)}) collective-permute-start(f32[256,256]{1,0:T(8,128)S(1)} %get-tuple-element.52.before), channel_id=1, source_target_pairs={{2,3},{10,11},{18,19},{26,27},{34,35},{42,43},{50,51},{58,59},{66,... | collective-permute-start | bytes 786440 | tf_op jit(solution)/shard_map/ppermute | solution.py:327
  23.8 1.5 copy-start.6
  23.8 26.4 %collective-permute-start.2 = (f32[256,256]{1,0:T(8,128)S(1)}, f32[256,256]{1,0:T(8,128)S(1)}, u32[]{:S(2)}, u32[]{:S(2)}) collective-permute-start(f32[256,256]{1,0:T(8,128)S(1)} %get-tuple-element.39.before), channel_id=1, source_target_pairs={{2,3},{10,11},{18,19},{26,27},{34,35},{42,43},{50,51},{58,59},{66,... | collective-permute-start | bytes 786440 | tf_op jit(solution)/shard_map/ppermute | solution.py:327
  25.3 31.0 %collective-permute-start.4 = (f32[2,256,256]{2,1,0:T(8,128)S(1)}, f32[2,256,256]{2,1,0:T(8,128)S(1)}, u32[]{:S(2)}, u32[]{:S(2)}) collective-permute-start(f32[2,256,256]{2,1,0:T(8,128)S(1)} %copy-done.6), channel_id=1, source_target_pairs={{4,5},{6,7},{12,13},{14,15},{20,21},{22,23},{28,29},{30,31},{36,37... | collective-permute-start | bytes 1572872 | tf_op jit(solution)/shard_map/ppermute | solution.py:321
  33.2 19.0 %collective-permute-start.10 = (f32[256,256]{1,0:T(8,128)S(1)}, f32[256,256]{1,0:T(8,128)S(1)}, u32[]{:S(2)}, u32[]{:S(2)}) collective-permute-start(f32[256,256]{1,0:T(8,128)S(1)} %get-tuple-element.54.before), channel_id=1, source_target_pairs={{3,5},{11,13},{19,21},{27,29},{35,37},{43,45},{51,53},{59,61},{67,... | collective-permute-start | bytes 786440 | tf_op jit(solution)/shard_map/ppermute | solution.py:327
  50.8 8.1 %collective-permute-start.3 = (f32[256,256]{1,0:T(8,128)S(1)}, f32[256,256]{1,0:T(8,128)S(1)}, u32[]{:S(2)}, u32[]{:S(2)}) collective-permute-start(f32[256,256]{1,0:T(8,128)S(1)} %get-tuple-element.41.before), channel_id=1, source_target_pairs={{3,5},{11,13},{19,21},{27,29},{35,37},{43,45},{51,53},{59,61},{67,... | collective-permute-start | bytes 786440 | tf_op jit(solution)/shard_map/ppermute | solution.py:327
  52.9 18.1 %collective-permute-start.12 = (f32[256,256]{1,0:T(8,128)}, f32[256,256]{1,0:T(8,128)}, u32[]{:S(2)}, u32[]{:S(2)}) collective-permute-start(f32[256,256]{1,0:T(8,128)} %get-tuple-element.57), channel_id=1, source_target_pairs={{5,7},{13,15},{21,23},{29,31},{37,39},{45,47},{53,55},{61,63},{69,... | collective-permute-start | bytes 786440 | tf_op jit(solution)/shard_map/ppermute | solution.py:327
  54.3 16.7 %collective-permute-start.13 = (f32[256,256]{1,0:T(8,128)}, f32[256,256]{1,0:T(8,128)}, u32[]{:S(2)}, u32[]{:S(2)}) collective-permute-start(f32[256,256]{1,0:T(8,128)} %get-tuple-element.57), channel_id=1, source_target_pairs={{3,4},{5,6},{11,12},{13,14},{19,20},{21,22},{27,28},{29,30},{35,36... | collective-permute-start | bytes 786440 | tf_op jit(solution)/shard_map/ppermute | solution.py:336
  59.7 5.8 %copy-start.5 = (s32[512]{0:T(512)S(1)}, s32[512]{0:T(512)}, u32[]{:S(2)}) copy-start(s32[512]{0:T(512)} %param.12) | copy-start | bytes 6148
  59.7 15.3 %collective-permute-start.5 = (f32[256,256]{1,0:T(8,128)}, f32[256,256]{1,0:T(8,128)S(1)}, u32[]{:S(2)}, u32[]{:S(2)}) collective-permute-start(f32[256,256]{1,0:T(8,128)} %get-tuple-element.44), channel_id=1, source_target_pairs={{5,7},{13,15},{21,23},{29,31},{37,39},{45,47},{53,55},{61,63},{69,... | collective-permute-start | bytes 786440 | tf_op jit(solution)/shard_map/ppermute | solution.py:327
  60.5 14.5 %collective-permute-start.6 = (f32[256,256]{1,0:T(8,128)}, f32[256,256]{1,0:T(8,128)S(1)}, u32[]{:S(2)}, u32[]{:S(2)}) collective-permute-start(f32[256,256]{1,0:T(8,128)} %get-tuple-element.44), channel_id=1, source_target_pairs={{3,4},{5,6},{11,12},{13,14},{19,20},{21,22},{27,28},{29,30},{35,36... | collective-permute-start | bytes 786440 | tf_op jit(solution)/shard_map/ppermute | solution.py:336
  65.4 0.8 copy-start.1
  65.5 0.8 copy-start.2
  77.8 39.1 %copy-start.3 = (bf16[128,128]{1,0:T(8,128)(2,1)S(1)}, bf16[128,128]{1,0:T(8,128)(2,1)}, u32[]{:S(2)}) copy-start(bf16[128,128]{1,0:T(8,128)(2,1)} %constant.21.inv_h) | copy-start | bytes 98308
  77.8 39.1 %copy-start.4 = (bf16[128,128]{1,0:T(8,128)(2,1)S(1)}, bf16[128,128]{1,0:T(8,128)(2,1)}, u32[]{:S(2)}) copy-start(bf16[128,128]{1,0:T(8,128)(2,1)} %constant.24.inv_l) | copy-start | bytes 98308

commit v4 on v3

--- a/solution.py
+++ b/solution.py
@@ -50,10 +50,11 @@
     return product(split(product(outer, inner)), outer, 1)
 
 
-def prepare_kernel(inv_all, coup_all, src_all, *refs):
+def prepare_kernel(senders, place, inv_all, coup_all, src_all, *refs):
     energies = inv_all.shape[0]
-    outs = [refs[5 * e : 5 * e + 5] for e in range(energies)]
-    inv, coup, src, kept, sem, out_sem = refs[5 * energies :]
+    outs = [refs[4 * e : 4 * e + 4] for e in range(energies)]
+    inv, coup, src, kept, sem, out_sem = refs[4 * energies :]
+    sends = functools.reduce(jnp.logical_or, [place[0] == z for z in senders])
     copies = {}
 
     def fetch(name, source, target):
@@ -72,58 +73,73 @@
             copies.pop(name).wait()
         return split(ref[name[1:]])
 
-    stores = []
     for e in range(energies):
-        map_h, map_l, add, first, pair = outs[e]
+        map_h, map_l, add, _ = outs[e]
         step, inj = [], []
         for b in range(2):
             left = ready(inv, "inv", e, b)
-            moved = product(left, ready(coup, "coup", b))
-            step.append(split(moved))
+            step.append(split(product(left, ready(coup, "coup", b))))
             inj.append(sandwich(left, ready(src, "src", e, b)))
-            if b == 0:
-                kept[e, 0, 0] = moved
-                kept[e, 0, 1] = inj[0]
-                stores.append(pltpu.make_async_copy(kept.at[e, 0], first, out_sem.at[e, 0]))
-                stores[-1].start()
         added = sandwich(step[1], split(inj[0])) + inj[1]
         mapped = product(step[1], step[0])
         add[...] = added
         map_h[...], map_l[...] = split(mapped)
-        kept[e, 1, 0] = mapped
-        kept[e, 1, 1] = added
-        stores.append(pltpu.make_async_copy(kept.at[e, 1], pair, out_sem.at[e, 1]))
-        stores[-1].start()
-    for store in stores:
-        store.wait()
-
-
-def prepare(inverses, coupling, source):
+        kept[e, 0] = mapped
+        kept[e, 1] = added
+
+    @pl.when(sends)
+    def _():
+        stores = [pltpu.make_async_copy(kept.at[e], outs[e][3], out_sem.at[e]) for e in range(energies)]
+        for store in stores:
+            store.start()
+        for store in stores:
+            store.wait()
+
+
+def prepare(inverses, coupling, source, place, senders):
     energies, _, width, _ = inverses.shape
     square = (width, width)
-    outs = [pltpu.VMEM(square, BF)] * 2 + [pltpu.VMEM(square, F32)] + [pltpu.HBM((2, *square), F32)] * 2
+    outs = [pltpu.VMEM(square, BF)] * 2 + [pltpu.VMEM(square, F32), pltpu.HBM((2, *square), F32)]
     results = pl.pallas_call(
-        prepare_kernel,
-        in_specs=[HBM] * 3,
-        out_specs=([VMEM] * 3 + [HBM] * 2) * energies,
+        functools.partial(prepare_kernel, senders),
+        in_specs=[SMEM] + [HBM] * 3,
+        out_specs=([VMEM] * 3 + [HBM]) * energies,
         out_shape=outs * energies,
         scratch_shapes=[
             pltpu.VMEM(inverses.shape, F32),
             pltpu.VMEM(coupling.shape, F32),
             pltpu.VMEM(source.shape, F32),
-            pltpu.VMEM((energies, 2, 2, *square), F32),
+            pltpu.VMEM((energies, 2, *square), F32),
             pltpu.SemaphoreType.DMA((2 + 4 * energies,)),
-            pltpu.SemaphoreType.DMA((energies, 2)),
+            pltpu.SemaphoreType.DMA((energies,)),
         ],
         compiler_params=params(16),
         cost_estimate=cost(18),
         name="prepare",
-    )(*[far(a) for a in (inverses, coupling, source)])
-    return [results[5 * e : 5 * e + 5] for e in range(energies)]
+    )(place, *[far(a) for a in (inverses, coupling, source)])
+    return [results[4 * e : 4 * e + 4] for e in range(energies)]
 
 
 def through(pair, state):
     return sandwich(split(pair[0]), split(state)) + pair[1]
+
+
+def tick_kernel(after, out):
+    out[...] = after[:8, :128]
+
+
+def tick(after):
+    parts = lax.axis_size("energy")
+    small = pl.pallas_call(
+        tick_kernel,
+        in_specs=[VMEM],
+        out_specs=VMEM,
+        out_shape=pltpu.VMEM((8, 128), F32),
+        compiler_params=params(),
+        cost_estimate=cost(0.01),
+        name="tick",
+    )(after)
+    return lax.ppermute(small, "energy", [(i, i ^ 1) for i in range(parts)])
 
 
 def hop_kernel(target, skips, place, entry, before, state, map_h, map_l, add, *refs):
@@ -157,12 +173,15 @@
     )(*operands)
 
 
-def pick_kernel(energy, end, late, place, live, rows, entry, state, side, map_h, map_l, add, pair, first, *refs):
-    out, begin, block, picked, sem = refs[-5:]
+def pick_kernel(energy, end, late, place, live, rows, entry, state, side, map_h, map_l, add, pair, *refs):
+    inv_all, coup_all, src_all = refs[:3]
+    out, begin, blocks, picked, sem = refs[-5:]
     here = place[0]
     sideways = functools.reduce(jnp.logical_or, [here == z for z in late])
-    fetch = pltpu.make_async_copy(first, block, sem.at[0])
-    fetch.start()
+    wanted = (inv_all.at[energy, 0], coup_all.at[0], src_all.at[energy, 0])
+    fetches = [pltpu.make_async_copy(source, blocks.at[i], sem.at[i]) for i, source in enumerate(wanted)]
+    for fetch in fetches:
+        fetch.start()
 
     @pl.when(here == end)
     def _():
@@ -183,20 +202,24 @@
     chosen = jnp.where((column == rows[...]) & (slot < live[0]), 1.0, 0.0).astype(BF)
     start = split(begin[...])
     last = sandwich((map_h[...], map_l[...]), start) + add[...]
-    fetch.wait()
-    high, low = split(jnp.concatenate([through(block, begin[...]), last], axis=0))
+    for fetch in fetches:
+        fetch.wait()
+    inner = sandwich(split(blocks[1]), start) + blocks[2]
+    first = sandwich(split(blocks[0]), split(inner))
+    high, low = split(jnp.concatenate([first, last], axis=0))
     dot = lambda a, b: jnp.dot(a, b, preferred_element_type=F32)
     picked[...] = (dot(chosen, high) + dot(chosen, low)).reshape(picked.shape)
-    store = pltpu.make_async_copy(picked, out.at[:, energy], sem.at[1])
+    store = pltpu.make_async_copy(picked, out.at[:, energy], sem.at[3])
     store.start()
     store.wait()
 
 
-def pick(energy, end, late, place, live, rows, entry, state, side, pair, given, before=None):
+def pick(energy, end, late, place, live, rows, entry, state, side, pair, given, inputs, before=None):
     width = entry.shape[1]
     slots = rows.shape[0]
-    operands = [place, live, rows, *[near(a) for a in (entry, state, side, *given[:3])], pair, far(given[3])]
-    specs = [SMEM, SMEM] + [VMEM] * (len(operands) - 3) + [HBM]
+    operands = [place, live, rows, *[near(a) for a in (entry, state, side, *given[:3])], pair]
+    specs = [SMEM, SMEM] + [VMEM] * (len(operands) - 2) + [HBM] * 3
+    operands += [far(a) for a in inputs]
     aliases = {}
     if before is not None:
         aliases = {len(operands): 0}
@@ -209,9 +232,9 @@
         out_shape=pltpu.HBM((slots // 8, 2, 8, width), F32),
         scratch_shapes=[
             pltpu.VMEM((width, width), F32),
-            pltpu.VMEM((2, width, width), F32),
+            pltpu.VMEM((3, width, width), F32),
             pltpu.VMEM((slots // 8, 8, width), F32),
-            pltpu.SemaphoreType.DMA((2,)),
+            pltpu.SemaphoreType.DMA((4,)),
         ],
         input_output_aliases=aliases,
         compiler_params=params(12),
@@ -317,8 +340,8 @@
     direct = list(range(middle))
     odd = list(range(middle + 1, spaces, 2))
     path = direct + odd
-    given = prepare(inverses, coupling, source)
-    pairs = [lax.ppermute(given[e][4], "space", [(z - 1, z) for z in odd]) for e in range(energies)]
+    given = prepare(inverses, coupling, source, place, [z - 1 for z in odd])
+    pairs = [lax.ppermute(given[e][3], "space", [(z - 1, z) for z in odd]) for e in range(energies)]
     outgoing = [given[e][2] for e in range(energies)]
     entry = [jnp.zeros((width, width), F32)] * energies
     state = [None] * energies
@@ -327,20 +350,20 @@
             state[e] = lax.ppermute(outgoing[e], "space", [(here, target)])
             if target != path[-1]:
                 pair = pairs[e] if target in odd else None
-                weight = 60 if step == 1 else 2
+                weight = 200 if step in (1, 2) else 2
                 outgoing[e], entry[e] = hop(target, place, entry[e], outgoing[e], state[e], given[e], pair, weight)
         if step == 0:
-            chunks = arrange(screened.reshape(energies, parts, group, width), outgoing[-1])
+            chunks = arrange(screened.reshape(energies, parts, group, width), tick(outgoing[-1]))
     late = [z - 1 for z in odd]
     other = spectrum(forward, exchange(chunks).reshape(count, group, width))
     side = [lax.ppermute(outgoing[e], "space", [(path[path.index(z) - 1], z - 1) for z in odd]) for e in range(energies)]
 
     rows = kept_rows.reshape(slots, 1)
-    other, state[0] = lax.optimization_barrier((other, state[0]))
+    inputs = (inverses, coupling, source)
     picked = None
     for e in range(energies):
         picked = pick(
-            e, path[-1], late, place, live_count, rows, entry[e], state[e], side[e], pairs[e], given[e], picked
+            e, path[-1], late, place, live_count, rows, entry[e], state[e], side[e], pairs[e], given[e], inputs, picked
         )
     data = exchange(picked).reshape(count, group, width)
     sigma = convolve(forward, inverse, data, other)

time: 157 us -> 154 us (0.981)
  the two profiles are of different devices: /device:TPU:192 before, /device:TPU:384 now
where the time goes in v4:
time: 154 us; the launch traced here: 153 us
  waiting for transfers between devices  49.8 us (32%)
  starting transfers between devices  39 us (25%)
  blocking collectives  34.3 us (22%)
  Pallas kernels  28.1 us (18%)
    all_to_all x1, blocking collectives, exchange(): lax.all_to_all(chunks, 'energy', split_axis=0, concat_axis=0, tiled=True)  34.3 us
    ppermute x2, waiting for transfers between devices, body(): lax.ppermute(outgoing[e], 'space', [(path[path.index(z) - 1], z - 1) for...  24.5 us
    all_to_all x2, waiting for transfers between devices, exchange(): lax.all_to_all(chunks, 'energy', split_axis=0, concat_axis=0, tiled=True)  24.1 us
    all_to_all x2, starting transfers between devices, exchange(): lax.all_to_all(chunks, 'energy', split_axis=0, concat_axis=0, tiled=True)  21.7 us
    ppermute x10, starting transfers between devices, body(): state[e] = lax.ppermute(outgoing[e], 'space', [(here, target)])  9.1 us
    pallas_call x2, Pallas kernels, pick(): pl.pallas_call(functools.partial(pick_kernel, energy, end, late), in_spec...  8.07 us
    pallas_call x1, Pallas kernels, prepare(): pl.pallas_call(functools.partial(prepare_kernel, senders), in_specs=[SMEM...  6.5 us
    pallas_call x1, Pallas kernels, spectrum(): pl.pallas_call(spectrum_kernel, in_specs=[VMEM] * 3, out_specs=VMEM, out_...  4.7 us
  transfers between devices with their start and end apart: 17, of which 4 were waited for; matrix products, arithmetic and copies ran while one was open for 0% of the time, Pallas kernels for 11%

profile of v4, /device:TPU:384, one launch (start us, length us, event | category | flops | bytes accessed | tf_op | source)
XLA Modules:
  0.0 153.5 jit_solution(4832609984823521269)
XLA Ops:
  0.0 6.5 %prepare.1 = (bf16[256,256]{1,0:T(8,128)(2,1)S(1)}, bf16[256,256]{1,0:T(8,128)(2,1)S(1)}, f32[256,256]{1,0:T(8,128)S(1)}, f32[2,256,256]{2,1,0:T(8,128)}, bf16[2...) custom-call(s32[1]{0:T(128)} %bitcast.place, ...), custom_call_target="tpu_custom_call" | custom-call | flops 1811939328 | bytes 1048576 | tf_op jit(solution)/shard_map/prepare/pallas_call | solution.py:103
  8.0 1.5 collective-permute-start.8
  9.5 1.9 %collective-permute-start.14 = (f32[8,128]{1,0:T(8,128)S(1)}, f32[8,128]{1,0:T(8,128)S(1)}, u32[]{:S(2)}, u32[]{:S(2)}) collective-permute-start(f32[8,128]{1,0:T(8,128)S(1)} %tick.1), channel_id=1, source_target_pairs={{0,8},{8,0},{16,24},{24,16},{32,40},{40,32},{48,56},{56,48},{64,72... | collective-permute-start | bytes 12296 | tf_op jit(solution)/shard_map/ppermute | solution.py:142
  11.5 2.4 %collective-permute-start.11 = (f32[2,256,256]{2,1,0:T(8,128)}, f32[2,256,256]{2,1,0:T(8,128)S(1)}, u32[]{:S(2)}, u32[]{:S(2)}) collective-permute-start(f32[2,256,256]{2,1,0:T(8,128)} %get-tuple-element.50), channel_id=1, source_target_pairs={{4,5},{6,7},{12,13},{14,15},{20,21},{22,23},{28,29},{30,31},{36,37... | collective-permute-start | bytes 1572872 | tf_op jit(solution)/shard_map/ppermute | solution.py:344
  13.9 1.3 collective-permute-start.4
  15.2 1.4 collective-permute-start.1
  16.6 1.0 arrange.1
  17.7 10.8 %all-to-all-start.1 = ((f32[64,2,8,256]{3,2,1,0:T(8,128)}), f32[64,2,8,256]{3,2,1,0:T(8,128)}, u32[]{:S(2)}, u32[]{:S(2)}) async-start(f32[64,2,8,256]{3,2,1,0:T(8,128)} %arrange.1), calls=%async_computation.1 | async-start | bytes 2097152 | tf_op jit(solution)/shard_map/all_to_all | solution.py:327
  28.5 1.0 hop.13
  30.2 1.0 hop.9
  34.8 1.3 collective-permute-start.13
  36.1 1.1 collective-permute-done.4.refs_0_.pair
  38.0 1.5 collective-permute-start.5
  39.5 1.3 collective-permute-start.6
  41.6 18.8 %collective-permute-done.13.side = f32[256,256]{1,0:T(8,128)S(1)} collective-permute-done((f32[256,256]{1,0:T(8,128)}, f32[256,256]{1,0:T(8,128)S(1)}, u32[]{:S(2)}, u32[]{:S(2)}) %collective-permute-start.13) | collective-permute-done | bytes 262176 | tf_op jit(solution)/shard_map/ppermute | solution.py:359
  60.5 3.5 %pick.2.refs_3_ = f32[64,2,8,256]{3,2,1,0:T(8,128)} custom-call(s32[1]{0:T(128)} %bitcast.place, s32[1]{0:T(128)S(6)} %copy.16.live, s32[512,1]{1,0:T(8,128)S(1)} %copy.12.rows, f32[256,256]{1,0:T(8,128)S(1)} %get-tuple-element.51.entry, f32[256,256]{1,0:T(8,128)S(1)} %collective-permute-done.12.state, f32[256,256]{1,0:T(8,128)S(1)} %collective-permute-done.13.side, ...), custom_call_target="tpu_custom_call" | custom-call | flops 805306368 | bytes 1048576 | tf_op jit(solution)/shard_map/pick/pallas_call | solution.py:228
  64.0 5.7 %collective-permute-done.6.side = f32[256,256]{1,0:T(8,128)} collective-permute-done((f32[256,256]{1,0:T(8,128)}, f32[256,256]{1,0:T(8,128)}, u32[]{:S(2)}, u32[]{:S(2)}) %collective-permute-start.6) | collective-permute-done | bytes 262176 | tf_op jit(solution)/shard_map/ppermute | solution.py:359
  69.7 4.5 %pick.3 = f32[64,2,8,256]{3,2,1,0:T(8,128)} custom-call(s32[1]{0:T(128)} %bitcast.place, s32[1]{0:T(128)S(6)} %copy.16.live, s32[512,1]{1,0:T(8,128)S(1)} %copy.12.rows, f32[256,256]{1,0:T(8,128)S(1)} %get-tuple-element.39.entry, f32[256,256]{1,0:T(8,128)} %collective-permute-done.5.state, ...), custom_call_target="tpu_custom_call", output_to_operand_aliasing={{}: (13, {})} | custom-call | flops 805306368 | bytes 1048576 | tf_op jit(solution)/shard_map/pick/pallas_call | solution.py:228
  74.3 10.8 %all-to-all-start = ((f32[64,2,8,256]{3,2,1,0:T(8,128)}), f32[64,2,8,256]{3,2,1,0:T(8,128)S(1)}, u32[]{:S(2)}, u32[]{:S(2)}) async-start(f32[64,2,8,256]{3,2,1,0:T(8,128)} %pick.3), calls=%async_computation | async-start | bytes 2097152 | tf_op jit(solution)/shard_map/all_to_all | solution.py:327
  85.1 4.7 %spectrum.1.other = f32[8,128,256]{2,1,0:T(8,128)S(1)} custom-call(bf16[128,128]{1,0:T(8,128)(2,1)S(1)} %copy-done.1, bf16[128,128]{1,0:T(8,128)(2,1)S(1)} %copy-done.2, f32[128,8,256]{2,1,0:T(8,128)} %bitcast.4.data), custom_call_target="tpu_custom_call" | custom-call | flops 201326592 | bytes 1048576 | tf_op jit(solution)/shard_map/spectrum/pallas_call | solution.py:265
  89.9 24.1 %all-to-all-done = f32[64,2,8,256]{3,2,1,0:T(8,128)S(1)} async-done(((f32[64,2,8,256]{3,2,1,0:T(8,128)}), f32[64,2,8,256]{3,2,1,0:T(8,128)S(1)}, u32[]{:S(2)}, u32[]{:S(2)}) %all-to-all-start) | async-done | bytes 1048608 | tf_op jit(solution)/shard_map/all_to_all | solution.py:327
  114.0 4.2 %convolve.1 = f32[128,8,256]{2,1,0:T(8,128)S(1)} custom-call(bf16[128,128]{1,0:T(8,128)(2,1)S(1)} %copy-done.1, bf16[128,128]{1,0:T(8,128)(2,1)S(1)} %copy-done.2, bf16[128,128]{1,0:T(8,128)(2,1)S(1)} %copy-done.3, bf16[128,128]{1,0:T(8,128)(2,1)S(1)} %copy-done.4, f32[128,8,256]{2,1,0:T(8,128)S(1)} %bitcast.11, f32[8,128,256]{2,1,0:T(8,128)S(1)} %spectrum.1.other), custom_call_target="tpu_custom_call" | custom-call | flops 402653184 | bytes 1048576 | tf_op jit(solution)/shard_map/convolve/pallas_call | solution.py:292
  118.2 34.3 %all_to_all.15 = f32[64,2,8,256]{3,2,1,0:T(8,128)S(1)} all-to-all(f32[64,2,8,256]{3,2,1,0:T(8,128)S(1)} %bitcast.12), channel_id=1, replica_groups=mesh['energy'=64,'space'=8] {'energy'}, dimensions={0} | all-to-all | bytes 2097152 | tf_op jit(solution)/shard_map/all_to_all | solution.py:327
  152.4 1.1 copy_bitcast_fusion
  (41 shorter events, 6.6 us)
Async XLA Ops:
  6.5 1.4 collective-permute-start.7
  7.2 2.3 %collective-permute-start = (f32[256,256]{1,0:T(8,128)S(1)}, f32[256,256]{1,0:T(8,128)S(1)}, u32[]{:S(2)}, u32[]{:S(2)}) collective-permute-start(f32[256,256]{1,0:T(8,128)S(1)} %get-tuple-element.29.before.add), channel_id=1, source_target_pairs={{0,1},{8,9},{16,17},{24,25},{32,33},{40,41},{48,49},{56,57},{64,65... | collective-permute-start | bytes 786440 | tf_op jit(solution)/shard_map/ppermute | solution.py:350
  8.0 8.6 %copy-start = (f32[2,512,256]{2,1,0:T(8,128)S(1)}, f32[2,512,256]{2,1,0:T(8,128)}, u32[]{:S(2)}) copy-start(f32[2,512,256]{2,1,0:T(8,128)} %param.11) | copy-start | bytes 3145732
  8.0 20.5 %collective-permute-start.8 = (f32[256,256]{1,0:T(8,128)S(1)}, f32[256,256]{1,0:T(8,128)}, u32[]{:S(2)}, u32[]{:S(2)}) collective-permute-start(f32[256,256]{1,0:T(8,128)S(1)} %get-tuple-element.45.before), channel_id=1, source_target_pairs={{1,2},{9,10},{17,18},{25,26},{33,34},{41,42},{49,50},{57,58},{65,6... | collective-permute-start | bytes 786440 | tf_op jit(solution)/shard_map/ppermute | solution.py:350
  9.5 7.1 %collective-permute-start.14 = (f32[8,128]{1,0:T(8,128)S(1)}, f32[8,128]{1,0:T(8,128)S(1)}, u32[]{:S(2)}, u32[]{:S(2)}) collective-permute-start(f32[8,128]{1,0:T(8,128)S(1)} %tick.1), channel_id=1, source_target_pairs={{0,8},{8,0},{16,24},{24,16},{32,40},{40,32},{48,56},{56,48},{64,72... | collective-permute-start | bytes 12296 | tf_op jit(solution)/shard_map/ppermute | solution.py:142
  11.5 21.9 %collective-permute-start.11 = (f32[2,256,256]{2,1,0:T(8,128)}, f32[2,256,256]{2,1,0:T(8,128)S(1)}, u32[]{:S(2)}, u32[]{:S(2)}) collective-permute-start(f32[2,256,256]{2,1,0:T(8,128)} %get-tuple-element.50), channel_id=1, source_target_pairs={{4,5},{6,7},{12,13},{14,15},{20,21},{22,23},{28,29},{30,31},{36,37... | collective-permute-start | bytes 1572872 | tf_op jit(solution)/shard_map/ppermute | solution.py:344
  13.9 23.3 %collective-permute-start.4 = (f32[2,256,256]{2,1,0:T(8,128)}, f32[2,256,256]{2,1,0:T(8,128)S(1)}, u32[]{:S(2)}, u32[]{:S(2)}) collective-permute-start(f32[2,256,256]{2,1,0:T(8,128)} %get-tuple-element.38), channel_id=1, source_target_pairs={{4,5},{6,7},{12,13},{14,15},{20,21},{22,23},{28,29},{30,31},{36,37... | collective-permute-start | bytes 1572872 | tf_op jit(solution)/shard_map/ppermute | solution.py:344
  15.2 15.0 %collective-permute-start.1 = (f32[256,256]{1,0:T(8,128)S(1)}, f32[256,256]{1,0:T(8,128)}, u32[]{:S(2)}, u32[]{:S(2)}) collective-permute-start(f32[256,256]{1,0:T(8,128)S(1)} %get-tuple-element.33.before.after), channel_id=1, source_target_pairs={{1,2},{9,10},{17,18},{25,26},{33,34},{41,42},{49,50},{57,58},{65,6... | collective-permute-start | bytes 786440 | tf_op jit(solution)/shard_map/ppermute | solution.py:350
  17.7 56.6 %all-to-all-start.1 = ((f32[64,2,8,256]{3,2,1,0:T(8,128)}), f32[64,2,8,256]{3,2,1,0:T(8,128)}, u32[]{:S(2)}, u32[]{:S(2)}) async-start(f32[64,2,8,256]{3,2,1,0:T(8,128)} %arrange.1), calls=%async_computation.1 | async-start | bytes 2097152 | tf_op jit(solution)/shard_map/all_to_all | solution.py:327
  29.5 2.4 %collective-permute-start.9 = (f32[256,256]{1,0:T(8,128)S(1)}, f32[256,256]{1,0:T(8,128)S(1)}, u32[]{:S(2)}, u32[]{:S(2)}) collective-permute-start(f32[256,256]{1,0:T(8,128)S(1)} %get-tuple-element.47.before), channel_id=1, source_target_pairs={{2,3},{10,11},{18,19},{26,27},{34,35},{42,43},{50,51},{58,59},{66,... | collective-permute-start | bytes 786440 | tf_op jit(solution)/shard_map/ppermute | solution.py:350
  31.2 1.4 collective-permute-start.2
  31.9 1.4 collective-permute-start.10
  32.7 4.6 %collective-permute-start.3 = (f32[256,256]{1,0:T(8,128)S(1)}, f32[256,256]{1,0:T(8,128)S(1)}, u32[]{:S(2)}, u32[]{:S(2)}) collective-permute-start(f32[256,256]{1,0:T(8,128)S(1)} %get-tuple-element.37.before), channel_id=1, source_target_pairs={{3,5},{11,13},{19,21},{27,29},{35,37},{43,45},{51,53},{59,61},{67,... | collective-permute-start | bytes 786440 | tf_op jit(solution)/shard_map/ppermute | solution.py:350
  34.2 7.5 %collective-permute-start.12 = (f32[256,256]{1,0:T(8,128)}, f32[256,256]{1,0:T(8,128)S(1)}, u32[]{:S(2)}, u32[]{:S(2)}) collective-permute-start(f32[256,256]{1,0:T(8,128)} %get-tuple-element.52), channel_id=1, source_target_pairs={{5,7},{13,15},{21,23},{29,31},{37,39},{45,47},{53,55},{61,63},{69,... | collective-permute-start | bytes 786440 | tf_op jit(solution)/shard_map/ppermute | solution.py:350
  34.8 25.6 %collective-permute-start.13 = (f32[256,256]{1,0:T(8,128)}, f32[256,256]{1,0:T(8,128)S(1)}, u32[]{:S(2)}, u32[]{:S(2)}) collective-permute-start(f32[256,256]{1,0:T(8,128)} %get-tuple-element.52), channel_id=1, source_target_pairs={{3,4},{5,6},{11,12},{13,14},{19,20},{21,22},{27,28},{29,30},{35,36... | collective-permute-start | bytes 786440 | tf_op jit(solution)/shard_map/ppermute | solution.py:359
  38.0 2.8 %copy-start.5 = (s32[512]{0:T(512)S(1)}, s32[512]{0:T(512)}, u32[]{:S(2)}) copy-start(s32[512]{0:T(512)} %param.12) | copy-start | bytes 6148
  38.0 26.0 %collective-permute-start.5 = (f32[256,256]{1,0:T(8,128)}, f32[256,256]{1,0:T(8,128)}, u32[]{:S(2)}, u32[]{:S(2)}) collective-permute-start(f32[256,256]{1,0:T(8,128)} %get-tuple-element.40), channel_id=1, source_target_pairs={{5,7},{13,15},{21,23},{29,31},{37,39},{45,47},{53,55},{61,63},{69,... | collective-permute-start | bytes 786440 | tf_op jit(solution)/shard_map/ppermute | solution.py:350
  39.5 30.2 %collective-permute-start.6 = (f32[256,256]{1,0:T(8,128)}, f32[256,256]{1,0:T(8,128)}, u32[]{:S(2)}, u32[]{:S(2)}) collective-permute-start(f32[256,256]{1,0:T(8,128)} %get-tuple-element.40), channel_id=1, source_target_pairs={{3,4},{5,6},{11,12},{13,14},{19,20},{21,22},{27,28},{29,30},{35,36... | collective-permute-start | bytes 786440 | tf_op jit(solution)/shard_map/ppermute | solution.py:359
  74.2 10.9 %copy-start.1 = (bf16[128,128]{1,0:T(8,128)(2,1)S(1)}, bf16[128,128]{1,0:T(8,128)(2,1)}, u32[]{:S(2)}) copy-start(bf16[128,128]{1,0:T(8,128)(2,1)} %constant.17.fwd_h) | copy-start | bytes 98308
  74.3 10.9 %copy-start.2 = (bf16[128,128]{1,0:T(8,128)(2,1)S(1)}, bf16[128,128]{1,0:T(8,128)(2,1)}, u32[]{:S(2)}) copy-start(bf16[128,128]{1,0:T(8,128)(2,1)} %constant.20.fwd_l) | copy-start | bytes 98308
  74.3 39.7 %all-to-all-start = ((f32[64,2,8,256]{3,2,1,0:T(8,128)}), f32[64,2,8,256]{3,2,1,0:T(8,128)S(1)}, u32[]{:S(2)}, u32[]{:S(2)}) async-start(f32[64,2,8,256]{3,2,1,0:T(8,128)} %pick.3), calls=%async_computation | async-start | bytes 2097152 | tf_op jit(solution)/shard_map/all_to_all | solution.py:327
  85.1 28.9 %copy-start.3 = (bf16[128,128]{1,0:T(8,128)(2,1)S(1)}, bf16[128,128]{1,0:T(8,128)(2,1)}, u32[]{:S(2)}) copy-start(bf16[128,128]{1,0:T(8,128)(2,1)} %constant.21.inv_h) | copy-start | bytes 98308
  85.1 28.9 %copy-start.4 = (bf16[128,128]{1,0:T(8,128)(2,1)S(1)}, bf16[128,128]{1,0:T(8,128)(2,1)}, u32[]{:S(2)}) copy-start(bf16[128,128]{1,0:T(8,128)(2,1)} %constant.24.inv_l) | copy-start | bytes 98308

commit v5 on v4

--- a/solution.py
+++ b/solution.py
@@ -58,15 +58,19 @@
     copies = {}
 
     def fetch(name, source, target):
-        copies[name] = pltpu.make_async_copy(source, target, sem.at[len(copies)])
+        copies[name] = pltpu.make_async_copy(source, target, sem.at[count[0]])
         copies[name].start()
-
-    for e in range(energies):
-        for b in range(2):
-            if e == 0:
-                fetch(("coup", b), coup_all.at[b], coup.at[b])
-            fetch(("inv", e, b), inv_all.at[e, b], inv.at[e, b])
-            fetch(("src", e, b), src_all.at[e, b], src.at[e, b])
+        count[0] += 1
+
+    def fetch_block(e, b):
+        if e == 0:
+            fetch(("coup", b), coup_all.at[b], coup.at[b])
+        fetch(("inv", e, b), inv_all.at[e, b], inv.at[e, b])
+        fetch(("src", e, b), src_all.at[e, b], src.at[e, b])
+
+    count = [0]
+    order = [(e, b) for e in range(energies) for b in range(2)]
+    fetch_block(*order.pop(0))
 
     def ready(ref, *name):
         if name in copies:
@@ -78,8 +82,12 @@
         step, inj = [], []
         for b in range(2):
             left = ready(inv, "inv", e, b)
-            step.append(split(product(left, ready(coup, "coup", b))))
-            inj.append(sandwich(left, ready(src, "src", e, b)))
+            right = ready(coup, "coup", b)
+            middle = ready(src, "src", e, b)
+            if order:
+                fetch_block(*order.pop(0))
+            step.append(split(product(left, right)))
+            inj.append(sandwich(left, middle))
         added = sandwich(step[1], split(inj[0])) + inj[1]
         mapped = product(step[1], step[0])
         add[...] = added
@@ -350,9 +358,9 @@
             state[e] = lax.ppermute(outgoing[e], "space", [(here, target)])
             if target != path[-1]:
                 pair = pairs[e] if target in odd else None
-                weight = 200 if step in (1, 2) else 2
+                weight = 200 if step in (2, 3) else 2
                 outgoing[e], entry[e] = hop(target, place, entry[e], outgoing[e], state[e], given[e], pair, weight)
-        if step == 0:
+        if step == 1:
             chunks = arrange(screened.reshape(energies, parts, group, width), tick(outgoing[-1]))
     late = [z - 1 for z in odd]
     other = spectrum(forward, exchange(chunks).reshape(count, group, width))

time: 154 us -> 152 us (0.987)
  waiting for transfers between devices: 49.8 us -> 47.9 us
    ppermute x2, waiting for transfers between devices: 24.5 us -> 21.1 us  [body(): lax.ppermute(outgoing[e], 'space', [(path[path.index(z) - 1], z - 1) for...]
  transfers between devices with their start and end apart: 17 -> 17, of which waited for: 4 -> 4; matrix products, arithmetic and copies ran while one was open for 0% -> 0% of each run, Pallas kernels for 11% -> 12%
where the time goes in v5:
time: 152 us; the launch traced here: 151 us
  waiting for transfers between devices  47.9 us (32%)
  starting transfers between devices  38.8 us (26%)
  blocking collectives  34.2 us (23%)
  Pallas kernels  27.9 us (18%)
    all_to_all x1, blocking collectives, exchange(): lax.all_to_all(chunks, 'energy', split_axis=0, concat_axis=0, tiled=True)  34.2 us
    all_to_all x2, waiting for transfers between devices, exchange(): lax.all_to_all(chunks, 'energy', split_axis=0, concat_axis=0, tiled=True)  24.1 us
    all_to_all x2, starting transfers between devices, exchange(): lax.all_to_all(chunks, 'energy', split_axis=0, concat_axis=0, tiled=True)  21.4 us
    ppermute x2, waiting for transfers between devices, body(): lax.ppermute(outgoing[e], 'space', [(path[path.index(z) - 1], z - 1) for...  21.1 us
    ppermute x10, starting transfers between devices, body(): state[e] = lax.ppermute(outgoing[e], 'space', [(here, target)])  9.1 us
    pallas_call x2, Pallas kernels, pick(): pl.pallas_call(functools.partial(pick_kernel, energy, end, late), in_spec...  8.07 us
    pallas_call x1, Pallas kernels, prepare(): pl.pallas_call(functools.partial(prepare_kernel, senders), in_specs=[SMEM...  6.32 us
    pallas_call x1, Pallas kernels, spectrum(): pl.pallas_call(spectrum_kernel, in_specs=[VMEM] * 3, out_specs=VMEM, out_...  4.71 us
  transfers between devices with their start and end apart: 17, of which 4 were waited for; matrix products, arithmetic and copies ran while one was open for 0% of the time, Pallas kernels for 12%

profile of v5, /device:TPU:384, one launch (start us, length us, event | category | flops | bytes accessed | tf_op | source)
XLA Modules:
  0.0 151.2 jit_solution(12008602256393634219)
XLA Ops:
  0.0 6.3 %prepare.1 = (bf16[256,256]{1,0:T(8,128)(2,1)S(1)}, bf16[256,256]{1,0:T(8,128)(2,1)S(1)}, f32[256,256]{1,0:T(8,128)S(1)}, f32[2,256,256]{2,1,0:T(8,128)}, bf16[2...) custom-call(s32[1]{0:T(128)} %bitcast.place, ...), custom_call_target="tpu_custom_call" | custom-call | flops 1811939328 | bytes 1048576 | tf_op jit(solution)/shard_map/prepare/pallas_call | solution.py:111
  9.3 1.5 collective-permute-start.9
  10.9 1.9 %collective-permute-start.14 = (f32[8,128]{1,0:T(8,128)S(1)}, f32[8,128]{1,0:T(8,128)S(1)}, u32[]{:S(2)}, u32[]{:S(2)}) collective-permute-start(f32[8,128]{1,0:T(8,128)S(1)} %tick.1), channel_id=1, source_target_pairs={{0,8},{8,0},{16,24},{24,16},{32,40},{40,32},{48,56},{56,48},{64,72... | collective-permute-start | bytes 12296 | tf_op jit(solution)/shard_map/ppermute | solution.py:150
  12.8 2.4 %collective-permute-start.11 = (f32[2,256,256]{2,1,0:T(8,128)}, f32[2,256,256]{2,1,0:T(8,128)S(1)}, u32[]{:S(2)}, u32[]{:S(2)}) collective-permute-start(f32[2,256,256]{2,1,0:T(8,128)} %get-tuple-element.50), channel_id=1, source_target_pairs={{4,5},{6,7},{12,13},{14,15},{20,21},{22,23},{28,29},{30,31},{36,37... | collective-permute-start | bytes 1572872 | tf_op jit(solution)/shard_map/ppermute | solution.py:352
  15.2 1.3 collective-permute-start.4
  16.6 1.4 collective-permute-start.2
  17.9 1.0 arrange.1
  19.0 10.8 %all-to-all-start.1 = ((f32[64,2,8,256]{3,2,1,0:T(8,128)}), f32[64,2,8,256]{3,2,1,0:T(8,128)}, u32[]{:S(2)}, u32[]{:S(2)}) async-start(f32[64,2,8,256]{3,2,1,0:T(8,128)} %arrange.1), calls=%async_computation.1 | async-start | bytes 2097152 | tf_op jit(solution)/shard_map/all_to_all | solution.py:335
  29.8 1.0 hop.14
  31.5 1.0 hop.10
  34.6 1.3 collective-permute-start.13
  35.9 2.6 %collective-permute-done.4.refs_0_.pair = f32[2,256,256]{2,1,0:T(8,128)S(1)} collective-permute-done((f32[2,256,256]{2,1,0:T(8,128)}, f32[2,256,256]{2,1,0:T(8,128)S(1)}, u32[]{:S(2)}, u32[]{:S(2)}) %collective-permute-start.4) | collective-permute-done | bytes 524320 | tf_op jit(solution)/shard_map/ppermute | solution.py:352
  39.3 1.5 collective-permute-start.5
  40.8 1.3 collective-permute-start.6
  42.9 14.1 %collective-permute-done.13.side = f32[256,256]{1,0:T(8,128)S(1)} collective-permute-done((f32[256,256]{1,0:T(8,128)}, f32[256,256]{1,0:T(8,128)S(1)}, u32[]{:S(2)}, u32[]{:S(2)}) %collective-permute-start.13) | collective-permute-done | bytes 262176 | tf_op jit(solution)/shard_map/ppermute | solution.py:367
  57.0 3.5 %pick.2.refs_3_ = f32[64,2,8,256]{3,2,1,0:T(8,128)} custom-call(s32[1]{0:T(128)} %bitcast.place, s32[1]{0:T(128)S(6)} %copy.16.live, s32[512,1]{1,0:T(8,128)S(1)} %copy.12.rows, f32[256,256]{1,0:T(8,128)S(1)} %get-tuple-element.51.entry, f32[256,256]{1,0:T(8,128)S(1)} %collective-permute-done.12.state, f32[256,256]{1,0:T(8,128)S(1)} %collective-permute-done.13.side, ...), custom_call_target="tpu_custom_call" | custom-call | flops 805306368 | bytes 1048576 | tf_op jit(solution)/shard_map/pick/pallas_call | solution.py:236
  60.6 7.0 %collective-permute-done.6.side = f32[256,256]{1,0:T(8,128)} collective-permute-done((f32[256,256]{1,0:T(8,128)}, f32[256,256]{1,0:T(8,128)}, u32[]{:S(2)}, u32[]{:S(2)}) %collective-permute-start.6) | collective-permute-done | bytes 262176 | tf_op jit(solution)/shard_map/ppermute | solution.py:367
  67.6 4.5 %pick.3 = f32[64,2,8,256]{3,2,1,0:T(8,128)} custom-call(s32[1]{0:T(128)} %bitcast.place, s32[1]{0:T(128)S(6)} %copy.16.live, s32[512,1]{1,0:T(8,128)S(1)} %copy.12.rows, f32[256,256]{1,0:T(8,128)S(1)} %get-tuple-element.39.entry, f32[256,256]{1,0:T(8,128)} %collective-permute-done.5.state, ...), custom_call_target="tpu_custom_call", output_to_operand_aliasing={{}: (13, {})} | custom-call | flops 805306368 | bytes 1048576 | tf_op jit(solution)/shard_map/pick/pallas_call | solution.py:236
  72.2 10.6 %all-to-all-start = ((f32[64,2,8,256]{3,2,1,0:T(8,128)}), f32[64,2,8,256]{3,2,1,0:T(8,128)S(1)}, u32[]{:S(2)}, u32[]{:S(2)}) async-start(f32[64,2,8,256]{3,2,1,0:T(8,128)} %pick.3), calls=%async_computation | async-start | bytes 2097152 | tf_op jit(solution)/shard_map/all_to_all | solution.py:335
  82.8 4.7 %spectrum.1.other = f32[8,128,256]{2,1,0:T(8,128)S(1)} custom-call(bf16[128,128]{1,0:T(8,128)(2,1)S(1)} %copy-done.1, bf16[128,128]{1,0:T(8,128)(2,1)S(1)} %copy-done.2, f32[128,8,256]{2,1,0:T(8,128)} %bitcast.4.data), custom_call_target="tpu_custom_call" | custom-call | flops 201326592 | bytes 1048576 | tf_op jit(solution)/shard_map/spectrum/pallas_call | solution.py:273
  87.6 24.1 %all-to-all-done = f32[64,2,8,256]{3,2,1,0:T(8,128)S(1)} async-done(((f32[64,2,8,256]{3,2,1,0:T(8,128)}), f32[64,2,8,256]{3,2,1,0:T(8,128)S(1)}, u32[]{:S(2)}, u32[]{:S(2)}) %all-to-all-start) | async-done | bytes 1048608 | tf_op jit(solution)/shard_map/all_to_all | solution.py:335
  111.7 4.2 %convolve.1 = f32[128,8,256]{2,1,0:T(8,128)S(1)} custom-call(bf16[128,128]{1,0:T(8,128)(2,1)S(1)} %copy-done.1, bf16[128,128]{1,0:T(8,128)(2,1)S(1)} %copy-done.2, bf16[128,128]{1,0:T(8,128)(2,1)S(1)} %copy-done.3, bf16[128,128]{1,0:T(8,128)(2,1)S(1)} %copy-done.4, f32[128,8,256]{2,1,0:T(8,128)S(1)} %bitcast.11, f32[8,128,256]{2,1,0:T(8,128)S(1)} %spectrum.1.other), custom_call_target="tpu_custom_call" | custom-call | flops 402653184 | bytes 1048576 | tf_op jit(solution)/shard_map/convolve/pallas_call | solution.py:300
  115.9 34.2 %all_to_all.15 = f32[64,2,8,256]{3,2,1,0:T(8,128)S(1)} all-to-all(f32[64,2,8,256]{3,2,1,0:T(8,128)S(1)} %bitcast.12), channel_id=1, replica_groups=mesh['energy'=64,'space'=8] {'energy'}, dimensions={0} | all-to-all | bytes 2097152 | tf_op jit(solution)/shard_map/all_to_all | solution.py:335
  150.1 1.1 copy_bitcast_fusion
  (41 shorter events, 6.6 us)
Async XLA Ops:
  6.3 1.4 collective-permute-start.7
  7.0 1.5 collective-permute-start
  7.8 1.4 collective-permute-start.8
  8.5 2.3 %collective-permute-start.1 = (f32[256,256]{1,0:T(8,128)S(1)}, f32[256,256]{1,0:T(8,128)S(1)}, u32[]{:S(2)}, u32[]{:S(2)}) collective-permute-start(f32[256,256]{1,0:T(8,128)S(1)} %get-tuple-element.33.before), channel_id=1, source_target_pairs={{1,2},{9,10},{17,18},{25,26},{33,34},{41,42},{49,50},{57,58},{65,6... | collective-permute-start | bytes 786440 | tf_op jit(solution)/shard_map/ppermute | solution.py:358
  9.3 8.6 %copy-start = (f32[2,512,256]{2,1,0:T(8,128)S(1)}, f32[2,512,256]{2,1,0:T(8,128)}, u32[]{:S(2)}) copy-start(f32[2,512,256]{2,1,0:T(8,128)} %param.11) | copy-start | bytes 3145732
  9.3 20.5 %collective-permute-start.9 = (f32[256,256]{1,0:T(8,128)S(1)}, f32[256,256]{1,0:T(8,128)}, u32[]{:S(2)}, u32[]{:S(2)}) collective-permute-start(f32[256,256]{1,0:T(8,128)S(1)} %get-tuple-element.47.before), channel_id=1, source_target_pairs={{2,3},{10,11},{18,19},{26,27},{34,35},{42,43},{50,51},{58,59},{66,... | collective-permute-start | bytes 786440 | tf_op jit(solution)/shard_map/ppermute | solution.py:358
  10.9 7.1 %collective-permute-start.14 = (f32[8,128]{1,0:T(8,128)S(1)}, f32[8,128]{1,0:T(8,128)S(1)}, u32[]{:S(2)}, u32[]{:S(2)}) collective-permute-start(f32[8,128]{1,0:T(8,128)S(1)} %tick.1), channel_id=1, source_target_pairs={{0,8},{8,0},{16,24},{24,16},{32,40},{40,32},{48,56},{56,48},{64,72... | collective-permute-start | bytes 12296 | tf_op jit(solution)/shard_map/ppermute | solution.py:150
  12.8 20.4 %collective-permute-start.11 = (f32[2,256,256]{2,1,0:T(8,128)}, f32[2,256,256]{2,1,0:T(8,128)S(1)}, u32[]{:S(2)}, u32[]{:S(2)}) collective-permute-start(f32[2,256,256]{2,1,0:T(8,128)} %get-tuple-element.50), channel_id=1, source_target_pairs={{4,5},{6,7},{12,13},{14,15},{20,21},{22,23},{28,29},{30,31},{36,37... | collective-permute-start | bytes 1572872 | tf_op jit(solution)/shard_map/ppermute | solution.py:352
  15.2 23.3 %collective-permute-start.4 = (f32[2,256,256]{2,1,0:T(8,128)}, f32[2,256,256]{2,1,0:T(8,128)S(1)}, u32[]{:S(2)}, u32[]{:S(2)}) collective-permute-start(f32[2,256,256]{2,1,0:T(8,128)} %get-tuple-element.38), channel_id=1, source_target_pairs={{4,5},{6,7},{12,13},{14,15},{20,21},{22,23},{28,29},{30,31},{36,37... | collective-permute-start | bytes 1572872 | tf_op jit(solution)/shard_map/ppermute | solution.py:352
  16.6 15.0 %collective-permute-start.2 = (f32[256,256]{1,0:T(8,128)S(1)}, f32[256,256]{1,0:T(8,128)}, u32[]{:S(2)}, u32[]{:S(2)}) collective-permute-start(f32[256,256]{1,0:T(8,128)S(1)} %get-tuple-element.35.before.after), channel_id=1, source_target_pairs={{2,3},{10,11},{18,19},{26,27},{34,35},{42,43},{50,51},{58,59},{66,... | collective-permute-start | bytes 786440 | tf_op jit(solution)/shard_map/ppermute | solution.py:358
  19.0 53.2 %all-to-all-start.1 = ((f32[64,2,8,256]{3,2,1,0:T(8,128)}), f32[64,2,8,256]{3,2,1,0:T(8,128)}, u32[]{:S(2)}, u32[]{:S(2)}) async-start(f32[64,2,8,256]{3,2,1,0:T(8,128)} %arrange.1), calls=%async_computation.1 | async-start | bytes 2097152 | tf_op jit(solution)/shard_map/all_to_all | solution.py:335
  30.8 2.4 %collective-permute-start.10 = (f32[256,256]{1,0:T(8,128)S(1)}, f32[256,256]{1,0:T(8,128)S(1)}, u32[]{:S(2)}, u32[]{:S(2)}) collective-permute-start(f32[256,256]{1,0:T(8,128)S(1)} %get-tuple-element.49.before), channel_id=1, source_target_pairs={{3,5},{11,13},{19,21},{27,29},{35,37},{43,45},{51,53},{59,61},{67,... | collective-permute-start | bytes 786440 | tf_op jit(solution)/shard_map/ppermute | solution.py:358
  32.5 6.1 %collective-permute-start.3 = (f32[256,256]{1,0:T(8,128)S(1)}, f32[256,256]{1,0:T(8,128)S(1)}, u32[]{:S(2)}, u32[]{:S(2)}) collective-permute-start(f32[256,256]{1,0:T(8,128)S(1)} %get-tuple-element.37.before), channel_id=1, source_target_pairs={{3,5},{11,13},{19,21},{27,29},{35,37},{43,45},{51,53},{59,61},{67,... | collective-permute-start | bytes 786440 | tf_op jit(solution)/shard_map/ppermute | solution.py:358
  34.0 9.0 %collective-permute-start.12 = (f32[256,256]{1,0:T(8,128)}, f32[256,256]{1,0:T(8,128)S(1)}, u32[]{:S(2)}, u32[]{:S(2)}) collective-permute-start(f32[256,256]{1,0:T(8,128)} %get-tuple-element.52), channel_id=1, source_target_pairs={{5,7},{13,15},{21,23},{29,31},{37,39},{45,47},{53,55},{61,63},{69,... | collective-permute-start | bytes 786440 | tf_op jit(solution)/shard_map/ppermute | solution.py:358
  34.6 22.4 %collective-permute-start.13 = (f32[256,256]{1,0:T(8,128)}, f32[256,256]{1,0:T(8,128)S(1)}, u32[]{:S(2)}, u32[]{:S(2)}) collective-permute-start(f32[256,256]{1,0:T(8,128)} %get-tuple-element.52), channel_id=1, source_target_pairs={{3,4},{5,6},{11,12},{13,14},{19,20},{21,22},{27,28},{29,30},{35,36... | collective-permute-start | bytes 786440 | tf_op jit(solution)/shard_map/ppermute | solution.py:367
  39.3 2.8 %copy-start.5 = (s32[512]{0:T(512)S(1)}, s32[512]{0:T(512)}, u32[]{:S(2)}) copy-start(s32[512]{0:T(512)} %param.12) | copy-start | bytes 6148
  39.3 21.2 %collective-permute-start.5 = (f32[256,256]{1,0:T(8,128)}, f32[256,256]{1,0:T(8,128)}, u32[]{:S(2)}, u32[]{:S(2)}) collective-permute-start(f32[256,256]{1,0:T(8,128)} %get-tuple-element.40), channel_id=1, source_target_pairs={{5,7},{13,15},{21,23},{29,31},{37,39},{45,47},{53,55},{61,63},{69,... | collective-permute-start | bytes 786440 | tf_op jit(solution)/shard_map/ppermute | solution.py:358
  40.8 26.8 %collective-permute-start.6 = (f32[256,256]{1,0:T(8,128)}, f32[256,256]{1,0:T(8,128)}, u32[]{:S(2)}, u32[]{:S(2)}) collective-permute-start(f32[256,256]{1,0:T(8,128)} %get-tuple-element.40), channel_id=1, source_target_pairs={{3,4},{5,6},{11,12},{13,14},{19,20},{21,22},{27,28},{29,30},{35,36... | collective-permute-start | bytes 786440 | tf_op jit(solution)/shard_map/ppermute | solution.py:367
  72.2 10.6 %copy-start.1 = (bf16[128,128]{1,0:T(8,128)(2,1)S(1)}, bf16[128,128]{1,0:T(8,128)(2,1)}, u32[]{:S(2)}) copy-start(bf16[128,128]{1,0:T(8,128)(2,1)} %constant.17.fwd_h) | copy-start | bytes 98308
  72.2 10.6 %copy-start.2 = (bf16[128,128]{1,0:T(8,128)(2,1)S(1)}, bf16[128,128]{1,0:T(8,128)(2,1)}, u32[]{:S(2)}) copy-start(bf16[128,128]{1,0:T(8,128)(2,1)} %constant.20.fwd_l) | copy-start | bytes 98308
  72.2 39.5 %all-to-all-start = ((f32[64,2,8,256]{3,2,1,0:T(8,128)}), f32[64,2,8,256]{3,2,1,0:T(8,128)S(1)}, u32[]{:S(2)}, u32[]{:S(2)}) async-start(f32[64,2,8,256]{3,2,1,0:T(8,128)} %pick.3), calls=%async_computation | async-start | bytes 2097152 | tf_op jit(solution)/shard_map/all_to_all | solution.py:335
  82.8 28.9 %copy-start.3 = (bf16[128,128]{1,0:T(8,128)(2,1)S(1)}, bf16[128,128]{1,0:T(8,128)(2,1)}, u32[]{:S(2)}) copy-start(bf16[128,128]{1,0:T(8,128)(2,1)} %constant.21.inv_h) | copy-start | bytes 98308
  82.8 28.9 %copy-start.4 = (bf16[128,128]{1,0:T(8,128)(2,1)S(1)}, bf16[128,128]{1,0:T(8,128)(2,1)}, u32[]{:S(2)}) copy-start(bf16[128,128]{1,0:T(8,128)(2,1)} %constant.24.inv_l) | copy-start | bytes 98308

commit v6 on v4

--- a/solution.py
+++ b/solution.py
@@ -50,74 +50,148 @@
     return product(split(product(outer, inner)), outer, 1)
 
 
-def prepare_kernel(senders, place, inv_all, coup_all, src_all, *refs):
+def prepare_energy(e, senders, place, inputs, outs, buffers, fetched, work, kept, sem, out_sem):
+    inv_all, coup_all, src_all = inputs
+    inv, coup, src = buffers
+    map_h, map_l, add, pair = outs
+
+    def fetch(b):
+        copies = [(inv_all.at[e, b], inv.at[e, b]), (src_all.at[e, b], src.at[e, b])]
+        if b not in fetched:
+            copies.append((coup_all.at[b], coup.at[b]))
+            fetched.append(b)
+        started = [pltpu.make_async_copy(*ends, sem.at[e, b, n]) for n, ends in enumerate(copies)]
+        for copy in started:
+            copy.start()
+        return started
+
+    coming = fetch(0)
+    for b in range(2):
+        for copy in coming:
+            copy.wait()
+        coming = fetch(1) if b == 0 else []
+        left = split(inv[e, b])
+        work[b, 0] = product(left, split(coup[b]))
+        work[b, 1] = sandwich(left, split(src[e, b]))
+    last = split(work[1, 0])
+    added = sandwich(last, split(work[0, 1])) + work[1, 1]
+    mapped = product(last, split(work[0, 0]))
+    add[...] = added
+    map_h[...], map_l[...] = split(mapped)
+    kept[0] = mapped
+    kept[1] = added
+
+    @pl.when(functools.reduce(jnp.logical_or, [place[0] == z for z in senders]))
+    def _():
+        store = pltpu.make_async_copy(kept, pair, out_sem)
+        store.start()
+        store.wait()
+
+
+def first_terms(inputs, outs, buffers, kept, sem, out_sem):
+    inv_all, coup_all, src_all = inputs
+    inv, coup, src = buffers
     energies = inv_all.shape[0]
-    outs = [refs[4 * e : 4 * e + 4] for e in range(energies)]
-    inv, coup, src, kept, sem, out_sem = refs[4 * energies :]
-    sends = functools.reduce(jnp.logical_or, [place[0] == z for z in senders])
-    copies = {}
-
-    def fetch(name, source, target):
-        copies[name] = pltpu.make_async_copy(source, target, sem.at[len(copies)])
-        copies[name].start()
-
+    copies = [pltpu.make_async_copy(coup_all.at[0], coup.at[0], sem.at[0, 0, 2])]
     for e in range(energies):
-        for b in range(2):
-            if e == 0:
-                fetch(("coup", b), coup_all.at[b], coup.at[b])
-            fetch(("inv", e, b), inv_all.at[e, b], inv.at[e, b])
-            fetch(("src", e, b), src_all.at[e, b], src.at[e, b])
-
-    def ready(ref, *name):
-        if name in copies:
-            copies.pop(name).wait()
-        return split(ref[name[1:]])
-
+        copies.append(pltpu.make_async_copy(inv_all.at[e, 0], inv.at[e, 0], sem.at[e, 0, 0]))
+        copies.append(pltpu.make_async_copy(src_all.at[e, 0], src.at[e, 0], sem.at[e, 0, 1]))
+    for copy in copies:
+        copy.start()
+    for copy in copies:
+        copy.wait()
+    right = split(coup[0])
+    stores = []
     for e in range(energies):
-        map_h, map_l, add, _ = outs[e]
-        step, inj = [], []
-        for b in range(2):
-            left = ready(inv, "inv", e, b)
-            step.append(split(product(left, ready(coup, "coup", b))))
-            inj.append(sandwich(left, ready(src, "src", e, b)))
-        added = sandwich(step[1], split(inj[0])) + inj[1]
-        mapped = product(step[1], step[0])
-        add[...] = added
-        map_h[...], map_l[...] = split(mapped)
-        kept[e, 0] = mapped
-        kept[e, 1] = added
-
-    @pl.when(sends)
-    def _():
-        stores = [pltpu.make_async_copy(kept.at[e], outs[e][3], out_sem.at[e]) for e in range(energies)]
-        for store in stores:
-            store.start()
-        for store in stores:
-            store.wait()
-
-
-def prepare(inverses, coupling, source, place, senders):
+        left = split(inv[e, 0])
+        kept[e, 0] = product(left, right)
+        kept[e, 1] = sandwich(left, split(src[e, 0]))
+        stores.append(pltpu.make_async_copy(kept.at[e], outs.at[e], out_sem.at[e]))
+        stores[-1].start()
+    for store in stores:
+        store.wait()
+
+
+def early_kernel(senders, place, core, *refs):
+    inputs, outs, (inv, coup, src, work, kept, sem, out_sem) = refs[:3], refs[3:11], refs[11:]
+    fetched = []
+    buffers = (inv, coup, src)
+    prepare_energy(0, senders, place, inputs, outs[:4], buffers, fetched, work, kept.at[0], sem, out_sem.at[0])
+
+    @pl.when(core[0] == 1)
+    def _():
+        prepare_energy(1, senders, place, inputs, outs[4:], buffers, fetched, work, kept.at[1], sem, out_sem.at[1])
+
+
+def later_kernel(senders, place, core, *refs):
+    inputs, before, outs, first = refs[:3], refs[3:7], refs[7:11], refs[11]
+    inv, coup, src, work, kept, sem, out_sem = refs[12:]
+    buffers = (inv, coup, src)
+
+    @pl.when(core[0] == 0)
+    def _():
+        prepare_energy(1, senders, place, inputs, outs, buffers, [], work, kept.at[1], sem, out_sem.at[1])
+
+    @pl.when(core[0] == 1)
+    def _():
+        for source, target in zip(before[:3], outs[:3]):
+            target[...] = source[...]
+        first_terms(inputs, first, buffers, kept, sem, out_sem)
+
+
+def rest_kernel(core, *refs):
+    inputs, first = refs[:3], refs[4]
+    inv, coup, src, kept, sem, out_sem = refs[5:]
+
+    @pl.when(core[0] == 0)
+    def _():
+        first_terms(inputs, first, (inv, coup, src), kept, sem, out_sem)
+
+
+def prepare(inverses, coupling, source, place, core, senders):
     energies, _, width, _ = inverses.shape
     square = (width, width)
+    inputs = [far(a) for a in (inverses, coupling, source)]
     outs = [pltpu.VMEM(square, BF)] * 2 + [pltpu.VMEM(square, F32), pltpu.HBM((2, *square), F32)]
-    results = pl.pallas_call(
-        functools.partial(prepare_kernel, senders),
-        in_specs=[SMEM] + [HBM] * 3,
-        out_specs=([VMEM] * 3 + [HBM]) * energies,
+    specs = [VMEM] * 3 + [HBM]
+    first = pltpu.HBM((energies, 2, *square), F32)
+    buffers = [pltpu.VMEM(a.shape, F32) for a in (inverses, coupling, source)]
+    work = pltpu.VMEM((2, 2, *square), F32)
+    kept = pltpu.VMEM((energies, 2, *square), F32)
+    sems = [pltpu.SemaphoreType.DMA((energies, 2, 3)), pltpu.SemaphoreType.DMA((energies,))]
+    early = pl.pallas_call(
+        functools.partial(early_kernel, senders),
+        in_specs=[SMEM] * 2 + [HBM] * 3,
+        out_specs=specs * energies,
         out_shape=outs * energies,
-        scratch_shapes=[
-            pltpu.VMEM(inverses.shape, F32),
-            pltpu.VMEM(coupling.shape, F32),
-            pltpu.VMEM(source.shape, F32),
-            pltpu.VMEM((energies, 2, *square), F32),
-            pltpu.SemaphoreType.DMA((2 + 4 * energies,)),
-            pltpu.SemaphoreType.DMA((energies,)),
-        ],
+        scratch_shapes=buffers + [work, kept] + sems,
         compiler_params=params(16),
-        cost_estimate=cost(18),
-        name="prepare",
-    )(place, *[far(a) for a in (inverses, coupling, source)])
-    return [results[4 * e : 4 * e + 4] for e in range(energies)]
+        cost_estimate=cost(12),
+        name="prepare_early",
+    )(place, core, *inputs)
+    later = pl.pallas_call(
+        functools.partial(later_kernel, senders),
+        in_specs=[SMEM] * 2 + [HBM] * 3 + specs,
+        out_specs=specs + [HBM],
+        out_shape=outs + [first],
+        input_output_aliases={8: 3},
+        scratch_shapes=buffers + [work, kept] + sems,
+        compiler_params=params(16),
+        cost_estimate=cost(9),
+        name="prepare_later",
+    )(place, core, *inputs, *early[4:])
+    first = pl.pallas_call(
+        rest_kernel,
+        in_specs=[SMEM] + [HBM] * 4,
+        out_specs=HBM,
+        out_shape=first,
+        input_output_aliases={4: 0},
+        scratch_shapes=buffers + [kept] + sems,
+        compiler_params=params(16),
+        cost_estimate=cost(4),
+        name="first_terms",
+    )(core, *inputs, later[4])
+    return [early[:4], later[:4]], first
 
 
 def through(pair, state):
@@ -174,14 +248,12 @@
 
 
 def pick_kernel(energy, end, late, place, live, rows, entry, state, side, map_h, map_l, add, pair, *refs):
-    inv_all, coup_all, src_all = refs[:3]
-    out, begin, blocks, picked, sem = refs[-5:]
+    first_all = refs[0]
+    out, begin, block, picked, sem = refs[-5:]
     here = place[0]
     sideways = functools.reduce(jnp.logical_or, [here == z for z in late])
-    wanted = (inv_all.at[energy, 0], coup_all.at[0], src_all.at[energy, 0])
-    fetches = [pltpu.make_async_copy(source, blocks.at[i], sem.at[i]) for i, source in enumerate(wanted)]
-    for fetch in fetches:
-        fetch.start()
+    fetch = pltpu.make_async_copy(first_all.at[energy], block, sem.at[0])
+    fetch.start()
 
     @pl.when(here == end)
     def _():
@@ -202,24 +274,26 @@
     chosen = jnp.where((column == rows[...]) & (slot < live[0]), 1.0, 0.0).astype(BF)
     start = split(begin[...])
     last = sandwich((map_h[...], map_l[...]), start) + add[...]
-    for fetch in fetches:
-        fetch.wait()
-    inner = sandwich(split(blocks[1]), start) + blocks[2]
-    first = sandwich(split(blocks[0]), split(inner))
-    high, low = split(jnp.concatenate([first, last], axis=0))
+    fetch.wait()
+    high, low = split(jnp.concatenate([sandwich(split(block[0]), start) + block[1], last], axis=0))
     dot = lambda a, b: jnp.dot(a, b, preferred_element_type=F32)
-    picked[...] = (dot(chosen, high) + dot(chosen, low)).reshape(picked.shape)
-    store = pltpu.make_async_copy(picked, out.at[:, energy], sem.at[3])
-    store.start()
-    store.wait()
-
-
-def pick(energy, end, late, place, live, rows, entry, state, side, pair, given, inputs, before=None):
+    stores = []
+    half = slots // 2
+    for n in range(2):
+        rows_in, groups = slice(n * half, (n + 1) * half), pl.ds(n * half // 8, half // 8)
+        picked[groups] = (dot(chosen[rows_in], high) + dot(chosen[rows_in], low)).reshape(half // 8, 8, width)
+        stores.append(pltpu.make_async_copy(picked.at[groups], out.at[groups, energy], sem.at[1 + n]))
+        stores[-1].start()
+    for store in stores:
+        store.wait()
+
+
+def pick(energy, end, late, place, live, rows, entry, state, side, pair, given, first, before=None):
     width = entry.shape[1]
     slots = rows.shape[0]
     operands = [place, live, rows, *[near(a) for a in (entry, state, side, *given[:3])], pair]
-    specs = [SMEM, SMEM] + [VMEM] * (len(operands) - 2) + [HBM] * 3
-    operands += [far(a) for a in inputs]
+    specs = [SMEM, SMEM] + [VMEM] * (len(operands) - 2) + [HBM]
+    operands.append(far(first))
     aliases = {}
     if before is not None:
         aliases = {len(operands): 0}
@@ -232,9 +306,9 @@
         out_shape=pltpu.HBM((slots // 8, 2, 8, width), F32),
         scratch_shapes=[
             pltpu.VMEM((width, width), F32),
-            pltpu.VMEM((3, width, width), F32),
+            pltpu.VMEM((2, width, width), F32),
             pltpu.VMEM((slots // 8, 8, width), F32),
-            pltpu.SemaphoreType.DMA((4,)),
+            pltpu.SemaphoreType.DMA((3,)),
         ],
         input_output_aliases=aliases,
         compiler_params=params(12),
@@ -340,7 +414,8 @@
     direct = list(range(middle))
     odd = list(range(middle + 1, spaces, 2))
     path = direct + odd
-    given = prepare(inverses, coupling, source, place, [z - 1 for z in odd])
+    core = (lax.axis_index("energy").astype(jnp.int32) % 2).reshape(1)
+    given, first = prepare(inverses, coupling, source, place, core, [z - 1 for z in odd])
     pairs = [lax.ppermute(given[e][3], "space", [(z - 1, z) for z in odd]) for e in range(energies)]
     outgoing = [given[e][2] for e in range(energies)]
     entry = [jnp.zeros((width, width), F32)] * energies
@@ -350,20 +425,19 @@
             state[e] = lax.ppermute(outgoing[e], "space", [(here, target)])
             if target != path[-1]:
                 pair = pairs[e] if target in odd else None
-                weight = 200 if step in (1, 2) else 2
+                weight = 200 if step in (2, 3) else 2
                 outgoing[e], entry[e] = hop(target, place, entry[e], outgoing[e], state[e], given[e], pair, weight)
-        if step == 0:
+        if step == 1:
             chunks = arrange(screened.reshape(energies, parts, group, width), tick(outgoing[-1]))
     late = [z - 1 for z in odd]
     other = spectrum(forward, exchange(chunks).reshape(count, group, width))
     side = [lax.ppermute(outgoing[e], "space", [(path[path.index(z) - 1], z - 1) for z in odd]) for e in range(energies)]
 
     rows = kept_rows.reshape(slots, 1)
-    inputs = (inverses, coupling, source)
     picked = None
     for e in range(energies):
         picked = pick(
-            e, path[-1], late, place, live_count, rows, entry[e], state[e], side[e], pairs[e], given[e], inputs, picked
+            e, path[-1], late, place, live_count, rows, entry[e], state[e], side[e], pairs[e], given[e], first, picked
         )
     data = exchange(picked).reshape(count, group, width)
     sigma = convolve(forward, inverse, data, other)

time: 154 us -> 155 us (level)
  waiting for transfers between devices: 49.8 us -> 45.2 us
  Pallas kernels: 28.1 us -> 31.8 us
  starting transfers between devices: 39 us -> 41 us
    ppermute x2, waiting for transfers between devices: 24.5 us -> 18.8 us  [body(): lax.ppermute(outgoing[e], 'space', [(path[path.index(z) - 1], z - 1) for...]
    pallas_call x1 -> x3, Pallas kernels: 6.5 us -> 11.4 us  [the longest x1 4.08 us: prepare(): pl.pallas_call(functools.partial(later_kernel, senders), in_specs=[SMEM]...]
    ppermute x1, starting transfers between devices: 1.92 us -> 4.76 us  [tick(): return lax.ppermute(small, 'energy', [(i, i ^ 1) for i in range(parts)])]
  transfers between devices with their start and end apart: 17 -> 17, of which waited for: 4 -> 4; matrix products, arithmetic and copies ran while one was open for 0% -> 0% of each run, Pallas kernels for 11% -> 15%
where the time goes in v6:
time: 155 us; the launch traced here: 154 us
  waiting for transfers between devices  45.2 us (29%)
  starting transfers between devices  41 us (26%)
  blocking collectives  34.3 us (22%)
  Pallas kernels  31.8 us (21%)
    all_to_all x1, blocking collectives, exchange(): lax.all_to_all(chunks, 'energy', split_axis=0, concat_axis=0, tiled=True)  34.3 us
    all_to_all x2, waiting for transfers between devices, exchange(): lax.all_to_all(chunks, 'energy', split_axis=0, concat_axis=0, tiled=True)  24.1 us
    all_to_all x2, starting transfers between devices, exchange(): lax.all_to_all(chunks, 'energy', split_axis=0, concat_axis=0, tiled=True)  21.4 us
    ppermute x2, waiting for transfers between devices, body(): lax.ppermute(outgoing[e], 'space', [(path[path.index(z) - 1], z - 1) for...  18.8 us
    ppermute x10, starting transfers between devices, body(): state[e] = lax.ppermute(outgoing[e], 'space', [(here, target)])  9.08 us
    pallas_call x2, Pallas kernels, pick(): pl.pallas_call(functools.partial(pick_kernel, energy, end, late), in_spec...  6.83 us
    ppermute x1, starting transfers between devices, tick(): return lax.ppermute(small, 'energy', [(i, i ^ 1) for i in range(parts)])  4.76 us
    pallas_call x1, Pallas kernels, spectrum(): pl.pallas_call(spectrum_kernel, in_specs=[VMEM] * 3, out_specs=VMEM, out_...  4.7 us
  transfers between devices with their start and end apart: 17, of which 4 were waited for; matrix products, arithmetic and copies ran while one was open for 0% of the time, Pallas kernels for 15%

profile of v6, /device:TPU:384, one launch (start us, length us, event | category | flops | bytes accessed | tf_op | source)
XLA Modules:
  0.0 154.5 jit_solution(95926841812345402)
XLA Ops:
  0.0 4.0 %prepare_early.1 = (bf16[256,256]{1,0:T(8,128)(2,1)S(1)}, bf16[256,256]{1,0:T(8,128)(2,1)S(1)}, f32[256,256]{1,0:T(8,128)S(1)}, f32[2,256,256]{2,1,0:T(8,128)}, ...) custom-call(s32[1]{0:T(128)} %bitcast.place, ...), custom_call_target="tpu_custom_call" | custom-call | flops 1207959552 | bytes 1048576 | tf_op jit(solution)/shard_map/prepare_early/pallas_call | solution.py:162
  4.7 4.1 %prepare_later.1 = (bf16[256,256]{1,0:T(8,128)(2,1)S(1)}, bf16[256,256]{1,0:T(8,128)(2,1)S(1)}, f32[256,256]{1,0:T(8,128)S(1)}, f32[2,256,256]{2,1,0:T(8,128)}, f32[2,2,256,256]{3,2,1,0:T(8,128)}) custom-call(s32[1]{0:T(128)} %bitcast.place, s32[1]{0:T(128)} %bitcast.2.core, f32[2,2,256,256]{3,2,1,0:T(8,128)} %refs_0_.5, ...), custom_call_target="tpu_custom_call", output_to_operand_aliasing={{3}: (8, {})} | custom-call | flops 905969664 | bytes 1048576 | tf_op jit(solution)/shard_map/prepare_later/pallas_call | solution.py:172
  11.1 1.5 collective-permute-start.9
  12.7 4.8 %collective-permute-start.14 = (f32[8,128]{1,0:T(8,128)S(1)}, f32[8,128]{1,0:T(8,128)S(1)}, u32[]{:S(2)}, u32[]{:S(2)}) collective-permute-start(f32[8,128]{1,0:T(8,128)S(1)} %tick.1), channel_id=1, source_target_pairs={{0,8},{8,0},{16,24},{24,16},{32,40},{40,32},{48,56},{56,48},{64,72... | collective-permute-start | bytes 12296 | tf_op jit(solution)/shard_map/ppermute | solution.py:216
  17.4 1.8 %collective-permute-start.11 = (f32[2,256,256]{2,1,0:T(8,128)}, f32[2,256,256]{2,1,0:T(8,128)S(1)}, u32[]{:S(2)}, u32[]{:S(2)}) collective-permute-start(f32[2,256,256]{2,1,0:T(8,128)} %get-tuple-element.60), channel_id=1, source_target_pairs={{4,5},{6,7},{12,13},{14,15},{20,21},{22,23},{28,29},{30,31},{36,37... | collective-permute-start | bytes 1572872 | tf_op jit(solution)/shard_map/ppermute | solution.py:419
  19.3 1.3 collective-permute-start.4
  20.6 1.4 collective-permute-start.2
  22.0 1.0 arrange.1
  23.0 10.8 %all-to-all-start.1 = ((f32[64,2,8,256]{3,2,1,0:T(8,128)}), f32[64,2,8,256]{3,2,1,0:T(8,128)}, u32[]{:S(2)}, u32[]{:S(2)}) async-start(f32[64,2,8,256]{3,2,1,0:T(8,128)} %arrange.1), calls=%async_computation.1 | async-start | bytes 2097152 | tf_op jit(solution)/shard_map/all_to_all | solution.py:401
  38.6 1.3 collective-permute-start.13
  39.9 2.2 %collective-permute-done.4.refs_0_.pair = f32[2,256,256]{2,1,0:T(8,128)S(1)} collective-permute-done((f32[2,256,256]{2,1,0:T(8,128)}, f32[2,256,256]{2,1,0:T(8,128)S(1)}, u32[]{:S(2)}, u32[]{:S(2)}) %collective-permute-start.4) | collective-permute-done | bytes 524320 | tf_op jit(solution)/shard_map/ppermute | solution.py:419
  42.8 1.5 collective-permute-start.5
  44.3 1.3 collective-permute-start.6
  46.4 3.3 %first_terms.1.refs_0_ = f32[2,2,256,256]{3,2,1,0:T(8,128)} custom-call(s32[1]{0:T(128)} %bitcast.2.core, f32[2,2,256,256]{3,2,1,0:T(8,128)} %refs_0_.5, f32[2,256,256]{2,1,0:T(8,128)} %refs_1_.5, f32[2,2,256,256]{3,2,1,0:T(8,128)} %refs_2_.5, f32[2,2,256,256]{3,2,1,0:T(8,128)} %get-tuple-element.50.refs_3_), custom_call_target="tpu_custom_call", output_to_operand_aliasing={{}: (4, {})} | custom-call | flops 402653184 | bytes 1048576 | tf_op jit(solution)/shard_map/first_terms/pallas_call | solution.py:183
  49.7 12.1 %collective-permute-done.13.side = f32[256,256]{1,0:T(8,128)S(1)} collective-permute-done((f32[256,256]{1,0:T(8,128)}, f32[256,256]{1,0:T(8,128)S(1)}, u32[]{:S(2)}, u32[]{:S(2)}) %collective-permute-start.13) | collective-permute-done | bytes 262176 | tf_op jit(solution)/shard_map/ppermute | solution.py:434
  61.9 2.9 %pick.2.refs_1_ = f32[64,2,8,256]{3,2,1,0:T(8,128)} custom-call(s32[1]{0:T(128)} %bitcast.place, s32[1]{0:T(128)S(6)} %copy.20.live, s32[512,1]{1,0:T(8,128)S(1)} %copy.14.rows, f32[256,256]{1,0:T(8,128)S(1)} %get-tuple-element.61.entry, f32[256,256]{1,0:T(8,128)S(1)} %collective-permute-done.12.state, f32[256,256]{1,0:T(8,128)S(1)} %collective-permute-done.13.side, ...), custom_call_target="tpu_custom_call" | custom-call | flops 805306368 | bytes 1048576 | tf_op jit(solution)/shard_map/pick/pallas_call | solution.py:302
  64.8 6.7 %collective-permute-done.6.side = f32[256,256]{1,0:T(8,128)} collective-permute-done((f32[256,256]{1,0:T(8,128)}, f32[256,256]{1,0:T(8,128)}, u32[]{:S(2)}, u32[]{:S(2)}) %collective-permute-start.6) | collective-permute-done | bytes 262176 | tf_op jit(solution)/shard_map/ppermute | solution.py:434
  71.5 3.9 %pick.3 = f32[64,2,8,256]{3,2,1,0:T(8,128)} custom-call(s32[1]{0:T(128)} %bitcast.place, s32[1]{0:T(128)S(6)} %copy.20.live, s32[512,1]{1,0:T(8,128)S(1)} %copy.14.rows, f32[256,256]{1,0:T(8,128)S(1)} %get-tuple-element.48.entry, f32[256,256]{1,0:T(8,128)} %collective-permute-done.5.state, ...), custom_call_target="tpu_custom_call", output_to_operand_aliasing={{}: (11, {})} | custom-call | flops 805306368 | bytes 1048576 | tf_op jit(solution)/shard_map/pick/pallas_call | solution.py:302
  75.5 10.6 %all-to-all-start = ((f32[64,2,8,256]{3,2,1,0:T(8,128)}), f32[64,2,8,256]{3,2,1,0:T(8,128)S(1)}, u32[]{:S(2)}, u32[]{:S(2)}) async-start(f32[64,2,8,256]{3,2,1,0:T(8,128)} %pick.3), calls=%async_computation | async-start | bytes 2097152 | tf_op jit(solution)/shard_map/all_to_all | solution.py:401
  86.1 4.7 %spectrum.1.other = f32[8,128,256]{2,1,0:T(8,128)S(1)} custom-call(bf16[128,128]{1,0:T(8,128)(2,1)S(1)} %copy-done.1, bf16[128,128]{1,0:T(8,128)(2,1)S(1)} %copy-done.2, f32[128,8,256]{2,1,0:T(8,128)} %bitcast.5.data), custom_call_target="tpu_custom_call" | custom-call | flops 201326592 | bytes 1048576 | tf_op jit(solution)/shard_map/spectrum/pallas_call | solution.py:339
  90.8 24.1 %all-to-all-done = f32[64,2,8,256]{3,2,1,0:T(8,128)S(1)} async-done(((f32[64,2,8,256]{3,2,1,0:T(8,128)}), f32[64,2,8,256]{3,2,1,0:T(8,128)S(1)}, u32[]{:S(2)}, u32[]{:S(2)}) %all-to-all-start) | async-done | bytes 1048608 | tf_op jit(solution)/shard_map/all_to_all | solution.py:401
  115.0 4.2 %convolve.1 = f32[128,8,256]{2,1,0:T(8,128)S(1)} custom-call(bf16[128,128]{1,0:T(8,128)(2,1)S(1)} %copy-done.1, bf16[128,128]{1,0:T(8,128)(2,1)S(1)} %copy-done.2, bf16[128,128]{1,0:T(8,128)(2,1)S(1)} %copy-done.3, bf16[128,128]{1,0:T(8,128)(2,1)S(1)} %copy-done.4, f32[128,8,256]{2,1,0:T(8,128)S(1)} %bitcast.12, f32[8,128,256]{2,1,0:T(8,128)S(1)} %spectrum.1.other), custom_call_target="tpu_custom_call" | custom-call | flops 402653184 | bytes 1048576 | tf_op jit(solution)/shard_map/convolve/pallas_call | solution.py:366
  119.1 34.3 %all_to_all.15 = f32[64,2,8,256]{3,2,1,0:T(8,128)S(1)} all-to-all(f32[64,2,8,256]{3,2,1,0:T(8,128)S(1)} %bitcast.13), channel_id=1, replica_groups=mesh['energy'=64,'space'=8] {'energy'}, dimensions={0} | all-to-all | bytes 2097152 | tf_op jit(solution)/shard_map/all_to_all | solution.py:401
  153.4 1.1 copy_bitcast_fusion
  (43 shorter events, 8.6 us)
Async XLA Ops:
  4.0 5.5 %collective-permute-start.7 = (f32[256,256]{1,0:T(8,128)S(1)}, f32[256,256]{1,0:T(8,128)S(1)}, u32[]{:S(2)}, u32[]{:S(2)}) collective-permute-start(f32[256,256]{1,0:T(8,128)S(1)} %get-tuple-element.51.before.add), channel_id=1, source_target_pairs={{0,1},{8,9},{16,17},{24,25},{32,33},{40,41},{48,49},{56,57},{64,65... | collective-permute-start | bytes 786440 | tf_op jit(solution)/shard_map/ppermute | solution.py:425
  8.8 1.5 collective-permute-start
  9.6 1.4 collective-permute-start.8
  10.3 2.3 %collective-permute-start.1 = (f32[256,256]{1,0:T(8,128)S(1)}, f32[256,256]{1,0:T(8,128)S(1)}, u32[]{:S(2)}, u32[]{:S(2)}) collective-permute-start(f32[256,256]{1,0:T(8,128)S(1)} %get-tuple-element.42.before), channel_id=1, source_target_pairs={{1,2},{9,10},{17,18},{25,26},{33,34},{41,42},{49,50},{57,58},{65,6... | collective-permute-start | bytes 786440 | tf_op jit(solution)/shard_map/ppermute | solution.py:425
  11.1 10.9 %copy-start = (f32[2,512,256]{2,1,0:T(8,128)S(1)}, f32[2,512,256]{2,1,0:T(8,128)}, u32[]{:S(2)}) copy-start(f32[2,512,256]{2,1,0:T(8,128)} %param.11) | copy-start | bytes 3145732
  11.1 22.7 %collective-permute-start.9 = (f32[256,256]{1,0:T(8,128)S(1)}, f32[256,256]{1,0:T(8,128)}, u32[]{:S(2)}, u32[]{:S(2)}) collective-permute-start(f32[256,256]{1,0:T(8,128)S(1)} %get-tuple-element.57.before), channel_id=1, source_target_pairs={{2,3},{10,11},{18,19},{26,27},{34,35},{42,43},{50,51},{58,59},{66,... | collective-permute-start | bytes 786440 | tf_op jit(solution)/shard_map/ppermute | solution.py:425
  12.7 9.3 %collective-permute-start.14 = (f32[8,128]{1,0:T(8,128)S(1)}, f32[8,128]{1,0:T(8,128)S(1)}, u32[]{:S(2)}, u32[]{:S(2)}) collective-permute-start(f32[8,128]{1,0:T(8,128)S(1)} %tick.1), channel_id=1, source_target_pairs={{0,8},{8,0},{16,24},{24,16},{32,40},{40,32},{48,56},{56,48},{64,72... | collective-permute-start | bytes 12296 | tf_op jit(solution)/shard_map/ppermute | solution.py:216
  17.4 19.8 %collective-permute-start.11 = (f32[2,256,256]{2,1,0:T(8,128)}, f32[2,256,256]{2,1,0:T(8,128)S(1)}, u32[]{:S(2)}, u32[]{:S(2)}) collective-permute-start(f32[2,256,256]{2,1,0:T(8,128)} %get-tuple-element.60), channel_id=1, source_target_pairs={{4,5},{6,7},{12,13},{14,15},{20,21},{22,23},{28,29},{30,31},{36,37... | collective-permute-start | bytes 1572872 | tf_op jit(solution)/shard_map/ppermute | solution.py:419
  19.3 22.9 %collective-permute-start.4 = (f32[2,256,256]{2,1,0:T(8,128)}, f32[2,256,256]{2,1,0:T(8,128)S(1)}, u32[]{:S(2)}, u32[]{:S(2)}) collective-permute-start(f32[2,256,256]{2,1,0:T(8,128)} %get-tuple-element.47), channel_id=1, source_target_pairs={{4,5},{6,7},{12,13},{14,15},{20,21},{22,23},{28,29},{30,31},{36,37... | collective-permute-start | bytes 1572872 | tf_op jit(solution)/shard_map/ppermute | solution.py:419
  20.6 14.9 %collective-permute-start.2 = (f32[256,256]{1,0:T(8,128)S(1)}, f32[256,256]{1,0:T(8,128)}, u32[]{:S(2)}, u32[]{:S(2)}) collective-permute-start(f32[256,256]{1,0:T(8,128)S(1)} %get-tuple-element.44.before.after), channel_id=1, source_target_pairs={{2,3},{10,11},{18,19},{26,27},{34,35},{42,43},{50,51},{58,59},{66,... | collective-permute-start | bytes 786440 | tf_op jit(solution)/shard_map/ppermute | solution.py:425
  23.0 52.5 %all-to-all-start.1 = ((f32[64,2,8,256]{3,2,1,0:T(8,128)}), f32[64,2,8,256]{3,2,1,0:T(8,128)}, u32[]{:S(2)}, u32[]{:S(2)}) async-start(f32[64,2,8,256]{3,2,1,0:T(8,128)} %arrange.1), calls=%async_computation.1 | async-start | bytes 2097152 | tf_op jit(solution)/shard_map/all_to_all | solution.py:401
  34.8 2.4 %collective-permute-start.10 = (f32[256,256]{1,0:T(8,128)S(1)}, f32[256,256]{1,0:T(8,128)S(1)}, u32[]{:S(2)}, u32[]{:S(2)}) collective-permute-start(f32[256,256]{1,0:T(8,128)S(1)} %get-tuple-element.59.before), channel_id=1, source_target_pairs={{3,5},{11,13},{19,21},{27,29},{35,37},{43,45},{51,53},{59,61},{67,... | collective-permute-start | bytes 786440 | tf_op jit(solution)/shard_map/ppermute | solution.py:425
  36.5 5.6 %collective-permute-start.3 = (f32[256,256]{1,0:T(8,128)S(1)}, f32[256,256]{1,0:T(8,128)S(1)}, u32[]{:S(2)}, u32[]{:S(2)}) collective-permute-start(f32[256,256]{1,0:T(8,128)S(1)} %get-tuple-element.46.before), channel_id=1, source_target_pairs={{3,5},{11,13},{19,21},{27,29},{35,37},{43,45},{51,53},{59,61},{67,... | collective-permute-start | bytes 786440 | tf_op jit(solution)/shard_map/ppermute | solution.py:425
  38.0 11.8 %collective-permute-start.12 = (f32[256,256]{1,0:T(8,128)}, f32[256,256]{1,0:T(8,128)S(1)}, u32[]{:S(2)}, u32[]{:S(2)}) collective-permute-start(f32[256,256]{1,0:T(8,128)} %get-tuple-element.62), channel_id=1, source_target_pairs={{5,7},{13,15},{21,23},{29,31},{37,39},{45,47},{53,55},{61,63},{69,... | collective-permute-start | bytes 786440 | tf_op jit(solution)/shard_map/ppermute | solution.py:425
  38.6 23.2 %collective-permute-start.13 = (f32[256,256]{1,0:T(8,128)}, f32[256,256]{1,0:T(8,128)S(1)}, u32[]{:S(2)}, u32[]{:S(2)}) collective-permute-start(f32[256,256]{1,0:T(8,128)} %get-tuple-element.62), channel_id=1, source_target_pairs={{3,4},{5,6},{11,12},{13,14},{19,20},{21,22},{27,28},{29,30},{35,36... | collective-permute-start | bytes 786440 | tf_op jit(solution)/shard_map/ppermute | solution.py:434
  42.8 2.8 %copy-start.5 = (s32[512]{0:T(512)S(1)}, s32[512]{0:T(512)}, u32[]{:S(2)}) copy-start(s32[512]{0:T(512)} %param.12) | copy-start | bytes 6148
  42.8 21.9 %collective-permute-start.5 = (f32[256,256]{1,0:T(8,128)}, f32[256,256]{1,0:T(8,128)}, u32[]{:S(2)}, u32[]{:S(2)}) collective-permute-start(f32[256,256]{1,0:T(8,128)} %get-tuple-element.49), channel_id=1, source_target_pairs={{5,7},{13,15},{21,23},{29,31},{37,39},{45,47},{53,55},{61,63},{69,... | collective-permute-start | bytes 786440 | tf_op jit(solution)/shard_map/ppermute | solution.py:425
  44.3 27.2 %collective-permute-start.6 = (f32[256,256]{1,0:T(8,128)}, f32[256,256]{1,0:T(8,128)}, u32[]{:S(2)}, u32[]{:S(2)}) collective-permute-start(f32[256,256]{1,0:T(8,128)} %get-tuple-element.49), channel_id=1, source_target_pairs={{3,4},{5,6},{11,12},{13,14},{19,20},{21,22},{27,28},{29,30},{35,36... | collective-permute-start | bytes 786440 | tf_op jit(solution)/shard_map/ppermute | solution.py:434
  75.4 10.6 %copy-start.1 = (bf16[128,128]{1,0:T(8,128)(2,1)S(1)}, bf16[128,128]{1,0:T(8,128)(2,1)}, u32[]{:S(2)}) copy-start(bf16[128,128]{1,0:T(8,128)(2,1)} %constant.35.fwd_h) | copy-start | bytes 98308
  75.5 10.6 %copy-start.2 = (bf16[128,128]{1,0:T(8,128)(2,1)S(1)}, bf16[128,128]{1,0:T(8,128)(2,1)}, u32[]{:S(2)}) copy-start(bf16[128,128]{1,0:T(8,128)(2,1)} %constant.38.fwd_l) | copy-start | bytes 98308
  75.5 39.5 %all-to-all-start = ((f32[64,2,8,256]{3,2,1,0:T(8,128)}), f32[64,2,8,256]{3,2,1,0:T(8,128)S(1)}, u32[]{:S(2)}, u32[]{:S(2)}) async-start(f32[64,2,8,256]{3,2,1,0:T(8,128)} %pick.3), calls=%async_computation | async-start | bytes 2097152 | tf_op jit(solution)/shard_map/all_to_all | solution.py:401
  86.1 28.9 %copy-start.3 = (bf16[128,128]{1,0:T(8,128)(2,1)S(1)}, bf16[128,128]{1,0:T(8,128)(2,1)}, u32[]{:S(2)}) copy-start(bf16[128,128]{1,0:T(8,128)(2,1)} %constant.39.inv_h) | copy-start | bytes 98308
  86.1 28.9 %copy-start.4 = (bf16[128,128]{1,0:T(8,128)(2,1)S(1)}, bf16[128,128]{1,0:T(8,128)(2,1)}, u32[]{:S(2)}) copy-start(bf16[128,128]{1,0:T(8,128)(2,1)} %constant.42.inv_l) | copy-start | bytes 98308

commit v7 on v5

--- a/solution.py
+++ b/solution.py
@@ -132,24 +132,6 @@
     return sandwich(split(pair[0]), split(state)) + pair[1]
 
 
-def tick_kernel(after, out):
-    out[...] = after[:8, :128]
-
-
-def tick(after):
-    parts = lax.axis_size("energy")
-    small = pl.pallas_call(
-        tick_kernel,
-        in_specs=[VMEM],
-        out_specs=VMEM,
-        out_shape=pltpu.VMEM((8, 128), F32),
-        compiler_params=params(),
-        cost_estimate=cost(0.01),
-        name="tick",
-    )(after)
-    return lax.ppermute(small, "energy", [(i, i ^ 1) for i in range(parts)])
-
-
 def hop_kernel(target, skips, place, entry, before, state, map_h, map_l, add, *refs):
     out, entry_out = refs[-2:]
     active = place[0] == target
@@ -181,15 +163,56 @@
     )(*operands)
 
 
+def first_kernel(inv_all, coup_all, src_all, out, inv, coup, src, kept, sem):
+    energies = inv_all.shape[0]
+    copies = [pltpu.make_async_copy(coup_all.at[0], coup, sem.at[0])]
+    for e in range(energies):
+        copies.append(pltpu.make_async_copy(inv_all.at[e, 0], inv.at[e], sem.at[1 + 2 * e]))
+        copies.append(pltpu.make_async_copy(src_all.at[e, 0], src.at[e], sem.at[2 + 2 * e]))
+    for copy in copies:
+        copy.start()
+    for copy in copies:
+        copy.wait()
+    right = split(coup[...])
+    stores = []
+    for e in range(energies):
+        left = split(inv[e])
+        kept[e, 0] = product(left, right)
+        kept[e, 1] = sandwich(left, split(src[e]))
+        stores.append(pltpu.make_async_copy(kept.at[e], out.at[e], sem.at[1 + 2 * energies + e]))
+        stores[-1].start()
+    for store in stores:
+        store.wait()
+
+
+def first_terms(inverses, coupling, source):
+    energies, _, width, _ = inverses.shape
+    square = (width, width)
+    return pl.pallas_call(
+        first_kernel,
+        in_specs=[HBM] * 3,
+        out_specs=HBM,
+        out_shape=pltpu.HBM((energies, 2, *square), F32),
+        scratch_shapes=[
+            pltpu.VMEM((energies, *square), F32),
+            pltpu.VMEM(square, F32),
+            pltpu.VMEM((energies, *square), F32),
+            pltpu.VMEM((energies, 2, *square), F32),
+            pltpu.SemaphoreType.DMA((1 + 3 * energies,)),
+        ],
+        compiler_params=params(16),
+        cost_estimate=cost(6),
+        name="first_terms",
+    )(*[far(a) for a in (inverses, coupling, source)])
+
+
 def pick_kernel(energy, end, late, place, live, rows, entry, state, side, map_h, map_l, add, pair, *refs):
-    inv_all, coup_all, src_all = refs[:3]
-    out, begin, blocks, picked, sem = refs[-5:]
+    first_all = refs[0]
+    out, begin, block, picked, sem = refs[-5:]
     here = place[0]
     sideways = functools.reduce(jnp.logical_or, [here == z for z in late])
-    wanted = (inv_all.at[energy, 0], coup_all.at[0], src_all.at[energy, 0])
-    fetches = [pltpu.make_async_copy(source, blocks.at[i], sem.at[i]) for i, source in enumerate(wanted)]
-    for fetch in fetches:
-        fetch.start()
+    fetch = pltpu.make_async_copy(first_all.at[energy], block, sem.at[0])
+    fetch.start()
 
     @pl.when(here == end)
     def _():
@@ -210,24 +233,26 @@
     chosen = jnp.where((column == rows[...]) & (slot < live[0]), 1.0, 0.0).astype(BF)
     start = split(begin[...])
     last = sandwich((map_h[...], map_l[...]), start) + add[...]
-    for fetch in fetches:
-        fetch.wait()
-    inner = sandwich(split(blocks[1]), start) + blocks[2]
-    first = sandwich(split(blocks[0]), split(inner))
-    high, low = split(jnp.concatenate([first, last], axis=0))
+    fetch.wait()
+    high, low = split(jnp.concatenate([sandwich(split(block[0]), start) + block[1], last], axis=0))
     dot = lambda a, b: jnp.dot(a, b, preferred_element_type=F32)
-    picked[...] = (dot(chosen, high) + dot(chosen, low)).reshape(picked.shape)
-    store = pltpu.make_async_copy(picked, out.at[:, energy], sem.at[3])
-    store.start()
-    store.wait()
-
-
-def pick(energy, end, late, place, live, rows, entry, state, side, pair, given, inputs, before=None):
+    stores = []
+    half = slots // 2
+    for n in range(2):
+        rows_in, groups = slice(n * half, (n + 1) * half), pl.ds(n * half // 8, half // 8)
+        picked[groups] = (dot(chosen[rows_in], high) + dot(chosen[rows_in], low)).reshape(half // 8, 8, width)
+        stores.append(pltpu.make_async_copy(picked.at[groups], out.at[groups, energy], sem.at[1 + n]))
+        stores[-1].start()
+    for store in stores:
+        store.wait()
+
+
+def pick(energy, end, late, place, live, rows, entry, state, side, pair, given, first, before=None):
     width = entry.shape[1]
     slots = rows.shape[0]
     operands = [place, live, rows, *[near(a) for a in (entry, state, side, *given[:3])], pair]
-    specs = [SMEM, SMEM] + [VMEM] * (len(operands) - 2) + [HBM] * 3
-    operands += [far(a) for a in inputs]
+    specs = [SMEM, SMEM] + [VMEM] * (len(operands) - 2) + [HBM]
+    operands.append(far(first))
     aliases = {}
     if before is not None:
         aliases = {len(operands): 0}
@@ -240,9 +265,9 @@
         out_shape=pltpu.HBM((slots // 8, 2, 8, width), F32),
         scratch_shapes=[
             pltpu.VMEM((width, width), F32),
-            pltpu.VMEM((3, width, width), F32),
+            pltpu.VMEM((2, width, width), F32),
             pltpu.VMEM((slots // 8, 8, width), F32),
-            pltpu.SemaphoreType.DMA((4,)),
+            pltpu.SemaphoreType.DMA((3,)),
         ],
         input_output_aliases=aliases,
         compiler_params=params(12),
@@ -263,49 +288,64 @@
     return forward.astype(np.float32), (forward.T * weight[None, :]).astype(np.float32)
 
 
-def spectrum_kernel(fwd_h, fwd_l, data, out):
-    for j in range(data.shape[1]):
-        out[j] = product((fwd_h[...], fwd_l[...]), split(data[:, j]))
+def stacked(matrix):
+    return jnp.concatenate(split(jnp.asarray(matrix)), axis=0)
+
+
+def transform(matrix, data):
+    count = data.shape[0]
+    high, low = split(data)
+    dot = lambda a, b: jnp.dot(a, b, preferred_element_type=F32)
+    both = dot(matrix, high)
+    return both[:count] + (both[count:] + dot(matrix[:count], low))
+
+
+def spectrum_kernel(fwd, data, out):
+    columns = jnp.swapaxes(data[...], 0, 1)
+    for j in range(columns.shape[0]):
+        out[j] = transform(fwd[...], columns[j])
 
 
 def spectrum(forward, data):
     count, group, width = data.shape
     return pl.pallas_call(
         spectrum_kernel,
-        in_specs=[VMEM] * 3,
+        in_specs=[VMEM] * 2,
         out_specs=VMEM,
         out_shape=pltpu.VMEM((group, count, width), F32),
         compiler_params=params(),
         cost_estimate=cost(2),
         name="spectrum",
-    )(*forward, far(data))
-
-
-def convolve_kernel(fwd_h, fwd_l, inv_h, inv_l, data, other, out):
-    count = data.shape[0]
-    half = count // 2
+    )(forward, far(data))
+
+
+def convolve_kernel(fwd, inv, data, other, out):
+    half = data.shape[0] // 2
     single = lax.broadcasted_iota(jnp.int32, (half, data.shape[2]), 0) == 0
-    for j in range(data.shape[1]):
-        left = product((fwd_h[...], fwd_l[...]), split(data[:, j]))
+    columns = jnp.swapaxes(data[...], 0, 1)
+    results = []
+    for j in range(columns.shape[0]):
+        left = transform(fwd[...], columns[j])
         right = other[j]
         real_a, imag_a = left[:half], left[half:]
         real_b, imag_b = right[:half], right[half:]
         real_p = real_a * real_b - jnp.where(single, 0.0, imag_a * imag_b)
         imag_p = jnp.where(single, imag_a * imag_b, real_a * imag_b + imag_a * real_b)
-        out[:, j] = product((inv_h[...], inv_l[...]), split(jnp.concatenate([real_p, imag_p], axis=0)))
+        results.append(transform(inv[...], jnp.concatenate([real_p, imag_p], axis=0)))
+    out[...] = jnp.swapaxes(jnp.stack(results), 0, 1)
 
 
 def convolve(forward, inverse, data, other):
     count, group, width = data.shape
     return pl.pallas_call(
         convolve_kernel,
-        in_specs=[VMEM] * 6,
+        in_specs=[VMEM] * 4,
         out_specs=VMEM,
         out_shape=jax.ShapeDtypeStruct((count, group, width), F32),
         compiler_params=params(),
         cost_estimate=cost(4),
         name="convolve",
-    )(*forward, *inverse, data, near(other))
+    )(forward, inverse, data, near(other))
 
 
 def arrange_kernel(data, after, out, sem):
@@ -342,7 +382,7 @@
     place = lax.axis_index("space").astype(jnp.int32).reshape(1)
     group = slots // parts
     count = energies * parts
-    forward, inverse = [split(jnp.asarray(m)) for m in transforms(count)]
+    forward, inverse = [stacked(m) for m in transforms(count)]
 
     middle = spaces // 2
     direct = list(range(middle))
@@ -361,17 +401,17 @@
                 weight = 200 if step in (2, 3) else 2
                 outgoing[e], entry[e] = hop(target, place, entry[e], outgoing[e], state[e], given[e], pair, weight)
         if step == 1:
-            chunks = arrange(screened.reshape(energies, parts, group, width), tick(outgoing[-1]))
+            chunks = arrange(screened.reshape(energies, parts, group, width), outgoing[-1])
     late = [z - 1 for z in odd]
     other = spectrum(forward, exchange(chunks).reshape(count, group, width))
     side = [lax.ppermute(outgoing[e], "space", [(path[path.index(z) - 1], z - 1) for z in odd]) for e in range(energies)]
 
     rows = kept_rows.reshape(slots, 1)
-    inputs = (inverses, coupling, source)
+    first = first_terms(inverses, coupling, source)
     picked = None
     for e in range(energies):
         picked = pick(
-            e, path[-1], late, place, live_count, rows, entry[e], state[e], side[e], pairs[e], given[e], inputs, picked
+            e, path[-1], late, place, live_count, rows, entry[e], state[e], side[e], pairs[e], given[e], first, picked
         )
     data = exchange(picked).reshape(count, group, width)
     sigma = convolve(forward, inverse, data, other)

time: 152 us -> 146 us (0.961)
  Pallas kernels: 27.9 us -> 23.4 us
  starting transfers between devices: 38.8 us -> 37.2 us
    ppermute x2, waiting for transfers between devices: 21.1 us -> 18.2 us  [body(): lax.ppermute(outgoing[e], 'space', [(path[path.index(z) - 1], z - 1) for...]
    all_to_all x2, waiting for transfers between devices: 24.1 us -> 27 us  [exchange(): lax.all_to_all(chunks, 'energy', split_axis=0, concat_axis=0, tiled=True)]
    pallas_call x3, Pallas kernels: 8.87 us -> 6.5 us  [the longest x1 3.22 us: first_terms(): pl.pallas_call(first_kernel, in_specs=[HBM] * 3, out_specs=HBM, out_shape...]
    ppermute x1 -> x0, starting transfers between devices: 1.92 us -> none  [tick(): return lax.ppermute(small, 'energy', [(i, i ^ 1) for i in range(parts)])]
  transfers between devices with their start and end apart: 17 -> 16, of which waited for: 4 -> 4; matrix products, arithmetic and copies ran while one was open for 0% -> 0% of each run, Pallas kernels for 12% -> 11%
where the time goes in v7:
time: 146 us; the launch traced here: 145 us
  waiting for transfers between devices  47.1 us (32%)
  starting transfers between devices  37.2 us (25%)
  blocking collectives  34.2 us (23%)
  Pallas kernels  23.4 us (16%)
  local copies, waits for them, and re-layouts  2.01 us (1%)
    all_to_all x1, blocking collectives, exchange(): lax.all_to_all(chunks, 'energy', split_axis=0, concat_axis=0, tiled=True)  34.2 us
    all_to_all x2, waiting for transfers between devices, exchange(): lax.all_to_all(chunks, 'energy', split_axis=0, concat_axis=0, tiled=True)  27 us
    all_to_all x2, starting transfers between devices, exchange(): lax.all_to_all(chunks, 'energy', split_axis=0, concat_axis=0, tiled=True)  22.3 us
    ppermute x2, waiting for transfers between devices, body(): lax.ppermute(outgoing[e], 'space', [(path[path.index(z) - 1], z - 1) for...  18.2 us
    ppermute x10, starting transfers between devices, body(): state[e] = lax.ppermute(outgoing[e], 'space', [(here, target)])  8.51 us
    pallas_call x2, Pallas kernels, pick(): pl.pallas_call(functools.partial(pick_kernel, energy, end, late), in_spec...  6.85 us
    pallas_call x1, Pallas kernels, prepare(): pl.pallas_call(functools.partial(prepare_kernel, senders), in_specs=[SMEM...  6.32 us
    ppermute x2, starting transfers between devices, body(): lax.ppermute(given[e][3], 'space', [(z - 1, z) for z in odd])  3.76 us
  transfers between devices with their start and end apart: 16, of which 4 were waited for; matrix products, arithmetic and copies ran while one was open for 0% of the time, Pallas kernels for 11%

profile of v7, /device:TPU:384, one launch (start us, length us, event | category | flops | bytes accessed | tf_op | source)
XLA Modules:
  0.0 145.0 jit_solution(10253907482047053208)
XLA Ops:
  0.0 6.3 %prepare.1 = (bf16[256,256]{1,0:T(8,128)(2,1)S(1)}, bf16[256,256]{1,0:T(8,128)(2,1)S(1)}, f32[256,256]{1,0:T(8,128)S(1)}, f32[2,256,256]{2,1,0:T(8,128)}, bf16[2...) custom-call(s32[1]{0:T(128)} %bitcast.place, ...), custom_call_target="tpu_custom_call" | custom-call | flops 1811939328 | bytes 1048576 | tf_op jit(solution)/shard_map/prepare/pallas_call | solution.py:111
  9.3 0.8 collective-permute-start.9
  10.1 2.4 %collective-permute-start.11 = (f32[2,256,256]{2,1,0:T(8,128)}, f32[2,256,256]{2,1,0:T(8,128)S(1)}, u32[]{:S(2)}, u32[]{:S(2)}) collective-permute-start(f32[2,256,256]{2,1,0:T(8,128)} %get-tuple-element.50), channel_id=1, source_target_pairs={{4,5},{6,7},{12,13},{14,15},{20,21},{22,23},{28,29},{30,31},{36,37... | collective-permute-start | bytes 1572872 | tf_op jit(solution)/shard_map/ppermute | solution.py:392
  12.6 1.3 collective-permute-start.4
  14.7 1.4 collective-permute-start.2
  16.0 1.0 arrange.1
  17.1 10.8 %all-to-all-start.1 = ((f32[64,2,8,256]{3,2,1,0:T(8,128)}), f32[64,2,8,256]{3,2,1,0:T(8,128)}, u32[]{:S(2)}, u32[]{:S(2)}) async-start(f32[64,2,8,256]{3,2,1,0:T(8,128)} %arrange.1), calls=%async_computation.1 | async-start | bytes 2097152 | tf_op jit(solution)/shard_map/all_to_all | solution.py:375
  28.0 0.8 collective-permute-start.10
  28.9 1.0 hop.10
  32.0 1.3 collective-permute-start.13
  33.3 1.9 %collective-permute-done.4.refs_0_.pair = f32[2,256,256]{2,1,0:T(8,128)S(1)} collective-permute-done((f32[2,256,256]{2,1,0:T(8,128)}, f32[2,256,256]{2,1,0:T(8,128)S(1)}, u32[]{:S(2)}, u32[]{:S(2)}) %collective-permute-start.4) | collective-permute-done | bytes 524320 | tf_op jit(solution)/shard_map/ppermute | solution.py:392
  36.0 1.5 %collective-permute-start.5 = (f32[256,256]{1,0:T(8,128)}, f32[256,256]{1,0:T(8,128)}, u32[]{:S(2)}, u32[]{:S(2)}) collective-permute-start(f32[256,256]{1,0:T(8,128)} %get-tuple-element.40), channel_id=1, source_target_pairs={{5,7},{13,15},{21,23},{29,31},{37,39},{45,47},{53,55},{61,63},{69,... | collective-permute-start | bytes 786440 | tf_op jit(solution)/shard_map/ppermute | solution.py:398
  37.5 1.3 collective-permute-start.6
  39.6 3.2 %first_terms.1.refs_0_ = f32[2,2,256,256]{3,2,1,0:T(8,128)} custom-call(f32[2,2,256,256]{3,2,1,0:T(8,128)} %inv_all.3, f32[2,256,256]{2,1,0:T(8,128)} %coup_all.3, f32[2,2,256,256]{3,2,1,0:T(8,128)} %src_all.3), custom_call_target="tpu_custom_call" | custom-call | flops 603979776 | bytes 1048576 | tf_op jit(solution)/shard_map/first_terms/pallas_call | solution.py:191
  42.8 11.8 %collective-permute-done.13.side = f32[256,256]{1,0:T(8,128)S(1)} collective-permute-done((f32[256,256]{1,0:T(8,128)}, f32[256,256]{1,0:T(8,128)S(1)}, u32[]{:S(2)}, u32[]{:S(2)}) %collective-permute-start.13) | collective-permute-done | bytes 262176 | tf_op jit(solution)/shard_map/ppermute | solution.py:407
  54.6 2.9 %pick.2.refs_1_ = f32[64,2,8,256]{3,2,1,0:T(8,128)} custom-call(s32[1]{0:T(128)} %bitcast.place, s32[1]{0:T(128)S(6)} %copy.16.live, s32[512,1]{1,0:T(8,128)S(1)} %copy.12.rows, f32[256,256]{1,0:T(8,128)S(1)} %get-tuple-element.51.entry, f32[256,256]{1,0:T(8,128)S(1)} %collective-permute-done.12.state, f32[256,256]{1,0:T(8,128)S(1)} %collective-permute-done.13.side, ...), custom_call_target="tpu_custom_call" | custom-call | flops 805306368 | bytes 1048576 | tf_op jit(solution)/shard_map/pick/pallas_call | solution.py:261
  57.5 6.4 %collective-permute-done.6.side = f32[256,256]{1,0:T(8,128)} collective-permute-done((f32[256,256]{1,0:T(8,128)}, f32[256,256]{1,0:T(8,128)}, u32[]{:S(2)}, u32[]{:S(2)}) %collective-permute-start.6) | collective-permute-done | bytes 262176 | tf_op jit(solution)/shard_map/ppermute | solution.py:407
  63.9 4.0 %pick.3 = f32[64,2,8,256]{3,2,1,0:T(8,128)} custom-call(s32[1]{0:T(128)} %bitcast.place, s32[1]{0:T(128)S(6)} %copy.16.live, s32[512,1]{1,0:T(8,128)S(1)} %copy.12.rows, f32[256,256]{1,0:T(8,128)S(1)} %get-tuple-element.39.entry, f32[256,256]{1,0:T(8,128)} %collective-permute-done.5.state, ...), custom_call_target="tpu_custom_call", output_to_operand_aliasing={{}: (11, {})} | custom-call | flops 805306368 | bytes 1048576 | tf_op jit(solution)/shard_map/pick/pallas_call | solution.py:261
  67.9 11.5 %all-to-all-start = ((f32[64,2,8,256]{3,2,1,0:T(8,128)}), f32[64,2,8,256]{3,2,1,0:T(8,128)S(1)}, u32[]{:S(2)}, u32[]{:S(2)}) async-start(f32[64,2,8,256]{3,2,1,0:T(8,128)} %pick.3), calls=%async_computation | async-start | bytes 2097152 | tf_op jit(solution)/shard_map/all_to_all | solution.py:375
  79.4 1.9 %spectrum.1.other = f32[8,128,256]{2,1,0:T(8,128)S(1)} custom-call(bf16[256,128]{1,0:T(8,128)(2,1)S(1)} %copy-done.1, f32[128,8,256]{2,1,0:T(8,128)} %bitcast.4.data), custom_call_target="tpu_custom_call" | custom-call | flops 201326592 | bytes 1048576 | tf_op jit(solution)/shard_map/spectrum/pallas_call | solution.py:311
  81.3 27.0 %all-to-all-done = f32[64,2,8,256]{3,2,1,0:T(8,128)S(1)} async-done(((f32[64,2,8,256]{3,2,1,0:T(8,128)}), f32[64,2,8,256]{3,2,1,0:T(8,128)S(1)}, u32[]{:S(2)}, u32[]{:S(2)}) %all-to-all-start) | async-done | bytes 1048608 | tf_op jit(solution)/shard_map/all_to_all | solution.py:375
  108.3 1.4 convolve.1
  109.7 34.2 %all_to_all.15 = f32[64,2,8,256]{3,2,1,0:T(8,128)S(1)} all-to-all(f32[64,2,8,256]{3,2,1,0:T(8,128)S(1)} %bitcast.12), channel_id=1, replica_groups=mesh['energy'=64,'space'=8] {'energy'}, dimensions={0} | all-to-all | bytes 2097152 | tf_op jit(solution)/shard_map/all_to_all | solution.py:375
  143.9 1.1 copy_bitcast_fusion
  (39 shorter events, 6.8 us)
Async XLA Ops:
  6.3 1.4 collective-permute-start.7
  7.0 1.5 %collective-permute-start = (f32[256,256]{1,0:T(8,128)S(1)}, f32[256,256]{1,0:T(8,128)S(1)}, u32[]{:S(2)}, u32[]{:S(2)}) collective-permute-start(f32[256,256]{1,0:T(8,128)S(1)} %get-tuple-element.29.before.add), channel_id=1, source_target_pairs={{0,1},{8,9},{16,17},{24,25},{32,33},{40,41},{48,49},{56,57},{64,65... | collective-permute-start | bytes 786440 | tf_op jit(solution)/shard_map/ppermute | solution.py:398
  7.8 1.4 collective-permute-start.8
  8.5 5.4 %collective-permute-start.1 = (f32[256,256]{1,0:T(8,128)S(1)}, f32[256,256]{1,0:T(8,128)S(1)}, u32[]{:S(2)}, u32[]{:S(2)}) collective-permute-start(f32[256,256]{1,0:T(8,128)S(1)} %get-tuple-element.33.before), channel_id=1, source_target_pairs={{1,2},{9,10},{17,18},{25,26},{33,34},{41,42},{49,50},{57,58},{65,6... | collective-permute-start | bytes 786440 | tf_op jit(solution)/shard_map/ppermute | solution.py:398
  9.2 6.8 %copy-start = (f32[2,512,256]{2,1,0:T(8,128)S(1)}, f32[2,512,256]{2,1,0:T(8,128)}, u32[]{:S(2)}) copy-start(f32[2,512,256]{2,1,0:T(8,128)} %param.11) | copy-start | bytes 3145732
  9.3 18.6 %collective-permute-start.9 = (f32[256,256]{1,0:T(8,128)S(1)}, f32[256,256]{1,0:T(8,128)S(1)}, u32[]{:S(2)}, u32[]{:S(2)}) collective-permute-start(f32[256,256]{1,0:T(8,128)S(1)} %get-tuple-element.47.before), channel_id=1, source_target_pairs={{2,3},{10,11},{18,19},{26,27},{34,35},{42,43},{50,51},{58,59},{66,... | collective-permute-start | bytes 786440 | tf_op jit(solution)/shard_map/ppermute | solution.py:398
  10.1 20.4 %collective-permute-start.11 = (f32[2,256,256]{2,1,0:T(8,128)}, f32[2,256,256]{2,1,0:T(8,128)S(1)}, u32[]{:S(2)}, u32[]{:S(2)}) collective-permute-start(f32[2,256,256]{2,1,0:T(8,128)} %get-tuple-element.50), channel_id=1, source_target_pairs={{4,5},{6,7},{12,13},{14,15},{20,21},{22,23},{28,29},{30,31},{36,37... | collective-permute-start | bytes 1572872 | tf_op jit(solution)/shard_map/ppermute | solution.py:392
  12.6 22.7 %collective-permute-start.4 = (f32[2,256,256]{2,1,0:T(8,128)}, f32[2,256,256]{2,1,0:T(8,128)S(1)}, u32[]{:S(2)}, u32[]{:S(2)}) collective-permute-start(f32[2,256,256]{2,1,0:T(8,128)} %get-tuple-element.38), channel_id=1, source_target_pairs={{4,5},{6,7},{12,13},{14,15},{20,21},{22,23},{28,29},{30,31},{36,37... | collective-permute-start | bytes 1572872 | tf_op jit(solution)/shard_map/ppermute | solution.py:392
  14.0 0.7 copy-start.3
  14.7 14.1 %collective-permute-start.2 = (f32[256,256]{1,0:T(8,128)S(1)}, f32[256,256]{1,0:T(8,128)}, u32[]{:S(2)}, u32[]{:S(2)}) collective-permute-start(f32[256,256]{1,0:T(8,128)S(1)} %get-tuple-element.35.before.after), channel_id=1, source_target_pairs={{2,3},{10,11},{18,19},{26,27},{34,35},{42,43},{50,51},{58,59},{66,... | collective-permute-start | bytes 786440 | tf_op jit(solution)/shard_map/ppermute | solution.py:398
  17.1 50.8 %all-to-all-start.1 = ((f32[64,2,8,256]{3,2,1,0:T(8,128)}), f32[64,2,8,256]{3,2,1,0:T(8,128)}, u32[]{:S(2)}, u32[]{:S(2)}) async-start(f32[64,2,8,256]{3,2,1,0:T(8,128)} %arrange.1), calls=%async_computation.1 | async-start | bytes 2097152 | tf_op jit(solution)/shard_map/all_to_all | solution.py:375
  27.9 1.0 copy-start.4
  28.0 2.6 %collective-permute-start.10 = (f32[256,256]{1,0:T(8,128)S(1)}, f32[256,256]{1,0:T(8,128)S(1)}, u32[]{:S(2)}, u32[]{:S(2)}) collective-permute-start(f32[256,256]{1,0:T(8,128)S(1)} %get-tuple-element.49.before), channel_id=1, source_target_pairs={{3,5},{11,13},{19,21},{27,29},{35,37},{43,45},{51,53},{59,61},{67,... | collective-permute-start | bytes 786440 | tf_op jit(solution)/shard_map/ppermute | solution.py:398
  29.9 5.4 %collective-permute-start.3 = (f32[256,256]{1,0:T(8,128)S(1)}, f32[256,256]{1,0:T(8,128)S(1)}, u32[]{:S(2)}, u32[]{:S(2)}) collective-permute-start(f32[256,256]{1,0:T(8,128)S(1)} %get-tuple-element.37.before), channel_id=1, source_target_pairs={{3,5},{11,13},{19,21},{27,29},{35,37},{43,45},{51,53},{59,61},{67,... | collective-permute-start | bytes 786440 | tf_op jit(solution)/shard_map/ppermute | solution.py:398
  31.3 11.5 %collective-permute-start.12 = (f32[256,256]{1,0:T(8,128)}, f32[256,256]{1,0:T(8,128)S(1)}, u32[]{:S(2)}, u32[]{:S(2)}) collective-permute-start(f32[256,256]{1,0:T(8,128)} %get-tuple-element.52), channel_id=1, source_target_pairs={{5,7},{13,15},{21,23},{29,31},{37,39},{45,47},{53,55},{61,63},{69,... | collective-permute-start | bytes 786440 | tf_op jit(solution)/shard_map/ppermute | solution.py:398
  32.0 22.6 %collective-permute-start.13 = (f32[256,256]{1,0:T(8,128)}, f32[256,256]{1,0:T(8,128)S(1)}, u32[]{:S(2)}, u32[]{:S(2)}) collective-permute-start(f32[256,256]{1,0:T(8,128)} %get-tuple-element.52), channel_id=1, source_target_pairs={{3,4},{5,6},{11,12},{13,14},{19,20},{21,22},{27,28},{29,30},{35,36... | collective-permute-start | bytes 786440 | tf_op jit(solution)/shard_map/ppermute | solution.py:407
  36.0 2.8 %copy-start.5 = (s32[512]{0:T(512)S(1)}, s32[512]{0:T(512)}, u32[]{:S(2)}) copy-start(s32[512]{0:T(512)} %param.12) | copy-start | bytes 6148
  36.0 21.6 %collective-permute-start.5 = (f32[256,256]{1,0:T(8,128)}, f32[256,256]{1,0:T(8,128)}, u32[]{:S(2)}, u32[]{:S(2)}) collective-permute-start(f32[256,256]{1,0:T(8,128)} %get-tuple-element.40), channel_id=1, source_target_pairs={{5,7},{13,15},{21,23},{29,31},{37,39},{45,47},{53,55},{61,63},{69,... | collective-permute-start | bytes 786440 | tf_op jit(solution)/shard_map/ppermute | solution.py:398
  37.5 26.5 %collective-permute-start.6 = (f32[256,256]{1,0:T(8,128)}, f32[256,256]{1,0:T(8,128)}, u32[]{:S(2)}, u32[]{:S(2)}) collective-permute-start(f32[256,256]{1,0:T(8,128)} %get-tuple-element.40), channel_id=1, source_target_pairs={{3,4},{5,6},{11,12},{13,14},{19,20},{21,22},{27,28},{29,30},{35,36... | collective-permute-start | bytes 786440 | tf_op jit(solution)/shard_map/ppermute | solution.py:407
  67.9 11.5 %copy-start.1 = (bf16[256,128]{1,0:T(8,128)(2,1)S(1)}, bf16[256,128]{1,0:T(8,128)(2,1)}, u32[]{:S(2)}) copy-start(bf16[256,128]{1,0:T(8,128)(2,1)} %constant.21.fwd) | copy-start | bytes 196612
  67.9 40.4 %all-to-all-start = ((f32[64,2,8,256]{3,2,1,0:T(8,128)}), f32[64,2,8,256]{3,2,1,0:T(8,128)S(1)}, u32[]{:S(2)}, u32[]{:S(2)}) async-start(f32[64,2,8,256]{3,2,1,0:T(8,128)} %pick.3), calls=%async_computation | async-start | bytes 2097152 | tf_op jit(solution)/shard_map/all_to_all | solution.py:375
  79.4 28.9 %copy-start.2 = (bf16[256,128]{1,0:T(8,128)(2,1)S(1)}, bf16[256,128]{1,0:T(8,128)(2,1)}, u32[]{:S(2)}) copy-start(bf16[256,128]{1,0:T(8,128)(2,1)} %constant.26.inv) | copy-start | bytes 196612

commit v8 on v7

--- a/solution.py
+++ b/solution.py
@@ -53,7 +53,7 @@
 def prepare_kernel(senders, place, inv_all, coup_all, src_all, *refs):
     energies = inv_all.shape[0]
     outs = [refs[4 * e : 4 * e + 4] for e in range(energies)]
-    inv, coup, src, kept, sem, out_sem = refs[4 * energies :]
+    inv, coup, src, work, kept, sem, out_sem = refs[4 * energies :]
     sends = functools.reduce(jnp.logical_or, [place[0] == z for z in senders])
     copies = {}
 
@@ -79,17 +79,17 @@
 
     for e in range(energies):
         map_h, map_l, add, _ = outs[e]
-        step, inj = [], []
         for b in range(2):
             left = ready(inv, "inv", e, b)
             right = ready(coup, "coup", b)
             middle = ready(src, "src", e, b)
             if order:
                 fetch_block(*order.pop(0))
-            step.append(split(product(left, right)))
-            inj.append(sandwich(left, middle))
-        added = sandwich(step[1], split(inj[0])) + inj[1]
-        mapped = product(step[1], step[0])
+            work[e, b, 0] = product(left, right)
+            work[e, b, 1] = sandwich(left, middle)
+        last = split(work[e, 1, 0])
+        added = sandwich(last, split(work[e, 0, 1])) + work[e, 1, 1]
+        mapped = product(last, split(work[e, 0, 0]))
         add[...] = added
         map_h[...], map_l[...] = split(mapped)
         kept[e, 0] = mapped
@@ -117,6 +117,7 @@
             pltpu.VMEM(inverses.shape, F32),
             pltpu.VMEM(coupling.shape, F32),
             pltpu.VMEM(source.shape, F32),
+            pltpu.VMEM((energies, 2, 2, *square), F32),
             pltpu.VMEM((energies, 2, *square), F32),
             pltpu.SemaphoreType.DMA((2 + 4 * energies,)),
             pltpu.SemaphoreType.DMA((energies,)),
@@ -250,7 +251,7 @@
 def pick(energy, end, late, place, live, rows, entry, state, side, pair, given, first, before=None):
     width = entry.shape[1]
     slots = rows.shape[0]
-    operands = [place, live, rows, *[near(a) for a in (entry, state, side, *given[:3])], pair]
+    operands = [place, live, rows, *[near(a) for a in (entry, state, side, *given[:3], pair)]]
     specs = [SMEM, SMEM] + [VMEM] * (len(operands) - 2) + [HBM]
     operands.append(far(first))
     aliases = {}

time: 146 us -> 146 us (level)
  no operation moved by 1% of the time
where the time goes in v8:
time: 146 us; the launch traced here: 145 us
  waiting for transfers between devices  47.1 us (32%)
  starting transfers between devices  37.2 us (25%)
  blocking collectives  34.2 us (23%)
  Pallas kernels  23.4 us (16%)
  local copies, waits for them, and re-layouts  2.01 us (1%)
    all_to_all x1, blocking collectives, exchange(): lax.all_to_all(chunks, 'energy', split_axis=0, concat_axis=0, tiled=True)  34.2 us
    all_to_all x2, waiting for transfers between devices, exchange(): lax.all_to_all(chunks, 'energy', split_axis=0, concat_axis=0, tiled=True)  27 us
    all_to_all x2, starting transfers between devices, exchange(): lax.all_to_all(chunks, 'energy', split_axis=0, concat_axis=0, tiled=True)  22.4 us
    ppermute x2, waiting for transfers between devices, body(): lax.ppermute(outgoing[e], 'space', [(path[path.index(z) - 1], z - 1) for...  18.2 us
    ppermute x10, starting transfers between devices, body(): state[e] = lax.ppermute(outgoing[e], 'space', [(here, target)])  8.51 us
    pallas_call x2, Pallas kernels, pick(): pl.pallas_call(functools.partial(pick_kernel, energy, end, late), in_spec...  6.85 us
    pallas_call x1, Pallas kernels, prepare(): pl.pallas_call(functools.partial(prepare_kernel, senders), in_specs=[SMEM...  6.33 us
    ppermute x2, starting transfers between devices, body(): lax.ppermute(given[e][3], 'space', [(z - 1, z) for z in odd])  3.76 us
  transfers between devices with their start and end apart: 16, of which 4 were waited for; matrix products, arithmetic and copies ran while one was open for 0% of the time, Pallas kernels for 11%

profile of v8, /device:TPU:384, one launch (start us, length us, event | category | flops | bytes accessed | tf_op | source)
XLA Modules:
  0.0 145.0 jit_solution(1976603342228684625)
XLA Ops:
  0.0 6.3 %prepare.1 = (bf16[256,256]{1,0:T(8,128)(2,1)S(1)}, bf16[256,256]{1,0:T(8,128)(2,1)S(1)}, f32[256,256]{1,0:T(8,128)S(1)}, f32[2,256,256]{2,1,0:T(8,128)}, bf16[2...) custom-call(s32[1]{0:T(128)} %bitcast.place, ...), custom_call_target="tpu_custom_call" | custom-call | flops 1811939328 | bytes 1048576 | tf_op jit(solution)/shard_map/prepare/pallas_call | solution.py:111
  9.3 0.8 collective-permute-start.9
  10.1 2.4 %collective-permute-start.11 = (f32[2,256,256]{2,1,0:T(8,128)}, f32[2,256,256]{2,1,0:T(8,128)S(1)}, u32[]{:S(2)}, u32[]{:S(2)}) collective-permute-start(f32[2,256,256]{2,1,0:T(8,128)} %get-tuple-element.50), channel_id=1, source_target_pairs={{4,5},{6,7},{12,13},{14,15},{20,21},{22,23},{28,29},{30,31},{36,37... | collective-permute-start | bytes 1572872 | tf_op jit(solution)/shard_map/ppermute | solution.py:393
  12.6 1.3 collective-permute-start.4
  14.7 1.4 collective-permute-start.2
  16.0 1.0 arrange.1
  17.1 10.8 %all-to-all-start.1 = ((f32[64,2,8,256]{3,2,1,0:T(8,128)}), f32[64,2,8,256]{3,2,1,0:T(8,128)}, u32[]{:S(2)}, u32[]{:S(2)}) async-start(f32[64,2,8,256]{3,2,1,0:T(8,128)} %arrange.1), calls=%async_computation.1 | async-start | bytes 2097152 | tf_op jit(solution)/shard_map/all_to_all | solution.py:376
  28.0 0.8 collective-permute-start.10
  28.9 1.0 hop.10
  32.0 1.3 collective-permute-start.13
  33.3 1.9 %collective-permute-done.4.refs_0_.pair = f32[2,256,256]{2,1,0:T(8,128)S(1)} collective-permute-done((f32[2,256,256]{2,1,0:T(8,128)}, f32[2,256,256]{2,1,0:T(8,128)S(1)}, u32[]{:S(2)}, u32[]{:S(2)}) %collective-permute-start.4) | collective-permute-done | bytes 524320 | tf_op jit(solution)/shard_map/ppermute | solution.py:393
  36.0 1.5 %collective-permute-start.5 = (f32[256,256]{1,0:T(8,128)}, f32[256,256]{1,0:T(8,128)}, u32[]{:S(2)}, u32[]{:S(2)}) collective-permute-start(f32[256,256]{1,0:T(8,128)} %get-tuple-element.40), channel_id=1, source_target_pairs={{5,7},{13,15},{21,23},{29,31},{37,39},{45,47},{53,55},{61,63},{69,... | collective-permute-start | bytes 786440 | tf_op jit(solution)/shard_map/ppermute | solution.py:399
  37.5 1.3 collective-permute-start.6
  39.6 3.2 %first_terms.1.refs_0_ = f32[2,2,256,256]{3,2,1,0:T(8,128)} custom-call(f32[2,2,256,256]{3,2,1,0:T(8,128)} %inv_all.3, f32[2,256,256]{2,1,0:T(8,128)} %coup_all.3, f32[2,2,256,256]{3,2,1,0:T(8,128)} %src_all.3), custom_call_target="tpu_custom_call" | custom-call | flops 603979776 | bytes 1048576 | tf_op jit(solution)/shard_map/first_terms/pallas_call | solution.py:192
  42.8 11.8 %collective-permute-done.13.side = f32[256,256]{1,0:T(8,128)S(1)} collective-permute-done((f32[256,256]{1,0:T(8,128)}, f32[256,256]{1,0:T(8,128)S(1)}, u32[]{:S(2)}, u32[]{:S(2)}) %collective-permute-start.13) | collective-permute-done | bytes 262176 | tf_op jit(solution)/shard_map/ppermute | solution.py:408
  54.6 2.9 %pick.2.refs_1_ = f32[64,2,8,256]{3,2,1,0:T(8,128)} custom-call(s32[1]{0:T(128)} %bitcast.place, s32[1]{0:T(128)S(6)} %copy.16.live, s32[512,1]{1,0:T(8,128)S(1)} %copy.12.rows, f32[256,256]{1,0:T(8,128)S(1)} %get-tuple-element.51.entry, f32[256,256]{1,0:T(8,128)S(1)} %collective-permute-done.12.state, f32[256,256]{1,0:T(8,128)S(1)} %collective-permute-done.13.side, ...), custom_call_target="tpu_custom_call" | custom-call | flops 805306368 | bytes 1048576 | tf_op jit(solution)/shard_map/pick/pallas_call | solution.py:262
  57.5 6.4 %collective-permute-done.6.side = f32[256,256]{1,0:T(8,128)} collective-permute-done((f32[256,256]{1,0:T(8,128)}, f32[256,256]{1,0:T(8,128)}, u32[]{:S(2)}, u32[]{:S(2)}) %collective-permute-start.6) | collective-permute-done | bytes 262176 | tf_op jit(solution)/shard_map/ppermute | solution.py:408
  63.9 4.0 %pick.3 = f32[64,2,8,256]{3,2,1,0:T(8,128)} custom-call(s32[1]{0:T(128)} %bitcast.place, s32[1]{0:T(128)S(6)} %copy.16.live, s32[512,1]{1,0:T(8,128)S(1)} %copy.12.rows, f32[256,256]{1,0:T(8,128)S(1)} %get-tuple-element.39.entry, f32[256,256]{1,0:T(8,128)} %collective-permute-done.5.state, ...), custom_call_target="tpu_custom_call", output_to_operand_aliasing={{}: (11, {})} | custom-call | flops 805306368 | bytes 1048576 | tf_op jit(solution)/shard_map/pick/pallas_call | solution.py:262
  67.9 11.5 %all-to-all-start = ((f32[64,2,8,256]{3,2,1,0:T(8,128)}), f32[64,2,8,256]{3,2,1,0:T(8,128)S(1)}, u32[]{:S(2)}, u32[]{:S(2)}) async-start(f32[64,2,8,256]{3,2,1,0:T(8,128)} %pick.3), calls=%async_computation | async-start | bytes 2097152 | tf_op jit(solution)/shard_map/all_to_all | solution.py:376
  79.4 1.9 %spectrum.1.other = f32[8,128,256]{2,1,0:T(8,128)S(1)} custom-call(bf16[256,128]{1,0:T(8,128)(2,1)S(1)} %copy-done.1, f32[128,8,256]{2,1,0:T(8,128)} %bitcast.4.data), custom_call_target="tpu_custom_call" | custom-call | flops 201326592 | bytes 1048576 | tf_op jit(solution)/shard_map/spectrum/pallas_call | solution.py:312
  81.3 27.0 %all-to-all-done = f32[64,2,8,256]{3,2,1,0:T(8,128)S(1)} async-done(((f32[64,2,8,256]{3,2,1,0:T(8,128)}), f32[64,2,8,256]{3,2,1,0:T(8,128)S(1)}, u32[]{:S(2)}, u32[]{:S(2)}) %all-to-all-start) | async-done | bytes 1048608 | tf_op jit(solution)/shard_map/all_to_all | solution.py:376
  108.3 1.4 convolve.1
  109.7 34.2 %all_to_all.15 = f32[64,2,8,256]{3,2,1,0:T(8,128)S(1)} all-to-all(f32[64,2,8,256]{3,2,1,0:T(8,128)S(1)} %bitcast.12), channel_id=1, replica_groups=mesh['energy'=64,'space'=8] {'energy'}, dimensions={0} | all-to-all | bytes 2097152 | tf_op jit(solution)/shard_map/all_to_all | solution.py:376
  143.9 1.1 copy_bitcast_fusion
  (39 shorter events, 6.8 us)
Async XLA Ops:
  6.3 1.4 collective-permute-start.7
  7.0 1.5 %collective-permute-start = (f32[256,256]{1,0:T(8,128)S(1)}, f32[256,256]{1,0:T(8,128)S(1)}, u32[]{:S(2)}, u32[]{:S(2)}) collective-permute-start(f32[256,256]{1,0:T(8,128)S(1)} %get-tuple-element.29.before.add), channel_id=1, source_target_pairs={{0,1},{8,9},{16,17},{24,25},{32,33},{40,41},{48,49},{56,57},{64,65... | collective-permute-start | bytes 786440 | tf_op jit(solution)/shard_map/ppermute | solution.py:399
  7.8 1.4 collective-permute-start.8
  8.5 5.4 %collective-permute-start.1 = (f32[256,256]{1,0:T(8,128)S(1)}, f32[256,256]{1,0:T(8,128)S(1)}, u32[]{:S(2)}, u32[]{:S(2)}) collective-permute-start(f32[256,256]{1,0:T(8,128)S(1)} %get-tuple-element.33.before), channel_id=1, source_target_pairs={{1,2},{9,10},{17,18},{25,26},{33,34},{41,42},{49,50},{57,58},{65,6... | collective-permute-start | bytes 786440 | tf_op jit(solution)/shard_map/ppermute | solution.py:399
  9.2 6.8 %copy-start = (f32[2,512,256]{2,1,0:T(8,128)S(1)}, f32[2,512,256]{2,1,0:T(8,128)}, u32[]{:S(2)}) copy-start(f32[2,512,256]{2,1,0:T(8,128)} %param.11) | copy-start | bytes 3145732
  9.3 18.6 %collective-permute-start.9 = (f32[256,256]{1,0:T(8,128)S(1)}, f32[256,256]{1,0:T(8,128)S(1)}, u32[]{:S(2)}, u32[]{:S(2)}) collective-permute-start(f32[256,256]{1,0:T(8,128)S(1)} %get-tuple-element.47.before), channel_id=1, source_target_pairs={{2,3},{10,11},{18,19},{26,27},{34,35},{42,43},{50,51},{58,59},{66,... | collective-permute-start | bytes 786440 | tf_op jit(solution)/shard_map/ppermute | solution.py:399
  10.1 20.4 %collective-permute-start.11 = (f32[2,256,256]{2,1,0:T(8,128)}, f32[2,256,256]{2,1,0:T(8,128)S(1)}, u32[]{:S(2)}, u32[]{:S(2)}) collective-permute-start(f32[2,256,256]{2,1,0:T(8,128)} %get-tuple-element.50), channel_id=1, source_target_pairs={{4,5},{6,7},{12,13},{14,15},{20,21},{22,23},{28,29},{30,31},{36,37... | collective-permute-start | bytes 1572872 | tf_op jit(solution)/shard_map/ppermute | solution.py:393
  12.6 22.7 %collective-permute-start.4 = (f32[2,256,256]{2,1,0:T(8,128)}, f32[2,256,256]{2,1,0:T(8,128)S(1)}, u32[]{:S(2)}, u32[]{:S(2)}) collective-permute-start(f32[2,256,256]{2,1,0:T(8,128)} %get-tuple-element.38), channel_id=1, source_target_pairs={{4,5},{6,7},{12,13},{14,15},{20,21},{22,23},{28,29},{30,31},{36,37... | collective-permute-start | bytes 1572872 | tf_op jit(solution)/shard_map/ppermute | solution.py:393
  14.0 0.7 copy-start.3
  14.7 14.1 %collective-permute-start.2 = (f32[256,256]{1,0:T(8,128)S(1)}, f32[256,256]{1,0:T(8,128)}, u32[]{:S(2)}, u32[]{:S(2)}) collective-permute-start(f32[256,256]{1,0:T(8,128)S(1)} %get-tuple-element.35.before.after), channel_id=1, source_target_pairs={{2,3},{10,11},{18,19},{26,27},{34,35},{42,43},{50,51},{58,59},{66,... | collective-permute-start | bytes 786440 | tf_op jit(solution)/shard_map/ppermute | solution.py:399
  17.1 50.8 %all-to-all-start.1 = ((f32[64,2,8,256]{3,2,1,0:T(8,128)}), f32[64,2,8,256]{3,2,1,0:T(8,128)}, u32[]{:S(2)}, u32[]{:S(2)}) async-start(f32[64,2,8,256]{3,2,1,0:T(8,128)} %arrange.1), calls=%async_computation.1 | async-start | bytes 2097152 | tf_op jit(solution)/shard_map/all_to_all | solution.py:376
  27.9 1.0 copy-start.4
  28.0 2.6 %collective-permute-start.10 = (f32[256,256]{1,0:T(8,128)S(1)}, f32[256,256]{1,0:T(8,128)S(1)}, u32[]{:S(2)}, u32[]{:S(2)}) collective-permute-start(f32[256,256]{1,0:T(8,128)S(1)} %get-tuple-element.49.before), channel_id=1, source_target_pairs={{3,5},{11,13},{19,21},{27,29},{35,37},{43,45},{51,53},{59,61},{67,... | collective-permute-start | bytes 786440 | tf_op jit(solution)/shard_map/ppermute | solution.py:399
  29.9 5.4 %collective-permute-start.3 = (f32[256,256]{1,0:T(8,128)S(1)}, f32[256,256]{1,0:T(8,128)S(1)}, u32[]{:S(2)}, u32[]{:S(2)}) collective-permute-start(f32[256,256]{1,0:T(8,128)S(1)} %get-tuple-element.37.before), channel_id=1, source_target_pairs={{3,5},{11,13},{19,21},{27,29},{35,37},{43,45},{51,53},{59,61},{67,... | collective-permute-start | bytes 786440 | tf_op jit(solution)/shard_map/ppermute | solution.py:399
  31.4 11.5 %collective-permute-start.12 = (f32[256,256]{1,0:T(8,128)}, f32[256,256]{1,0:T(8,128)S(1)}, u32[]{:S(2)}, u32[]{:S(2)}) collective-permute-start(f32[256,256]{1,0:T(8,128)} %get-tuple-element.52), channel_id=1, source_target_pairs={{5,7},{13,15},{21,23},{29,31},{37,39},{45,47},{53,55},{61,63},{69,... | collective-permute-start | bytes 786440 | tf_op jit(solution)/shard_map/ppermute | solution.py:399
  32.0 22.6 %collective-permute-start.13 = (f32[256,256]{1,0:T(8,128)}, f32[256,256]{1,0:T(8,128)S(1)}, u32[]{:S(2)}, u32[]{:S(2)}) collective-permute-start(f32[256,256]{1,0:T(8,128)} %get-tuple-element.52), channel_id=1, source_target_pairs={{3,4},{5,6},{11,12},{13,14},{19,20},{21,22},{27,28},{29,30},{35,36... | collective-permute-start | bytes 786440 | tf_op jit(solution)/shard_map/ppermute | solution.py:408
  36.0 2.8 %copy-start.5 = (s32[512]{0:T(512)S(1)}, s32[512]{0:T(512)}, u32[]{:S(2)}) copy-start(s32[512]{0:T(512)} %param.12) | copy-start | bytes 6148
  36.0 21.5 %collective-permute-start.5 = (f32[256,256]{1,0:T(8,128)}, f32[256,256]{1,0:T(8,128)}, u32[]{:S(2)}, u32[]{:S(2)}) collective-permute-start(f32[256,256]{1,0:T(8,128)} %get-tuple-element.40), channel_id=1, source_target_pairs={{5,7},{13,15},{21,23},{29,31},{37,39},{45,47},{53,55},{61,63},{69,... | collective-permute-start | bytes 786440 | tf_op jit(solution)/shard_map/ppermute | solution.py:399
  37.5 26.4 %collective-permute-start.6 = (f32[256,256]{1,0:T(8,128)}, f32[256,256]{1,0:T(8,128)}, u32[]{:S(2)}, u32[]{:S(2)}) collective-permute-start(f32[256,256]{1,0:T(8,128)} %get-tuple-element.40), channel_id=1, source_target_pairs={{3,4},{5,6},{11,12},{13,14},{19,20},{21,22},{27,28},{29,30},{35,36... | collective-permute-start | bytes 786440 | tf_op jit(solution)/shard_map/ppermute | solution.py:408
  67.9 11.5 %copy-start.1 = (bf16[256,128]{1,0:T(8,128)(2,1)S(1)}, bf16[256,128]{1,0:T(8,128)(2,1)}, u32[]{:S(2)}) copy-start(bf16[256,128]{1,0:T(8,128)(2,1)} %constant.21.fwd) | copy-start | bytes 196612
  67.9 40.4 %all-to-all-start = ((f32[64,2,8,256]{3,2,1,0:T(8,128)}), f32[64,2,8,256]{3,2,1,0:T(8,128)S(1)}, u32[]{:S(2)}, u32[]{:S(2)}) async-start(f32[64,2,8,256]{3,2,1,0:T(8,128)} %pick.3), calls=%async_computation | async-start | bytes 2097152 | tf_op jit(solution)/shard_map/all_to_all | solution.py:376
  79.4 28.9 %copy-start.2 = (bf16[256,128]{1,0:T(8,128)(2,1)S(1)}, bf16[256,128]{1,0:T(8,128)(2,1)}, u32[]{:S(2)}) copy-start(bf16[256,128]{1,0:T(8,128)(2,1)} %constant.26.inv) | copy-start | bytes 196612
